TPU v7x, 512 devices: a whole 4x8x8 slice. The times are simulated.
512 devices in a mesh: row: 32 (over z, x), col: 16 (over y, core).
Axes of the slice: x: 4, y: 8, z: 8, core: 2. Of those that a mesh axis runs over, the one named last changes fastest.
Arguments:
- momentum: bfloat16 [4, 1536, 7168], P(None, 'row', 'col'), may hold values from -0.048339844 to 0.048339844
Outputs:
- orthogonal: bfloat16 [4, 1536, 7168], P(None, 'row', 'col')
All inputs are finite; a program needn't handle non-finite values.
Results may differ from a plain program's by a relative error of at most 0.0054.
Values may be sent and summed in bfloat16 or wider, within the bound.
No kernel may reach another device: no remote copies, remote signals or barrier semaphores. Data moves between devices by JAX's collectives and lax.ppermute only.
A program may use at most 64 MiB of HBM per device.

v0:
```python
import math

import jax
import jax.numpy as jnp
from jax import lax
from jax.sharding import PartitionSpec as P


def local(momentum):
    col_parts = lax.axis_size("col")
    width = momentum.shape[2] * col_parts
    partial_gram = jnp.einsum(
        "lin,ljn->lij",
        momentum,
        lax.all_gather(momentum, "row", axis=1, tiled=True),
        preferred_element_type=jnp.float32,
    )
    gram_block = lax.psum_scatter(partial_gram, "col", scatter_dimension=2, tiled=True).astype(
        jnp.bfloat16
    )
    gram_rows = lax.all_gather(gram_block, "col", axis=2, tiled=True)
    gram_cols = lax.all_gather(gram_block, "row", axis=1, tiled=True)
    square_block = jnp.einsum(
        "lik,lkj->lij", gram_rows, gram_cols, preferred_element_type=jnp.float32
    )
    poly_block = (-4.775 * gram_block.astype(jnp.float32) + 2.0315 * square_block).astype(
        jnp.bfloat16
    )
    poly_rows = lax.all_gather(poly_block, "col", axis=2, tiled=True)
    product = jnp.einsum(
        "lik,lkn->lin",
        poly_rows,
        lax.all_gather(momentum, "row", axis=1, tiled=True),
        preferred_element_type=jnp.float32,
    )
    result = 0.2 * math.sqrt(width) * (3.4445 * momentum.astype(jnp.float32) + product)
    return result.astype(jnp.bfloat16)


def solution(mesh):
    placed = (P(None, "row", "col"),)
    return jax.shard_map(
        local, mesh=mesh, in_specs=placed, out_specs=P(None, "row", "col"), check_vma=False
    )
```

profile of v0, /device:TPU:1, one launch (start us, length us, event | category | flops | bytes accessed | tf_op | source)
XLA Modules:
  0.0 300.6 jit_solution(5601518225593307363)
XLA Ops:
  6.5 0.0 all-gather.3.cloned.1.call-start
  6.5 0.7 all-gather.3.cloned.1.call-update
  7.3 0.0 reduce-scatter.4.cloned.1.call-start
  7.3 103.2 %all-gather.3.cloned.1.call-done = bf16[4,1536,448]{2,1,0:T(8,128)(2,1)} async-done(((bf16[4,48,448]{2,1,0:T(8,128)(2,1)}), bf16[4,1536,448]{2,1,0:T(8,128)(2,1)}) %all-gather.3.cloned.1.call-update) | async-done | bytes 5505040 | tf_op jit(solution)/shard_map/all_gather | solution.py:15
  110.5 5.9 %fusion.22 = f32[4,48,1536]{2,1,0:T(8,128)} fusion(bf16[4,48,448]{2,1,0:T(8,128)(2,1)} %param.1, bf16[4,1536,448]{2,1,0:T(8,128)(2,1)} %all-gather.3.cloned.1.call-done), kind=kOutput, calls=%fused_computation.10 | convolution fusion | flops 264241152 | bytes 6856704 | tf_op jit(solution)/shard_map/lin,ljn->lij/dot_general | solution.py:12
  116.3 2.8 copy.6
  119.1 2.3 reshape
  121.4 0.0 reduce-scatter.4.cloned.1.call-update
  121.4 0.0 all-gather.5.cloned.1.call-start
  121.5 55.7 %reduce-scatter.4.cloned.1.call-done = f32[96,192]{1,0:T(8,128)} async-done(((f32[1536,192]{1,0:T(8,128)}), f32[96,192]{1,0:T(8,128)}) %reduce-scatter.4.cloned.1.call-update) | async-done | bytes 73744
  177.2 1.0 reshape.1
  178.2 0.7 copy.7
  178.9 0.0 copy-start.1
  178.9 0.0 all-gather.5.cloned.1.call-update
  179.0 1.0 copy.2
  179.9 22.3 %all_gather.14 = bf16[4,48,1536]{1,0,2:T(4,128)(2,1)S(1)} all-gather(bf16[4,48,96]{1,0,2:T(4,128)(2,1)S(1)} %copy.2), channel_id=1, replica_groups=mesh['row'=32,'col'=16] {'col'}, dimensions={2}, use_global_device_ids=true | all-gather | bytes 626688 | tf_op jit(solution)/shard_map/all_gather | solution.py:21
  202.2 58.5 %all-gather.5.cloned.1.call-done = bf16[4,1536,96]{2,1,0:T(8,128)(2,1)} async-done(((bf16[4,48,96]{2,1,0:T(8,128)(2,1)}), bf16[4,1536,96]{2,1,0:T(8,128)(2,1)}) %all-gather.5.cloned.1.call-update) | async-done | bytes 1179664 | tf_op jit(solution)/shard_map/all_gather | solution.py:22
  260.7 0.0 copy-done.1
  260.7 2.0 fusion.19
  262.7 0.0 copy-start
  262.7 0.1 copy.3
  262.8 26.5 %all_gather.16 = bf16[4,48,1536]{1,0,2:T(4,128)(2,1)S(1)} all-gather(bf16[4,48,96]{1,0,2:T(4,128)(2,1)S(1)} %copy.3), channel_id=1, replica_groups=mesh['row'=32,'col'=16] {'col'}, dimensions={2}, use_global_device_ids=true | all-gather | bytes 626688 | tf_op jit(solution)/shard_map/all_gather | solution.py:29
  289.4 0.0 copy-done
  289.4 4.7 %fusion.10 = bf16[4,48,448]{2,1,0:T(8,128)(2,1)} fusion(bf16[4,1536,448]{2,1,0:T(8,128)(2,1)} %all-gather.3.cloned.1.call-done, bf16[4,48,1536]{1,0,2:T(4,128)(2,1)S(1)} %all_gather.16, bf16[4,48,448]{2,1,0:T(8,128)(2,1)S(1)} %copy-done), kind=kOutput, calls=%fused_computation.6 | convolution fusion | flops 264671232 | bytes 6438912 | tf_op jit(solution)/shard_map/lik,lkn->lin/dot_general | solution.py:30
Async XLA Ops:
  6.5 103.9 %all-gather.3.cloned.1.call-start = ((), (), s32[]{:S(2)}) async-start(), calls=%async_computation.1 | async-start | bytes 6488064 | tf_op jit(solution)/shard_map/all_gather | solution.py:15
  7.3 170.0 %reduce-scatter.4.cloned.1.call-start = ((), (), s32[]{:S(2)}) async-start(), calls=%async_computation.3 | async-start | bytes 1671168
  121.4 139.2 %all-gather.5.cloned.1.call-start = ((), (), s32[]{:S(2)}) async-start(), calls=%async_computation.2 | async-start | bytes 1622016 | tf_op jit(solution)/shard_map/all_gather | solution.py:22
  178.9 81.7 %copy-start.1 = (bf16[4,48,96]{2,1,0:T(8,128)(2,1)S(1)}, bf16[4,48,96]{2,1,0:T(8,128)(2,1)}, u32[]{:S(2)}) copy-start(bf16[4,48,96]{2,1,0:T(8,128)(2,1)} %copy.7) | copy-start | bytes 110596
  262.7 26.7 %copy-start = (bf16[4,48,448]{2,1,0:T(8,128)(2,1)S(1)}, bf16[4,48,448]{2,1,0:T(8,128)(2,1)}, u32[]{:S(2)}) copy-start(bf16[4,48,448]{2,1,0:T(8,128)(2,1)} %param.1) | copy-start | bytes 516100
Sparse Core Ops, SparseCore 0:
  10.5 99.8 all-gather.2
  121.6 55.6 reduce-scatter.3
  180.9 79.7 all-gather.4
where the time goes:
time: 301 us
  waiting for transfers between devices  218 us (72%)
  blocking collectives  48.8 us (16%)
  between operations  13.1 us (4%)
  matrix products  12.6 us (4%)
  local copies, waits for them, and re-layouts  7.88 us (3%)
    all_gather x1, waiting for transfers between devices, local(): lax.all_gather(momentum, 'row', axis=1, tiled=True)  103 us
    all_gather x1, waiting for transfers between devices, local(): gram_cols = lax.all_gather(gram_block, 'row', axis=1, tiled=True)  58.5 us
    unnamed x4, waiting for transfers between devices  56.5 us
    all_gather x1, blocking collectives, local(): poly_rows = lax.all_gather(poly_block, 'col', axis=2, tiled=True)  26.5 us
    all_gather x1, blocking collectives, local(): gram_rows = lax.all_gather(gram_block, 'col', axis=2, tiled=True)  22.3 us
    unnamed x8, local copies, waits for them, and re-layouts  6.79 us
  transfers between devices with their start and end apart: 3, of which 3 were waited for; matrix products, arithmetic and copies ran while one was open for 0% of the time, Pallas kernels for 0%

commit v1 on v0

v1 whole, which is shorter than its diff:
```python
import math

import jax
import jax.numpy as jnp
from jax import lax
from jax.sharding import Mesh, PartitionSpec as P

F32 = jnp.float32
BF16 = jnp.bfloat16
A1, A3, A5 = 3.4445, -4.775, 2.0315
ZX = ("zq", "zh", "x")
HY = ("zh", "y")


def swap(array):
    return lax.ppermute(array, "core", [(0, 1), (1, 0)])


def exchange(array, axes):
    return lax.all_to_all(array, axes, 0, 0, tiled=True)


def tiles(panel):
    return panel.reshape(4, 48, 4, 384).transpose(0, 2, 1, 3).reshape(16, 48, 384)


def panel_of(tiled):
    return tiled.reshape(4, 4, 48, 384).transpose(0, 2, 1, 3).reshape(192, 1536)


def local(momentum):
    width = 7168
    zq, core = lax.axis_index("zq"), lax.axis_index("core")
    own, other = zq * 384 + core * 192, zq * 384 + (1 - core) * 192

    low = momentum[:, :, :256]
    high = jnp.pad(momentum[:, :, 256:], ((0, 0), (0, 0), (0, 64)))
    halves = jnp.stack([low, high])
    sent = jnp.broadcast_to(halves[None], (4, 2, 4, 48, 256)).reshape(32, 48, 256)
    m = exchange(sent, ZX).reshape(1536, 256)

    m_own = lax.dynamic_slice(m, (own, 0), (192, 256))
    m_other = lax.dynamic_slice(m, (other, 0), (192, 256))

    def gram(rows):
        return lax.dot_general(rows, m, (((1,), (1,)), ((), ())), preferred_element_type=F32)

    away = swap(tiles(gram(m_other).astype(BF16)))
    part = (tiles(gram(m_own)) + away.astype(F32)).astype(BF16)
    parts = exchange(part, HY)
    tile = jnp.sum(parts.astype(F32), axis=0).astype(BF16)
    gathered = exchange(jnp.broadcast_to(tile[None], (16, 48, 384)), HY)

    def partial(tiled, rows):
        g = panel_of(tiled)
        gm = jnp.dot(g, m, preferred_element_type=F32)
        w = (A3 * rows.astype(F32) + A5 * gm).astype(BF16)
        return lax.dot_general(g, w, (((0,), (0,)), ((), ())), preferred_element_type=F32)

    total = partial(gathered, m_own) + partial(swap(gathered), m_other)
    back = exchange(total.astype(BF16).reshape(32, 48, 256), ZX)
    summed = jnp.sum(back.reshape(4, 2, 4, 48, 256).astype(F32), axis=0)
    product = jnp.concatenate([summed[0], summed[1][:, :, :192]], axis=2)
    result = 0.2 * math.sqrt(width) * (A1 * momentum.astype(F32) + product)
    return result.astype(BF16)


def solution(mesh):
    split = Mesh(mesh.devices.reshape(4, 2, 4, 8, 2), ("zq", "zh", "x", "y", "core"))
    placed = P(None, ZX, ("y", "core"))
    return jax.shard_map(local, mesh=split, in_specs=(placed,), out_specs=placed, check_vma=False)
```

time: 301 us -> 129 us (0.43)
  the two profiles are of different devices: /device:TPU:1 before, /device:TPU:2 now
where the time goes in v1:
time: 129 us
  blocking collectives  77 us (60%)
  waiting for transfers between devices  23.7 us (18%)
  starting transfers between devices  17.3 us (13%)
  local copies, waits for them, and re-layouts  4.97 us (4%)
  matrix products  4.53 us (4%)
    all_to_all x3, blocking collectives, exchange(): return lax.all_to_all(array, axes, 0, 0, tiled=True)  77 us
    all_to_all x1, waiting for transfers between devices, exchange(): return lax.all_to_all(array, axes, 0, 0, tiled=True)  22.4 us
    all_to_all x1, starting transfers between devices, exchange(): return lax.all_to_all(array, axes, 0, 0, tiled=True)  13.5 us
    ppermute x2, starting transfers between devices, swap(): return lax.ppermute(array, 'core', [(0, 1), (1, 0)])  3.83 us
    dot_general x2, matrix products, partial(): lax.dot_general(g, w, (((0,), (0,)), ((), ())), preferred_element_type=F32)  3.7 us
  transfers between devices with their start and end apart: 3, of which 2 were waited for; matrix products, arithmetic and copies ran while one was open for 2% of the time, Pallas kernels for 0%

profile of v1, /device:TPU:2, one launch (start us, length us, event | category | flops | bytes accessed | tf_op | source)
XLA Modules:
  0.0 128.8 jit_solution(12778311761524568806)
XLA Ops:
  0.0 0.9 slice.16
  0.9 0.9 pad_bitcast_fusion
  1.8 1.0 broadcast_in_dim.4
  2.8 13.5 %all-to-all-start = ((bf16[32,48,256]{2,1,0:T(8,128)(2,1)}), bf16[32,48,256]{2,1,0:T(8,128)(2,1)S(1)}, u32[]{:S(2)}, u32[]{:S(2)}) async-start(bf16[32,48,256]{2,1,0:T(8,128)(2,1)} %bitcast.2), calls=%async_computation | async-start | bytes 1572864 | tf_op jit(solution)/shard_map/all_to_all | solution.py:20
  16.3 22.4 %all-to-all-done = bf16[32,48,256]{2,1,0:T(8,128)(2,1)S(1)} async-done(((bf16[32,48,256]{2,1,0:T(8,128)(2,1)}), bf16[32,48,256]{2,1,0:T(8,128)(2,1)S(1)}, u32[]{:S(2)}, u32[]{:S(2)}) %all-to-all-start) | async-done | bytes 786464 | tf_op jit(solution)/shard_map/all_to_all | solution.py:20
  38.7 0.4 convolution_convert_fusion
  39.1 0.1 reshape.42
  39.3 0.1 copy.4
  39.4 1.9 %collective-permute-start = (bf16[16,48,384]{2,1,0:T(8,128)(2,1)S(1)}, bf16[16,48,384]{2,1,0:T(8,128)(2,1)S(1)}, u32[]{:S(2)}, u32[]{:S(2)}) collective-permute-start(bf16[16,48,384]{2,1,0:T(8,128)(2,1)S(1)} %bitcast.66), channel_id=1, source_target_pairs={{0,1},{1,0},{2,3},{3,2},{4,5},{5,4},{6,7},{7,6},{8,9},{9,8},{10,11... | collective-permute-start | bytes 1769480 | tf_op jit(solution)/shard_map/ppermute | solution.py:16
  41.3 0.0 copy-start
  41.3 0.4 fusion.25
  41.7 0.2 copy-done
  42.0 1.3 %collective-permute-done = bf16[16,48,384]{2,1,0:T(8,128)(2,1)S(1)} collective-permute-done((bf16[16,48,384]{2,1,0:T(8,128)(2,1)S(1)}, bf16[16,48,384]{2,1,0:T(8,128)(2,1)S(1)}, u32[]{:S(2)}, u32[]{:S(2)}) %collective-permute-start) | collective-permute-done | bytes 589856 | tf_op jit(solution)/shard_map/ppermute | solution.py:16
  43.3 0.1 fusion.1
  43.4 26.4 %all_to_all.20 = bf16[16,48,384]{2,1,0:T(8,128)(2,1)S(1)} all-to-all(bf16[16,48,384]{2,1,0:T(8,128)(2,1)S(1)} %fusion.1), channel_id=1, replica_groups=mesh['zq'=4,'zh'=2,'x'=4,'y'=8,'core'=2] {'zh','y'}, dimensions={0} | all-to-all | bytes 1179648 | tf_op jit(solution)/shard_map/all_to_all | solution.py:20
  69.8 0.1 reduce_sum.21
  69.9 0.1 broadcast_in_dim.5
  69.9 21.6 %all_to_all.21 = bf16[16,48,384]{2,1,0:T(8,128)(2,1)S(1)} all-to-all(bf16[16,48,384]{2,1,0:T(8,128)(2,1)S(1)} %broadcast_in_dim.5), channel_id=1, replica_groups=mesh['zq'=4,'zh'=2,'x'=4,'y'=8,'core'=2] {'zh','y'}, dimensions={0} | all-to-all | bytes 1179648 | tf_op jit(solution)/shard_map/all_to_all | solution.py:20
  91.5 1.9 %collective-permute-start.1 = (bf16[16,48,384]{2,1,0:T(8,128)(2,1)S(1)}, bf16[16,48,384]{2,1,0:T(8,128)(2,1)}, u32[]{:S(2)}, u32[]{:S(2)}) collective-permute-start(bf16[16,48,384]{2,1,0:T(8,128)(2,1)S(1)} %all_to_all.21), channel_id=1, source_target_pairs={{0,1},{1,0},{2,3},{3,2},{4,5},{5,4},{6,7},{7,6},{8,9},{9,8},{10,11... | collective-permute-start | bytes 1769480 | tf_op jit(solution)/shard_map/ppermute | solution.py:16
  93.4 0.2 copy.5
  93.6 0.1 copy.8
  93.7 1.8 %fusion.6 = f32[1536,256]{1,0:T(8,128)S(1)} fusion(bf16[192,1536]{1,0:T(8,128)(2,1)S(1)} %bitcast.57, bf16[1536,256]{1,0:T(8,128)(2,1)S(1)} %bitcast.54, bf16[192,256]{1,0:T(8,128)(2,1)} %copy-done), kind=kOutput, calls=%fused_computation.12 | convolution fusion | flops 302235648 | bytes 3047424 | tf_op jit(solution)/shard_map/dot_general | solution.py:58
  95.6 0.0 collective-permute-done.1
  95.6 1.3 %copy.6 = bf16[4,48,4,384]{3,2,1,0:T(4,128)(2,1)S(1)} copy(bf16[4,48,4,384]{3,1,2,0:T(8,128)(2,1)} %bitcast.16) | data formatting | bytes 1179648 | tf_op jit(solution)/shard_map/transpose | solution.py:28
  96.9 0.1 copy.9
  97.0 1.9 %fusion = bf16[1536,256]{1,0:T(8,128)(2,1)} fusion(f32[1536,256]{1,0:T(8,128)S(1)} %fusion.6, bf16[192,1536]{1,0:T(8,128)(2,1)S(1)} %bitcast.56, bf16[1536,256]{1,0:T(8,128)(2,1)S(1)} %bitcast.55, s32[]{:T(128)S(6)} %select_n.7), kind=kOutput, calls=%fused_computation.1 | convolution fusion | flops 303022080 | bytes 4423684 | tf_op jit(solution)/shard_map/dot_general | solution.py:58
  98.8 0.0 copy-start.1
  98.8 29.1 %all_to_all.22 = bf16[32,48,256]{2,1,0:T(8,128)(2,1)S(1)} all-to-all(bf16[32,48,256]{2,1,0:T(8,128)(2,1)} %bitcast.58), channel_id=1, replica_groups=mesh['zq'=4,'zh'=2,'x'=4,'y'=8,'core'=2] {'zq','zh','x'}, dimensions={0} | all-to-all | bytes 1572864 | tf_op jit(solution)/shard_map/all_to_all | solution.py:20
  127.9 0.1 convert_reduce_fusion
  128.1 0.0 copy-done.1
  128.1 0.7 fusion.8
  (3 shorter events, 0.1 us)
Async XLA Ops:
  2.8 35.9 %all-to-all-start = ((bf16[32,48,256]{2,1,0:T(8,128)(2,1)}), bf16[32,48,256]{2,1,0:T(8,128)(2,1)S(1)}, u32[]{:S(2)}, u32[]{:S(2)}) async-start(bf16[32,48,256]{2,1,0:T(8,128)(2,1)} %bitcast.2), calls=%async_computation | async-start | bytes 1572864 | tf_op jit(solution)/shard_map/all_to_all | solution.py:20
  39.4 3.9 %collective-permute-start = (bf16[16,48,384]{2,1,0:T(8,128)(2,1)S(1)}, bf16[16,48,384]{2,1,0:T(8,128)(2,1)S(1)}, u32[]{:S(2)}, u32[]{:S(2)}) collective-permute-start(bf16[16,48,384]{2,1,0:T(8,128)(2,1)S(1)} %bitcast.66), channel_id=1, source_target_pairs={{0,1},{1,0},{2,3},{3,2},{4,5},{5,4},{6,7},{7,6},{8,9},{9,8},{10,11... | collective-permute-start | bytes 1769480 | tf_op jit(solution)/shard_map/ppermute | solution.py:16
  41.3 0.6 copy-start
  91.5 4.1 %collective-permute-start.1 = (bf16[16,48,384]{2,1,0:T(8,128)(2,1)S(1)}, bf16[16,48,384]{2,1,0:T(8,128)(2,1)}, u32[]{:S(2)}, u32[]{:S(2)}) collective-permute-start(bf16[16,48,384]{2,1,0:T(8,128)(2,1)S(1)} %all_to_all.21), channel_id=1, source_target_pairs={{0,1},{1,0},{2,3},{3,2},{4,5},{5,4},{6,7},{7,6},{8,9},{9,8},{10,11... | collective-permute-start | bytes 1769480 | tf_op jit(solution)/shard_map/ppermute | solution.py:16
  98.8 29.2 %copy-start.1 = (bf16[4,48,448]{2,1,0:T(8,128)(2,1)S(1)}, bf16[4,48,448]{2,1,0:T(8,128)(2,1)}, u32[]{:S(2)}) copy-start(bf16[4,48,448]{2,1,0:T(8,128)(2,1)} %param.1) | copy-start | bytes 516100

commit v2 on v1

v2 whole, which is shorter than its diff:
```python
import math

import jax
import jax.numpy as jnp
from jax import lax
from jax.experimental import pallas as pl
from jax.experimental.pallas import tpu as pltpu
from jax.sharding import Mesh, PartitionSpec as P

F32 = jnp.float32
BF16 = jnp.bfloat16
A1, A3, A5 = 3.4445, -4.775, 2.0315
ZX = ("zq", "zh", "x")
HY = ("zh", "y")
VMEM = pl.BlockSpec(memory_space=pltpu.VMEM)


def kernel_call(body, inputs, shape, dtype, flops):
    return pl.pallas_call(
        body,
        out_shape=jax.ShapeDtypeStruct(shape, dtype),
        in_specs=[VMEM] * len(inputs),
        out_specs=VMEM,
        cost_estimate=pl.CostEstimate(flops=flops, bytes_accessed=0, transcendentals=0),
        compiler_params=pltpu.CompilerParams(vmem_limit_bytes=40 * 2**20),
    )(*inputs)


def swap(array):
    return lax.ppermute(array, "core", [(0, 1), (1, 0)])


def exchange(array, axes):
    return lax.all_to_all(array, axes, 0, 0, tiled=True)


def first_block(other):
    core = lax.axis_index("core")
    return lax.axis_index("zq") * 8 + (1 - core if other else core) * 4


def pack_body(momentum, sent):
    for layer in range(4):
        low = momentum[layer, :, :256]
        high = jnp.concatenate([momentum[layer, :, 256:], jnp.zeros((48, 64), BF16)], axis=1)
        for quarter in range(4):
            sent[quarter * 8 + layer] = low
            sent[quarter * 8 + 4 + layer] = high


def gram_body(other):
    def body(m, out):
        rows = m[pl.ds(first_block(other), 4)].reshape(192, 256)
        for cg in range(4):
            columns = m[cg * 8 : cg * 8 + 8].reshape(384, 256)
            block = lax.dot_general(
                rows, columns, (((1,), (1,)), ((), ())), preferred_element_type=F32
            )
            for rg in range(4):
                out[rg * 4 + cg] = block[rg * 48 : rg * 48 + 48].astype(out.dtype)

    return body


def product_terms(m, tiles, other):
    panels = [jnp.concatenate([tiles[rg * 4 + cg] for rg in range(4)], axis=0) for cg in range(4)]
    gm = jnp.zeros((192, 256), F32)
    for cg in range(4):
        rows = m[cg * 8 : cg * 8 + 8].reshape(384, 256)
        gm = gm + jnp.dot(panels[cg], rows, preferred_element_type=F32)
    own = m[pl.ds(first_block(other), 4)].reshape(192, 256).astype(F32)
    w = (A3 * own + A5 * gm).astype(BF16)
    for cg in range(4):
        yield lax.dot_general(panels[cg], w, (((0,), (0,)), ((), ())), preferred_element_type=F32)


def product_body(m, tiles, out):
    for cg, piece in enumerate(product_terms(m, tiles, False)):
        out[cg * 8 : cg * 8 + 8] = piece.reshape(8, 48, 256)


def product_add_body(m, tiles, partial, out):
    for cg, piece in enumerate(product_terms(m, tiles, True)):
        block = slice(cg * 8, cg * 8 + 8)
        out[block] = (partial[block] + piece.reshape(8, 48, 256)).astype(BF16)


def local(momentum):
    width = 7168
    m = exchange(kernel_call(pack_body, [momentum], (32, 48, 256), BF16, 10**6), ZX)

    gram_flops = 2 * 192 * 1536 * 256
    away = swap(kernel_call(gram_body(True), [m], (16, 48, 384), BF16, gram_flops))
    own = kernel_call(gram_body(False), [m], (16, 48, 384), F32, gram_flops)
    part = (own + away.astype(F32)).astype(BF16)
    parts = exchange(part, HY)
    tile = jnp.sum(parts.astype(F32), axis=0).astype(BF16)
    gathered = exchange(jnp.broadcast_to(tile[None], (16, 48, 384)), HY)

    others = swap(gathered)
    partial = kernel_call(product_body, [m, gathered], (32, 48, 256), F32, 2 * gram_flops)
    total = kernel_call(
        product_add_body, [m, others, partial], (32, 48, 256), BF16, 2 * gram_flops
    )
    back = exchange(total, ZX)
    summed = jnp.sum(back.reshape(4, 2, 4, 48, 256).astype(F32), axis=0)
    product = jnp.concatenate([summed[0], summed[1][:, :, :192]], axis=2)
    result = 0.2 * math.sqrt(width) * (A1 * momentum.astype(F32) + product)
    return result.astype(BF16)


def solution(mesh):
    split = Mesh(mesh.devices.reshape(4, 2, 4, 8, 2), ("zq", "zh", "x", "y", "core"))
    placed = P(None, ZX, ("y", "core"))
    return jax.shard_map(local, mesh=split, in_specs=(placed,), out_specs=placed, check_vma=False)
```

time: 129 us -> 125 us (0.969)
  blocking collectives: 77 us -> 112 us
  waiting for transfers between devices: 23.7 us -> 2.43 us
  starting transfers between devices: 17.3 us -> 3.83 us
  matrix products: 4.53 us -> 0 us
  local copies, waits for them, and re-layouts: 4.97 us -> 1.78 us
  Pallas kernels: 0 us -> 3.06 us
    all_to_all x3 -> x4, blocking collectives: 77 us -> 112 us  [exchange(): return lax.all_to_all(array, axes, 0, 0, tiled=True)]
    all_to_all x1 -> x0, waiting for transfers between devices: 22.4 us -> none  [exchange(): return lax.all_to_all(array, axes, 0, 0, tiled=True)]
    all_to_all x1 -> x0, starting transfers between devices: 13.5 us -> none  [exchange(): return lax.all_to_all(array, axes, 0, 0, tiled=True)]
    dot_general x4 -> x0, matrix products: 4.53 us -> none  [the longest x2 3.7 us: partial(): lax.dot_general(g, w, (((0,), (0,)), ((), ())), preferred_element_type=F32)]
    pallas_call x0 -> x5, Pallas kernels: none -> 3.06 us  [kernel_call(): pl.pallas_call(body, out_shape=jax.ShapeDtypeStruct(shape, dtype), in_spe...]
    transpose x3 -> x0, local copies, waits for them, and re-layouts: 1.6 us -> none  [the longest x2 1.52 us: panel_of(): return tiled.reshape(4, 4, 48, 384).transpose(0, 2, 1, 3).reshape(192, 1536)]
    unnamed x6 -> x4, local copies, waits for them, and re-layouts: 0.38 us -> 1.7 us
  transfers between devices with their start and end apart: 3 -> 2, of which waited for: 2 -> 2; matrix products, arithmetic and copies ran while one was open for 2% -> 0% of each run, Pallas kernels for 0% -> 1%
where the time goes in v2:
time: 125 us; the launch traced here: 124 us
  blocking collectives  112 us (90%)
  starting transfers between devices  3.83 us (3%)
  Pallas kernels  3.06 us (2%)
  waiting for transfers between devices  2.43 us (2%)
  local copies, waits for them, and re-layouts  1.78 us (1%)
    all_to_all x4, blocking collectives, exchange(): return lax.all_to_all(array, axes, 0, 0, tiled=True)  112 us
    ppermute x2, starting transfers between devices, swap(): return lax.ppermute(array, 'core', [(0, 1), (1, 0)])  3.83 us
    pallas_call x5, Pallas kernels, kernel_call(): pl.pallas_call(body, out_shape=jax.ShapeDtypeStruct(shape, dtype), in_spe...  3.06 us
  transfers between devices with their start and end apart: 2, of which 2 were waited for; matrix products, arithmetic and copies ran while one was open for 0% of the time, Pallas kernels for 1%

profile of v2, /device:TPU:2, one launch (start us, length us, event | category | flops | bytes accessed | tf_op | source)
XLA Modules:
  0.0 124.3 jit_solution(14595967460262139017)
XLA Ops:
  0.0 0.0 copy-start
  0.0 0.9 copy-done
  0.9 0.1 shard_map.17
  1.0 35.7 %all_to_all.20.m = bf16[32,48,256]{2,1,0:T(8,128)(2,1)S(1)} all-to-all(bf16[32,48,256]{2,1,0:T(8,128)(2,1)S(1)} %shard_map.17), channel_id=1, replica_groups=mesh['zq'=4,'zh'=2,'x'=4,'y'=8,'core'=2] {'zq','zh','x'}, dimensions={0} | all-to-all | bytes 1572864 | tf_op jit(solution)/shard_map/all_to_all | solution.py:34
  36.7 0.4 shard_map.19
  37.1 1.9 %collective-permute-start = (bf16[16,48,384]{2,1,0:T(8,128)(2,1)S(1)}, bf16[16,48,384]{2,1,0:T(8,128)(2,1)S(1)}, u32[]{:S(2)}, u32[]{:S(2)}) collective-permute-start(bf16[16,48,384]{2,1,0:T(8,128)(2,1)S(1)} %shard_map.19), channel_id=1, source_target_pairs={{0,1},{1,0},{2,3},{3,2},{4,5},{5,4},{6,7},{7,6},{8,9},{9,8},{10,11... | collective-permute-start | bytes 1769480 | tf_op jit(solution)/shard_map/ppermute | solution.py:30
  39.0 0.4 shard_map.18
  39.5 1.5 %collective-permute-done = bf16[16,48,384]{2,1,0:T(8,128)(2,1)S(1)} collective-permute-done((bf16[16,48,384]{2,1,0:T(8,128)(2,1)S(1)}, bf16[16,48,384]{2,1,0:T(8,128)(2,1)S(1)}, u32[]{:S(2)}, u32[]{:S(2)}) %collective-permute-start) | collective-permute-done | bytes 589856 | tf_op jit(solution)/shard_map/ppermute | solution.py:30
  41.0 0.1 add_convert_fusion
  41.1 26.4 %all_to_all.21 = bf16[16,48,384]{2,1,0:T(8,128)(2,1)S(1)} all-to-all(bf16[16,48,384]{2,1,0:T(8,128)(2,1)S(1)} %add_convert_fusion), channel_id=1, replica_groups=mesh['zq'=4,'zh'=2,'x'=4,'y'=8,'core'=2] {'zh','y'}, dimensions={0} | all-to-all | bytes 1179648 | tf_op jit(solution)/shard_map/all_to_all | solution.py:34
  67.5 0.1 reduce_sum.21
  67.6 0.1 broadcast_in_dim.2
  67.7 21.6 %all_to_all.22.tiles = bf16[16,48,384]{2,1,0:T(8,128)(2,1)S(1)} all-to-all(bf16[16,48,384]{2,1,0:T(8,128)(2,1)S(1)} %broadcast_in_dim.2), channel_id=1, replica_groups=mesh['zq'=4,'zh'=2,'x'=4,'y'=8,'core'=2] {'zh','y'}, dimensions={0} | all-to-all | bytes 1179648 | tf_op jit(solution)/shard_map/all_to_all | solution.py:34
  89.2 1.9 %collective-permute-start.1 = (bf16[16,48,384]{2,1,0:T(8,128)(2,1)S(1)}, bf16[16,48,384]{2,1,0:T(8,128)(2,1)S(1)}, u32[]{:S(2)}, u32[]{:S(2)}) collective-permute-start(bf16[16,48,384]{2,1,0:T(8,128)(2,1)S(1)} %all_to_all.22.tiles), channel_id=1, source_target_pairs={{0,1},{1,0},{2,3},{3,2},{4,5},{5,4},{6,7},{7,6},{8,9},{9,8},{10,11... | collective-permute-start | bytes 1769480 | tf_op jit(solution)/shard_map/ppermute | solution.py:30
  91.2 1.1 shard_map.20.partial
  92.2 0.9 collective-permute-done.1.tiles
  93.1 1.1 shard_map.21
  94.2 28.4 %all_to_all.23 = bf16[32,48,256]{2,1,0:T(8,128)(2,1)S(1)} all-to-all(bf16[32,48,256]{2,1,0:T(8,128)(2,1)S(1)} %shard_map.21), channel_id=1, replica_groups=mesh['zq'=4,'zh'=2,'x'=4,'y'=8,'core'=2] {'zq','zh','x'}, dimensions={0} | all-to-all | bytes 1572864 | tf_op jit(solution)/shard_map/all_to_all | solution.py:34
  122.6 0.0 copy-start.1
  122.6 0.1 convert_reduce_fusion
  122.8 0.8 copy-done.1
  123.5 0.7 fusion.1
  (1 shorter events, 0.0 us)
Async XLA Ops:
  0.0 0.9 copy-start
  37.1 3.9 %collective-permute-start = (bf16[16,48,384]{2,1,0:T(8,128)(2,1)S(1)}, bf16[16,48,384]{2,1,0:T(8,128)(2,1)S(1)}, u32[]{:S(2)}, u32[]{:S(2)}) collective-permute-start(bf16[16,48,384]{2,1,0:T(8,128)(2,1)S(1)} %shard_map.19), channel_id=1, source_target_pairs={{0,1},{1,0},{2,3},{3,2},{4,5},{5,4},{6,7},{7,6},{8,9},{9,8},{10,11... | collective-permute-start | bytes 1769480 | tf_op jit(solution)/shard_map/ppermute | solution.py:30
  89.2 3.9 %collective-permute-start.1 = (bf16[16,48,384]{2,1,0:T(8,128)(2,1)S(1)}, bf16[16,48,384]{2,1,0:T(8,128)(2,1)S(1)}, u32[]{:S(2)}, u32[]{:S(2)}) collective-permute-start(bf16[16,48,384]{2,1,0:T(8,128)(2,1)S(1)} %all_to_all.22.tiles), channel_id=1, source_target_pairs={{0,1},{1,0},{2,3},{3,2},{4,5},{5,4},{6,7},{7,6},{8,9},{9,8},{10,11... | collective-permute-start | bytes 1769480 | tf_op jit(solution)/shard_map/ppermute | solution.py:30
  122.6 0.9 copy-start.1

commit v3 on v2

v3 whole, which is shorter than its diff:
```python
import math

import jax
import jax.numpy as jnp
from jax import lax
from jax.experimental import pallas as pl
from jax.experimental.pallas import tpu as pltpu
from jax.sharding import Mesh, PartitionSpec as P

F32 = jnp.float32
BF16 = jnp.bfloat16
A1, A3, A5 = 3.4445, -4.775, 2.0315
Z = ("zl", "zh")
XZ = ("x", "zl", "zh")
HY = ("zh", "y")
VMEM = pl.BlockSpec(memory_space=pltpu.VMEM)


def kernel_call(body, inputs, shape, dtype, flops):
    return kernel_calls(body, inputs, [jax.ShapeDtypeStruct(shape, dtype)], flops)[0]


def kernel_calls(body, inputs, outputs, flops):
    return pl.pallas_call(
        body,
        out_shape=outputs,
        in_specs=[VMEM] * len(inputs),
        out_specs=[VMEM] * len(outputs),
        cost_estimate=pl.CostEstimate(flops=flops, bytes_accessed=0, transcendentals=0),
        compiler_params=pltpu.CompilerParams(vmem_limit_bytes=40 * 2**20),
    )(*inputs)


def swap(array):
    return lax.ppermute(array, "core", [(0, 1), (1, 0)])


def exchange(array, axes):
    return lax.all_to_all(array, axes, 0, 0, tiled=True)


def first_block(other):
    core = lax.axis_index("core")
    return lax.axis_index("x") * 8 + (1 - core if other else core) * 4


def pack_body(momentum, sent, kept):
    for layer in range(4):
        sent[layer * 2] = momentum[layer, :, :224]
        sent[layer * 2 + 1] = momentum[layer, :, 224:]
    kept[...] = momentum[...]


def gram_body(other):
    def body(m, out):
        rows = m[pl.ds(first_block(other), 4)].reshape(192, 224)
        for cg in range(4):
            columns = m[cg * 8 : cg * 8 + 8].reshape(384, 224)
            block = lax.dot_general(
                rows, columns, (((1,), (1,)), ((), ())), preferred_element_type=F32
            )
            for rg in range(4):
                out[rg * 4 + cg] = block[rg * 48 : rg * 48 + 48].astype(out.dtype)

    return body


def product_terms(m, tiles, other):
    panels = [jnp.concatenate([tiles[rg * 4 + cg] for rg in range(4)], axis=0) for cg in range(4)]
    gm = jnp.zeros((192, 224), F32)
    for cg in range(4):
        rows = m[cg * 8 : cg * 8 + 8].reshape(384, 224)
        gm = gm + jnp.dot(panels[cg], rows, preferred_element_type=F32)
    own = m[pl.ds(first_block(other), 4)].reshape(192, 224).astype(F32)
    w = (A3 * own + A5 * gm).astype(BF16)
    for cg in range(4):
        yield lax.dot_general(panels[cg], w, (((0,), (0,)), ((), ())), preferred_element_type=F32)


def product_body(m, tiles, out):
    for cg, piece in enumerate(product_terms(m, tiles, False)):
        out[cg * 8 : cg * 8 + 8] = piece.reshape(8, 48, 224)


def product_add_body(m, tiles, partial, out):
    for cg, piece in enumerate(product_terms(m, tiles, True)):
        block = slice(cg * 8, cg * 8 + 8)
        out[block] = (partial[block] + piece.reshape(8, 48, 224)).astype(BF16)


def local(momentum):
    width = 7168
    packed = jax.ShapeDtypeStruct((8, 48, 224), BF16)
    kept = jax.ShapeDtypeStruct(momentum.shape, BF16)
    sent, kept = kernel_calls(pack_body, [momentum], [packed, kept], 10**6)
    m = lax.all_gather(exchange(sent, Z), "x", axis=0, tiled=True)

    gram_flops = 2 * 192 * 1536 * 224
    away = swap(kernel_call(gram_body(True), [m], (16, 48, 384), BF16, gram_flops))
    own = kernel_call(gram_body(False), [m], (16, 48, 384), F32, gram_flops)
    part = (own + away.astype(F32)).astype(BF16)
    parts = exchange(part, HY)
    tile = jnp.sum(parts.astype(F32), axis=0).astype(BF16)
    gathered = exchange(jnp.broadcast_to(tile[None], (16, 48, 384)), HY)

    others = swap(gathered)
    partial = kernel_call(product_body, [m, gathered], (32, 48, 224), F32, 2 * gram_flops)
    total = kernel_call(
        product_add_body, [m, others, partial], (32, 48, 224), BF16, 2 * gram_flops
    )
    back = exchange(total, XZ)
    summed = jnp.sum(back.reshape(4, 4, 2, 48, 224).astype(F32), axis=0)
    product = jnp.concatenate([summed[:, 0], summed[:, 1]], axis=2)
    result = 0.2 * math.sqrt(width) * (A1 * kept.astype(F32) + product)
    return result.astype(BF16)


def solution(mesh):
    split = Mesh(mesh.devices.reshape(4, 2, 4, 8, 2), ("zl", "zh", "x", "y", "core"))
    placed = P(None, ("zl", "zh", "x"), ("y", "core"))
    return jax.shard_map(local, mesh=split, in_specs=(placed,), out_specs=placed, check_vma=False)
```

time: 125 us -> 122 us (0.976)
  the two profiles are of different devices: /device:TPU:2 before, /device:TPU:64 now
where the time goes in v3:
time: 122 us; the launch traced here: 121 us
  blocking collectives  110 us (90%)
  starting transfers between devices  3.83 us (3%)
  Pallas kernels  3.11 us (3%)
  waiting for transfers between devices  2.43 us (2%)
    all_to_all x4, blocking collectives, exchange(): return lax.all_to_all(array, axes, 0, 0, tiled=True)  95.1 us
    all_gather x1, blocking collectives, local(): m = lax.all_gather(exchange(sent, Z), 'x', axis=0, tiled=True)  14.6 us
    ppermute x2, starting transfers between devices, swap(): return lax.ppermute(array, 'core', [(0, 1), (1, 0)])  3.83 us
    pallas_call x5, Pallas kernels, kernel_calls(): pl.pallas_call(body, out_shape=outputs, in_specs=[VMEM] * len(inputs), ou...  3.11 us
  transfers between devices with their start and end apart: 2, of which 2 were waited for; matrix products, arithmetic and copies ran while one was open for 0% of the time, Pallas kernels for 1%

profile of v3, /device:TPU:64, one launch (start us, length us, event | category | flops | bytes accessed | tf_op | source)
XLA Modules:
  0.0 121.3 jit_solution(13541666692226006205)
XLA Ops:
  0.0 0.0 copy-start
  0.0 0.9 copy-done
  0.9 0.1 shard_map.17
  1.0 18.8 %all_to_all.20 = bf16[8,48,224]{2,1,0:T(8,128)(2,1)S(1)} all-to-all(bf16[8,48,224]{2,1,0:T(8,128)(2,1)S(1)} %get-tuple-element.8), channel_id=1, replica_groups=mesh['zl'=4,'zh'=2,'x'=4,'y'=8,'core'=2] {'zl','zh'}, dimensions={0} | all-to-all | bytes 344064 | tf_op jit(solution)/shard_map/all_to_all | solution.py:39
  19.8 14.6 %all_gather.3.m = bf16[32,48,224]{2,1,0:T(8,128)(2,1)S(1)} all-gather(bf16[8,48,224]{2,1,0:T(8,128)(2,1)S(1)} %all_to_all.20), channel_id=1, replica_groups=mesh['zl'=4,'zh'=2,'x'=4,'y'=8,'core'=2] {'x'}, dimensions={0}, use_global_device_ids=true | all-gather | bytes 860160 | tf_op jit(solution)/shard_map/all_gather | solution.py:96
  34.4 0.4 shard_map.19
  34.9 1.9 %collective-permute-start = (bf16[16,48,384]{2,1,0:T(8,128)(2,1)S(1)}, bf16[16,48,384]{2,1,0:T(8,128)(2,1)S(1)}, u32[]{:S(2)}, u32[]{:S(2)}) collective-permute-start(bf16[16,48,384]{2,1,0:T(8,128)(2,1)S(1)} %shard_map.19), channel_id=1, source_target_pairs={{0,1},{1,0},{2,3},{3,2},{4,5},{5,4},{6,7},{7,6},{8,9},{9,8},{10,11... | collective-permute-start | bytes 1769480 | tf_op jit(solution)/shard_map/ppermute | solution.py:35
  36.8 0.4 shard_map.18
  37.2 1.5 %collective-permute-done = bf16[16,48,384]{2,1,0:T(8,128)(2,1)S(1)} collective-permute-done((bf16[16,48,384]{2,1,0:T(8,128)(2,1)S(1)}, bf16[16,48,384]{2,1,0:T(8,128)(2,1)S(1)}, u32[]{:S(2)}, u32[]{:S(2)}) %collective-permute-start) | collective-permute-done | bytes 589856 | tf_op jit(solution)/shard_map/ppermute | solution.py:35
  38.8 0.1 add_convert_fusion
  38.9 26.7 %all_to_all.21 = bf16[16,48,384]{2,1,0:T(8,128)(2,1)S(1)} all-to-all(bf16[16,48,384]{2,1,0:T(8,128)(2,1)S(1)} %add_convert_fusion), channel_id=1, replica_groups=mesh['zl'=4,'zh'=2,'x'=4,'y'=8,'core'=2] {'zh','y'}, dimensions={0} | all-to-all | bytes 1179648 | tf_op jit(solution)/shard_map/all_to_all | solution.py:39
  65.6 0.1 reduce_sum.21
  65.7 0.1 broadcast_in_dim.2
  65.8 21.5 %all_to_all.22.tiles = bf16[16,48,384]{2,1,0:T(8,128)(2,1)S(1)} all-to-all(bf16[16,48,384]{2,1,0:T(8,128)(2,1)S(1)} %broadcast_in_dim.2), channel_id=1, replica_groups=mesh['zl'=4,'zh'=2,'x'=4,'y'=8,'core'=2] {'zh','y'}, dimensions={0} | all-to-all | bytes 1179648 | tf_op jit(solution)/shard_map/all_to_all | solution.py:39
  87.3 1.9 %collective-permute-start.1 = (bf16[16,48,384]{2,1,0:T(8,128)(2,1)S(1)}, bf16[16,48,384]{2,1,0:T(8,128)(2,1)S(1)}, u32[]{:S(2)}, u32[]{:S(2)}) collective-permute-start(bf16[16,48,384]{2,1,0:T(8,128)(2,1)S(1)} %all_to_all.22.tiles), channel_id=1, source_target_pairs={{0,1},{1,0},{2,3},{3,2},{4,5},{5,4},{6,7},{7,6},{8,9},{9,8},{10,11... | collective-permute-start | bytes 1769480 | tf_op jit(solution)/shard_map/ppermute | solution.py:35
  89.2 1.1 shard_map.20.partial
  90.3 0.9 collective-permute-done.1.tiles
  91.1 1.1 shard_map.21
  92.2 28.1 %all_to_all.23 = bf16[32,48,224]{2,1,0:T(8,128)(2,1)S(1)} all-to-all(bf16[32,48,224]{2,1,0:T(8,128)(2,1)S(1)} %shard_map.21), channel_id=1, replica_groups=mesh['zl'=4,'zh'=2,'x'=4,'y'=8,'core'=2] {'x','zl','zh'}, dimensions={0} | all-to-all | bytes 1376256 | tf_op jit(solution)/shard_map/all_to_all | solution.py:39
  120.3 0.1 convert_reduce_fusion
  120.5 0.8 fusion.1
  (1 shorter events, 0.0 us)
Async XLA Ops:
  0.0 0.9 copy-start
  34.9 3.9 %collective-permute-start = (bf16[16,48,384]{2,1,0:T(8,128)(2,1)S(1)}, bf16[16,48,384]{2,1,0:T(8,128)(2,1)S(1)}, u32[]{:S(2)}, u32[]{:S(2)}) collective-permute-start(bf16[16,48,384]{2,1,0:T(8,128)(2,1)S(1)} %shard_map.19), channel_id=1, source_target_pairs={{0,1},{1,0},{2,3},{3,2},{4,5},{5,4},{6,7},{7,6},{8,9},{9,8},{10,11... | collective-permute-start | bytes 1769480 | tf_op jit(solution)/shard_map/ppermute | solution.py:35
  87.3 3.9 %collective-permute-start.1 = (bf16[16,48,384]{2,1,0:T(8,128)(2,1)S(1)}, bf16[16,48,384]{2,1,0:T(8,128)(2,1)S(1)}, u32[]{:S(2)}, u32[]{:S(2)}) collective-permute-start(bf16[16,48,384]{2,1,0:T(8,128)(2,1)S(1)} %all_to_all.22.tiles), channel_id=1, source_target_pairs={{0,1},{1,0},{2,3},{3,2},{4,5},{5,4},{6,7},{7,6},{8,9},{9,8},{10,11... | collective-permute-start | bytes 1769480 | tf_op jit(solution)/shard_map/ppermute | solution.py:35

commit v4 on v3

--- a/solution.py
+++ b/solution.py
@@ -11,7 +11,6 @@
 BF16 = jnp.bfloat16
 A1, A3, A5 = 3.4445, -4.775, 2.0315
 Z = ("zl", "zh")
-XZ = ("x", "zl", "zh")
 HY = ("zh", "y")
 VMEM = pl.BlockSpec(memory_space=pltpu.VMEM)
 
@@ -65,27 +64,37 @@
     return body
 
 
-def product_terms(m, tiles, other):
-    panels = [jnp.concatenate([tiles[rg * 4 + cg] for rg in range(4)], axis=0) for cg in range(4)]
-    gm = jnp.zeros((192, 224), F32)
-    for cg in range(4):
-        rows = m[cg * 8 : cg * 8 + 8].reshape(384, 224)
-        gm = gm + jnp.dot(panels[cg], rows, preferred_element_type=F32)
-    own = m[pl.ds(first_block(other), 4)].reshape(192, 224).astype(F32)
-    w = (A3 * own + A5 * gm).astype(BF16)
-    for cg in range(4):
-        yield lax.dot_general(panels[cg], w, (((0,), (0,)), ((), ())), preferred_element_type=F32)
+def panel(tiles):
+    return [jnp.concatenate([tiles[rg * 4 + cg] for rg in range(4)], axis=0) for cg in range(4)]
 
 
-def product_body(m, tiles, out):
-    for cg, piece in enumerate(product_terms(m, tiles, False)):
-        out[cg * 8 : cg * 8 + 8] = piece.reshape(8, 48, 224)
+def times(tiles, m):
+    total = jnp.zeros((192, 224), F32)
+    for cg, piece in enumerate(panel(tiles)):
+        rows = m[cg * 8 : cg * 8 + 8].reshape(384, 224)
+        total = total + jnp.dot(piece, rows, preferred_element_type=F32)
+    return total
 
 
-def product_add_body(m, tiles, partial, out):
-    for cg, piece in enumerate(product_terms(m, tiles, True)):
-        block = slice(cg * 8, cg * 8 + 8)
-        out[block] = (partial[block] + piece.reshape(8, 48, 224)).astype(BF16)
+def weight(m, tiles, other):
+    rows = m[pl.ds(first_block(other), 4)].reshape(192, 224).astype(F32)
+    return (A3 * rows + A5 * times(tiles, m)).astype(BF16).reshape(4, 48, 224)
+
+
+def weight_body(m, tiles, out):
+    out[...] = weight(m, tiles, False)
+
+
+def weight_both_body(m, tiles, own, out):
+    core = lax.axis_index("core")
+    out[pl.ds(core * 4, 4)] = own[...]
+    out[pl.ds((1 - core) * 4, 4)] = weight(m, tiles, True)
+
+
+def product_body(w, tiles, others, out):
+    core = lax.axis_index("core")
+    out[pl.ds(core * 4, 4)] = times(tiles, w).astype(BF16).reshape(4, 48, 224)
+    out[pl.ds((1 - core) * 4, 4)] = times(others, w).astype(BF16).reshape(4, 48, 224)
 
 
 def local(momentum):
@@ -104,13 +113,12 @@
     gathered = exchange(jnp.broadcast_to(tile[None], (16, 48, 384)), HY)
 
     others = swap(gathered)
-    partial = kernel_call(product_body, [m, gathered], (32, 48, 224), F32, 2 * gram_flops)
-    total = kernel_call(
-        product_add_body, [m, others, partial], (32, 48, 224), BF16, 2 * gram_flops
-    )
-    back = exchange(total, XZ)
-    summed = jnp.sum(back.reshape(4, 4, 2, 48, 224).astype(F32), axis=0)
-    product = jnp.concatenate([summed[:, 0], summed[:, 1]], axis=2)
+    own = kernel_call(weight_body, [m, gathered], (4, 48, 224), BF16, gram_flops)
+    both = kernel_call(weight_both_body, [m, others, own], (8, 48, 224), BF16, gram_flops)
+    w = lax.all_gather(both, "x", axis=0, tiled=True)
+    rows = kernel_call(product_body, [w, gathered, others], (8, 48, 224), BF16, 2 * gram_flops)
+    back = exchange(rows, Z).reshape(4, 2, 48, 224).astype(F32)
+    product = jnp.concatenate([back[:, 0], back[:, 1]], axis=2)
     result = 0.2 * math.sqrt(width) * (A1 * kept.astype(F32) + product)
     return result.astype(BF16)
 

time: 122 us -> 121 us (level)
  the two profiles are of different devices: /device:TPU:64 before, /device:TPU:8 now
where the time goes in v4:
time: 121 us; the launch traced here: 120 us
  blocking collectives  109 us (90%)
  starting transfers between devices  3.83 us (3%)
  waiting for transfers between devices  3.16 us (3%)
  Pallas kernels  2.22 us (2%)
    all_to_all x4, blocking collectives, exchange(): return lax.all_to_all(array, axes, 0, 0, tiled=True)  79.9 us
    all_gather x1, blocking collectives, local(): m = lax.all_gather(exchange(sent, Z), 'x', axis=0, tiled=True)  14.6 us
    all_gather x1, blocking collectives, local(): w = lax.all_gather(both, 'x', axis=0, tiled=True)  14.2 us
    ppermute x2, starting transfers between devices, swap(): return lax.ppermute(array, 'core', [(0, 1), (1, 0)])  3.83 us
    ppermute x2, waiting for transfers between devices, swap(): return lax.ppermute(array, 'core', [(0, 1), (1, 0)])  3.16 us
  transfers between devices with their start and end apart: 2, of which 2 were waited for; matrix products, arithmetic and copies ran while one was open for 0% of the time, Pallas kernels for 1%

profile of v4, /device:TPU:8, one launch (start us, length us, event | category | flops | bytes accessed | tf_op | source)
XLA Modules:
  0.0 120.2 jit_solution(11431574734774633613)
XLA Ops:
  0.0 0.0 copy-start
  0.0 0.9 copy-done
  0.9 0.1 shard_map.17
  1.0 20.6 %all_to_all.20 = bf16[8,48,224]{2,1,0:T(8,128)(2,1)S(1)} all-to-all(bf16[8,48,224]{2,1,0:T(8,128)(2,1)S(1)} %get-tuple-element.8), channel_id=1, replica_groups=mesh['zl'=4,'zh'=2,'x'=4,'y'=8,'core'=2] {'zl','zh'}, dimensions={0} | all-to-all | bytes 344064 | tf_op jit(solution)/shard_map/all_to_all | solution.py:38
  21.6 14.6 %all_gather.6.m = bf16[32,48,224]{2,1,0:T(8,128)(2,1)S(1)} all-gather(bf16[8,48,224]{2,1,0:T(8,128)(2,1)S(1)} %all_to_all.20), channel_id=1, replica_groups=mesh['zl'=4,'zh'=2,'x'=4,'y'=8,'core'=2] {'x'}, dimensions={0}, use_global_device_ids=true | all-gather | bytes 860160 | tf_op jit(solution)/shard_map/all_gather | solution.py:105
  36.3 0.4 shard_map.19
  36.7 1.9 %collective-permute-start = (bf16[16,48,384]{2,1,0:T(8,128)(2,1)S(1)}, bf16[16,48,384]{2,1,0:T(8,128)(2,1)S(1)}, u32[]{:S(2)}, u32[]{:S(2)}) collective-permute-start(bf16[16,48,384]{2,1,0:T(8,128)(2,1)S(1)} %shard_map.19), channel_id=1, source_target_pairs={{0,1},{1,0},{2,3},{3,2},{4,5},{5,4},{6,7},{7,6},{8,9},{9,8},{10,11... | collective-permute-start | bytes 1769480 | tf_op jit(solution)/shard_map/ppermute | solution.py:34
  38.6 0.4 shard_map.18
  39.1 1.5 %collective-permute-done = bf16[16,48,384]{2,1,0:T(8,128)(2,1)S(1)} collective-permute-done((bf16[16,48,384]{2,1,0:T(8,128)(2,1)S(1)}, bf16[16,48,384]{2,1,0:T(8,128)(2,1)S(1)}, u32[]{:S(2)}, u32[]{:S(2)}) %collective-permute-start) | collective-permute-done | bytes 589856 | tf_op jit(solution)/shard_map/ppermute | solution.py:34
  40.6 0.1 add_convert_fusion
  40.7 25.7 %all_to_all.21 = bf16[16,48,384]{2,1,0:T(8,128)(2,1)S(1)} all-to-all(bf16[16,48,384]{2,1,0:T(8,128)(2,1)S(1)} %add_convert_fusion), channel_id=1, replica_groups=mesh['zl'=4,'zh'=2,'x'=4,'y'=8,'core'=2] {'zh','y'}, dimensions={0} | all-to-all | bytes 1179648 | tf_op jit(solution)/shard_map/all_to_all | solution.py:38
  66.4 0.1 reduce_sum.12
  66.5 0.1 broadcast_in_dim.2
  66.6 21.5 %all_to_all.22.tiles = bf16[16,48,384]{2,1,0:T(8,128)(2,1)S(1)} all-to-all(bf16[16,48,384]{2,1,0:T(8,128)(2,1)S(1)} %broadcast_in_dim.2), channel_id=1, replica_groups=mesh['zl'=4,'zh'=2,'x'=4,'y'=8,'core'=2] {'zh','y'}, dimensions={0} | all-to-all | bytes 1179648 | tf_op jit(solution)/shard_map/all_to_all | solution.py:38
  88.1 1.9 %collective-permute-start.1 = (bf16[16,48,384]{2,1,0:T(8,128)(2,1)S(1)}, bf16[16,48,384]{2,1,0:T(8,128)(2,1)S(1)}, u32[]{:S(2)}, u32[]{:S(2)}) collective-permute-start(bf16[16,48,384]{2,1,0:T(8,128)(2,1)S(1)} %all_to_all.22.tiles), channel_id=1, source_target_pairs={{0,1},{1,0},{2,3},{3,2},{4,5},{5,4},{6,7},{7,6},{8,9},{9,8},{10,11... | collective-permute-start | bytes 1769480 | tf_op jit(solution)/shard_map/ppermute | solution.py:34
  90.0 0.4 shard_map.20.own
  90.3 1.6 %collective-permute-done.1.tiles.others = bf16[16,48,384]{2,1,0:T(8,128)(2,1)S(1)} collective-permute-done((bf16[16,48,384]{2,1,0:T(8,128)(2,1)S(1)}, bf16[16,48,384]{2,1,0:T(8,128)(2,1)S(1)}, u32[]{:S(2)}, u32[]{:S(2)}) %collective-permute-start.1) | collective-permute-done | bytes 589856 | tf_op jit(solution)/shard_map/ppermute | solution.py:34
  92.0 0.4 shard_map.21
  92.3 14.2 %all_gather.7.w = bf16[32,48,224]{2,1,0:T(8,128)(2,1)S(1)} all-gather(bf16[8,48,224]{2,1,0:T(8,128)(2,1)S(1)} %shard_map.21), channel_id=1, replica_groups=mesh['zl'=4,'zh'=2,'x'=4,'y'=8,'core'=2] {'x'}, dimensions={0}, use_global_device_ids=true | all-gather | bytes 860160 | tf_op jit(solution)/shard_map/all_gather | solution.py:118
  106.6 0.6 shard_map.22
  107.1 12.2 %all_to_all.23 = bf16[8,48,224]{2,1,0:T(8,128)(2,1)S(1)} all-to-all(bf16[8,48,224]{2,1,0:T(8,128)(2,1)S(1)} %shard_map.22), channel_id=1, replica_groups=mesh['zl'=4,'zh'=2,'x'=4,'y'=8,'core'=2] {'zl','zh'}, dimensions={0} | all-to-all | bytes 344064 | tf_op jit(solution)/shard_map/all_to_all | solution.py:38
  119.4 0.8 fusion.1
  (2 shorter events, 0.1 us)
Async XLA Ops:
  0.0 0.9 copy-start
  36.7 3.9 %collective-permute-start = (bf16[16,48,384]{2,1,0:T(8,128)(2,1)S(1)}, bf16[16,48,384]{2,1,0:T(8,128)(2,1)S(1)}, u32[]{:S(2)}, u32[]{:S(2)}) collective-permute-start(bf16[16,48,384]{2,1,0:T(8,128)(2,1)S(1)} %shard_map.19), channel_id=1, source_target_pairs={{0,1},{1,0},{2,3},{3,2},{4,5},{5,4},{6,7},{7,6},{8,9},{9,8},{10,11... | collective-permute-start | bytes 1769480 | tf_op jit(solution)/shard_map/ppermute | solution.py:34
  88.1 3.9 %collective-permute-start.1 = (bf16[16,48,384]{2,1,0:T(8,128)(2,1)S(1)}, bf16[16,48,384]{2,1,0:T(8,128)(2,1)S(1)}, u32[]{:S(2)}, u32[]{:S(2)}) collective-permute-start(bf16[16,48,384]{2,1,0:T(8,128)(2,1)S(1)} %all_to_all.22.tiles), channel_id=1, source_target_pairs={{0,1},{1,0},{2,3},{3,2},{4,5},{5,4},{6,7},{7,6},{8,9},{9,8},{10,11... | collective-permute-start | bytes 1769480 | tf_op jit(solution)/shard_map/ppermute | solution.py:34

commit v5 on v4

--- a/solution.py
+++ b/solution.py
@@ -10,21 +10,18 @@
 F32 = jnp.float32
 BF16 = jnp.bfloat16
 A1, A3, A5 = 3.4445, -4.775, 2.0315
+SCALE = 0.2 * math.sqrt(7168)
 Z = ("zl", "zh")
 HY = ("zh", "y")
 VMEM = pl.BlockSpec(memory_space=pltpu.VMEM)
 
 
 def kernel_call(body, inputs, shape, dtype, flops):
-    return kernel_calls(body, inputs, [jax.ShapeDtypeStruct(shape, dtype)], flops)[0]
-
-
-def kernel_calls(body, inputs, outputs, flops):
     return pl.pallas_call(
         body,
-        out_shape=outputs,
+        out_shape=jax.ShapeDtypeStruct(shape, dtype),
         in_specs=[VMEM] * len(inputs),
-        out_specs=[VMEM] * len(outputs),
+        out_specs=VMEM,
         cost_estimate=pl.CostEstimate(flops=flops, bytes_accessed=0, transcendentals=0),
         compiler_params=pltpu.CompilerParams(vmem_limit_bytes=40 * 2**20),
     )(*inputs)
@@ -43,11 +40,52 @@
     return lax.axis_index("x") * 8 + (1 - core if other else core) * 4
 
 
-def pack_body(momentum, sent, kept):
+def pack_body(momentum, sent, kept, arrived):
+    copies = [
+        pltpu.make_async_copy(momentum.at[layer], kept.at[layer], arrived.at[layer])
+        for layer in range(4)
+    ]
+    for copy in copies:
+        copy.start()
     for layer in range(4):
-        sent[layer * 2] = momentum[layer, :, :224]
-        sent[layer * 2 + 1] = momentum[layer, :, 224:]
-    kept[...] = momentum[...]
+        copies[layer].wait()
+        sent[layer * 2] = kept[layer, :, :224]
+        sent[layer * 2 + 1] = kept[layer, :, 224:]
+
+
+def pack(momentum):
+    return pl.pallas_call(
+        pack_body,
+        out_shape=[
+            jax.ShapeDtypeStruct((8, 48, 224), BF16),
+            jax.ShapeDtypeStruct(momentum.shape, BF16),
+        ],
+        in_specs=[pl.BlockSpec(memory_space=pltpu.HBM)],
+        out_specs=[VMEM, VMEM],
+        scratch_shapes=[pltpu.SemaphoreType.DMA((4,))],
+    )(momentum)
+
+
+def finish_body(kept, back, out, held, left):
+    copies = []
+    for layer in range(4):
+        product = jnp.concatenate([back[layer * 2], back[layer * 2 + 1]], axis=1).astype(F32)
+        result = SCALE * (A1 * kept[layer].astype(F32) + product)
+        held[layer] = result.astype(BF16)
+        copies.append(pltpu.make_async_copy(held.at[layer], out.at[layer], left.at[layer]))
+        copies[layer].start()
+    for copy in copies:
+        copy.wait()
+
+
+def finish(kept, back):
+    return pl.pallas_call(
+        finish_body,
+        out_shape=jax.ShapeDtypeStruct(kept.shape, BF16),
+        in_specs=[VMEM, VMEM],
+        out_specs=pl.BlockSpec(memory_space=pltpu.HBM),
+        scratch_shapes=[pltpu.VMEM(kept.shape, BF16), pltpu.SemaphoreType.DMA((4,))],
+    )(kept, back)
 
 
 def gram_body(other):
@@ -98,10 +136,7 @@
 
 
 def local(momentum):
-    width = 7168
-    packed = jax.ShapeDtypeStruct((8, 48, 224), BF16)
-    kept = jax.ShapeDtypeStruct(momentum.shape, BF16)
-    sent, kept = kernel_calls(pack_body, [momentum], [packed, kept], 10**6)
+    sent, kept = pack(momentum)
     m = lax.all_gather(exchange(sent, Z), "x", axis=0, tiled=True)
 
     gram_flops = 2 * 192 * 1536 * 224
@@ -117,10 +152,7 @@
     both = kernel_call(weight_both_body, [m, others, own], (8, 48, 224), BF16, gram_flops)
     w = lax.all_gather(both, "x", axis=0, tiled=True)
     rows = kernel_call(product_body, [w, gathered, others], (8, 48, 224), BF16, 2 * gram_flops)
-    back = exchange(rows, Z).reshape(4, 2, 48, 224).astype(F32)
-    product = jnp.concatenate([back[:, 0], back[:, 1]], axis=2)
-    result = 0.2 * math.sqrt(width) * (A1 * kept.astype(F32) + product)
-    return result.astype(BF16)
+    return finish(kept, exchange(rows, Z))
 
 
 def solution(mesh):

time: 121 us -> 123 us (1.017)
  Pallas kernels: 2.22 us -> 5.75 us
    pallas_call x6 -> x7, Pallas kernels: 2.22 us -> 5.75 us  [the longest x5 2.1 us: kernel_call(): pl.pallas_call(body, out_shape=jax.ShapeDtypeStruct(shape, dtype), in_spe...]
where the time goes in v5:
time: 123 us
  blocking collectives  110 us (89%)
  Pallas kernels  5.75 us (5%)
  starting transfers between devices  3.83 us (3%)
  waiting for transfers between devices  3.16 us (3%)
    all_to_all x4, blocking collectives, exchange(): return lax.all_to_all(array, axes, 0, 0, tiled=True)  80.8 us
    all_gather x1, blocking collectives, local(): m = lax.all_gather(exchange(sent, Z), 'x', axis=0, tiled=True)  14.6 us
    all_gather x1, blocking collectives, local(): w = lax.all_gather(both, 'x', axis=0, tiled=True)  14.2 us
    ppermute x2, starting transfers between devices, swap(): return lax.ppermute(array, 'core', [(0, 1), (1, 0)])  3.83 us
    ppermute x2, waiting for transfers between devices, swap(): return lax.ppermute(array, 'core', [(0, 1), (1, 0)])  3.16 us
  transfers between devices with their start and end apart: 2, of which 2 were waited for; matrix products, arithmetic and copies ran while one was open for 0% of the time, Pallas kernels for 1%

profile of v5, /device:TPU:8, one launch (start us, length us, event | category | flops | bytes accessed | tf_op | source)
XLA Modules:
  0.0 122.8 jit_solution(160957413304703172)
XLA Ops:
  0.0 1.8 %shard_map.17 = (bf16[8,48,224]{2,1,0:T(8,128)(2,1)}, bf16[4,48,448]{2,1,0:T(8,128)(2,1)}) custom-call(bf16[4,48,448]{2,1,0:T(8,128)(2,1)} %momentum.1), custom_call_target="tpu_custom_call" | custom-call | tf_op jit(solution)/shard_map/pallas_call | solution.py:57
  1.8 20.8 %all_to_all.20 = bf16[8,48,224]{2,1,0:T(8,128)(2,1)S(1)} all-to-all(bf16[8,48,224]{2,1,0:T(8,128)(2,1)} %get-tuple-element.8), channel_id=1, replica_groups=mesh['zl'=4,'zh'=2,'x'=4,'y'=8,'core'=2] {'zl','zh'}, dimensions={0} | all-to-all | bytes 344064 | tf_op jit(solution)/shard_map/all_to_all | solution.py:35
  22.6 14.6 %all_gather.6.m = bf16[32,48,224]{2,1,0:T(8,128)(2,1)S(1)} all-gather(bf16[8,48,224]{2,1,0:T(8,128)(2,1)S(1)} %all_to_all.20), channel_id=1, replica_groups=mesh['zl'=4,'zh'=2,'x'=4,'y'=8,'core'=2] {'x'}, dimensions={0}, use_global_device_ids=true | all-gather | bytes 860160 | tf_op jit(solution)/shard_map/all_gather | solution.py:140
  37.3 0.4 shard_map.19
  37.7 1.9 %collective-permute-start = (bf16[16,48,384]{2,1,0:T(8,128)(2,1)S(1)}, bf16[16,48,384]{2,1,0:T(8,128)(2,1)S(1)}, u32[]{:S(2)}, u32[]{:S(2)}) collective-permute-start(bf16[16,48,384]{2,1,0:T(8,128)(2,1)S(1)} %shard_map.19), channel_id=1, source_target_pairs={{0,1},{1,0},{2,3},{3,2},{4,5},{5,4},{6,7},{7,6},{8,9},{9,8},{10,11... | collective-permute-start | bytes 1769480 | tf_op jit(solution)/shard_map/ppermute | solution.py:31
  39.6 0.4 shard_map.18
  40.1 1.6 %collective-permute-done = bf16[16,48,384]{2,1,0:T(8,128)(2,1)S(1)} collective-permute-done((bf16[16,48,384]{2,1,0:T(8,128)(2,1)S(1)}, bf16[16,48,384]{2,1,0:T(8,128)(2,1)S(1)}, u32[]{:S(2)}, u32[]{:S(2)}) %collective-permute-start) | collective-permute-done | bytes 589856 | tf_op jit(solution)/shard_map/ppermute | solution.py:31
  41.6 0.1 add_convert_fusion
  41.7 25.7 %all_to_all.21 = bf16[16,48,384]{2,1,0:T(8,128)(2,1)S(1)} all-to-all(bf16[16,48,384]{2,1,0:T(8,128)(2,1)S(1)} %add_convert_fusion), channel_id=1, replica_groups=mesh['zl'=4,'zh'=2,'x'=4,'y'=8,'core'=2] {'zh','y'}, dimensions={0} | all-to-all | bytes 1179648 | tf_op jit(solution)/shard_map/all_to_all | solution.py:35
  67.4 0.1 reduce_sum.12
  67.5 0.1 broadcast_in_dim.2
  67.6 21.5 %all_to_all.22.tiles = bf16[16,48,384]{2,1,0:T(8,128)(2,1)S(1)} all-to-all(bf16[16,48,384]{2,1,0:T(8,128)(2,1)S(1)} %broadcast_in_dim.2), channel_id=1, replica_groups=mesh['zl'=4,'zh'=2,'x'=4,'y'=8,'core'=2] {'zh','y'}, dimensions={0} | all-to-all | bytes 1179648 | tf_op jit(solution)/shard_map/all_to_all | solution.py:35
  89.1 1.9 %collective-permute-start.1 = (bf16[16,48,384]{2,1,0:T(8,128)(2,1)S(1)}, bf16[16,48,384]{2,1,0:T(8,128)(2,1)S(1)}, u32[]{:S(2)}, u32[]{:S(2)}) collective-permute-start(bf16[16,48,384]{2,1,0:T(8,128)(2,1)S(1)} %all_to_all.22.tiles), channel_id=1, source_target_pairs={{0,1},{1,0},{2,3},{3,2},{4,5},{5,4},{6,7},{7,6},{8,9},{9,8},{10,11... | collective-permute-start | bytes 1769480 | tf_op jit(solution)/shard_map/ppermute | solution.py:31
  91.0 0.4 shard_map.20.own
  91.4 1.6 %collective-permute-done.1.tiles.others = bf16[16,48,384]{2,1,0:T(8,128)(2,1)S(1)} collective-permute-done((bf16[16,48,384]{2,1,0:T(8,128)(2,1)S(1)}, bf16[16,48,384]{2,1,0:T(8,128)(2,1)S(1)}, u32[]{:S(2)}, u32[]{:S(2)}) %collective-permute-start.1) | collective-permute-done | bytes 589856 | tf_op jit(solution)/shard_map/ppermute | solution.py:31
  93.0 0.4 shard_map.21
  93.3 14.2 %all_gather.7.w = bf16[32,48,224]{2,1,0:T(8,128)(2,1)S(1)} all-gather(bf16[8,48,224]{2,1,0:T(8,128)(2,1)S(1)} %shard_map.21), channel_id=1, replica_groups=mesh['zl'=4,'zh'=2,'x'=4,'y'=8,'core'=2] {'x'}, dimensions={0}, use_global_device_ids=true | all-gather | bytes 860160 | tf_op jit(solution)/shard_map/all_gather | solution.py:153
  107.6 0.6 shard_map.22
  108.1 12.8 %all_to_all.23.back = bf16[8,48,224]{2,1,0:T(8,128)(2,1)} all-to-all(bf16[8,48,224]{2,1,0:T(8,128)(2,1)S(1)} %shard_map.22), channel_id=1, replica_groups=mesh['zl'=4,'zh'=2,'x'=4,'y'=8,'core'=2] {'zl','zh'}, dimensions={0} | all-to-all | bytes 344064 | tf_op jit(solution)/shard_map/all_to_all | solution.py:35
  121.0 1.8 %shard_map.23 = bf16[4,48,448]{2,1,0:T(8,128)(2,1)} custom-call(bf16[4,48,448]{2,1,0:T(8,128)(2,1)} %get-tuple-element.7.kept, bf16[8,48,224]{2,1,0:T(8,128)(2,1)} %all_to_all.23.back), custom_call_target="tpu_custom_call" | custom-call | tf_op jit(solution)/shard_map/pallas_call | solution.py:82
Async XLA Ops:
  37.7 3.9 %collective-permute-start = (bf16[16,48,384]{2,1,0:T(8,128)(2,1)S(1)}, bf16[16,48,384]{2,1,0:T(8,128)(2,1)S(1)}, u32[]{:S(2)}, u32[]{:S(2)}) collective-permute-start(bf16[16,48,384]{2,1,0:T(8,128)(2,1)S(1)} %shard_map.19), channel_id=1, source_target_pairs={{0,1},{1,0},{2,3},{3,2},{4,5},{5,4},{6,7},{7,6},{8,9},{9,8},{10,11... | collective-permute-start | bytes 1769480 | tf_op jit(solution)/shard_map/ppermute | solution.py:31
  89.1 3.9 %collective-permute-start.1 = (bf16[16,48,384]{2,1,0:T(8,128)(2,1)S(1)}, bf16[16,48,384]{2,1,0:T(8,128)(2,1)S(1)}, u32[]{:S(2)}, u32[]{:S(2)}) collective-permute-start(bf16[16,48,384]{2,1,0:T(8,128)(2,1)S(1)} %all_to_all.22.tiles), channel_id=1, source_target_pairs={{0,1},{1,0},{2,3},{3,2},{4,5},{5,4},{6,7},{7,6},{8,9},{9,8},{10,11... | collective-permute-start | bytes 1769480 | tf_op jit(solution)/shard_map/ppermute | solution.py:31

commit v6 on v4

v6 whole, which is shorter than its diff:
```python
import math

import jax
import jax.numpy as jnp
from jax import lax
from jax.experimental import pallas as pl
from jax.experimental.pallas import tpu as pltpu
from jax.sharding import Mesh, PartitionSpec as P

F32 = jnp.float32
BF16 = jnp.bfloat16
A1, A3, A5 = 3.4445, -4.775, 2.0315
Z = ("zl", "zh")
HY = ("zh", "y")
VMEM = pl.BlockSpec(memory_space=pltpu.VMEM)


def kernel_call(body, inputs, shape, dtype, flops):
    return kernel_calls(body, inputs, [jax.ShapeDtypeStruct(shape, dtype)], flops)[0]


def kernel_calls(body, inputs, outputs, flops):
    return pl.pallas_call(
        body,
        out_shape=outputs,
        in_specs=[VMEM] * len(inputs),
        out_specs=[VMEM] * len(outputs),
        cost_estimate=pl.CostEstimate(flops=flops, bytes_accessed=0, transcendentals=0),
        compiler_params=pltpu.CompilerParams(vmem_limit_bytes=40 * 2**20),
    )(*inputs)


def swap(array):
    return lax.ppermute(array, "core", [(0, 1), (1, 0)])


def exchange(array, axes):
    return lax.all_to_all(array, axes, 0, 0, tiled=True)


def half(m, x, h):
    return m[pl.ds(x * 8 + h * 4, 4)]


def half_rows(m, group, h):
    return jnp.concatenate([half(m, 2 * group + i, h) for i in range(2)]).reshape(384, 224)


def pack_body(momentum, sent, kept):
    for layer in range(4):
        sent[layer * 2] = momentum[layer, :, :224]
        sent[layer * 2 + 1] = momentum[layer, :, 224:]
    kept[...] = momentum[...]


def send_body(m, out):
    core = lax.axis_index("core")
    for x in range(4):
        out[x * 4 : x * 4 + 4] = half(m, x, 1 - core)
    out[16:20] = half(m, lax.axis_index("x"), core)


def gram_body(m, got, out):
    core, x = lax.axis_index("core"), lax.axis_index("x")
    other = 1 - core
    theirs = got.at[other]

    def product(rows, columns):
        return lax.dot_general(
            rows, columns, (((1,), (1,)), ((), ())), preferred_element_type=F32
        )

    for h, far in ((core, theirs[pl.ds(x * 4, 4)]), (other, theirs[16:20])):
        near = half(m, x, h).reshape(192, 224)
        far = far.reshape(192, 224)
        for group in range(2):
            block = product(near, half_rows(m, group, core))
            block = block + product(far, theirs[group * 8 : group * 8 + 8].reshape(384, 224))
            out[pl.ds(h * 4, 4), group] = block.astype(BF16).reshape(4, 48, 384)


def times(tiles, m, h):
    total = jnp.zeros((384, 224), F32)
    for group in range(2):
        panel = jnp.concatenate([tiles[2 * block + group] for block in range(8)], axis=0)
        total = total + jnp.dot(panel, half_rows(m, group, h), preferred_element_type=F32)
    return total.reshape(8, 48, 224)


def first_body(m, tiles, out):
    out[...] = times(tiles, m, lax.axis_index("core"))


def weight_body(m, others, first, out):
    gm = first[...] + times(others, m, 1 - lax.axis_index("core"))
    own = m[pl.ds(lax.axis_index("x") * 8, 8)].astype(F32)
    out[...] = (A3 * own + A5 * gm).astype(BF16)


def product_body(w, tiles, others, out):
    core = lax.axis_index("core")
    out[...] = (times(tiles, w, core) + times(others, w, 1 - core)).astype(BF16)


def local(momentum):
    width = 7168
    packed = jax.ShapeDtypeStruct((8, 48, 224), BF16)
    kept = jax.ShapeDtypeStruct(momentum.shape, BF16)
    sent, kept = kernel_calls(pack_body, [momentum], [packed, kept], 10**6)
    m = lax.all_gather(exchange(sent, Z), "x", axis=0, tiled=True)

    flops = 2 * 384 * 768 * 224
    send = kernel_call(send_body, [m], (20, 48, 224), BF16, 10**6)
    got = lax.all_gather(send, "core", axis=0)
    part = kernel_call(gram_body, [m, got], (8, 2, 48, 384), BF16, 2 * flops)
    parts = exchange(part.reshape(16, 48, 384), HY)
    tile = jnp.sum(parts.astype(F32), axis=0).astype(BF16)
    gathered = exchange(jnp.broadcast_to(tile[None], (16, 48, 384)), HY)

    others = swap(gathered)
    first = kernel_call(first_body, [m, gathered], (8, 48, 224), F32, flops)
    both = kernel_call(weight_body, [m, others, first], (8, 48, 224), BF16, flops)
    w = lax.all_gather(both, "x", axis=0, tiled=True)
    rows = kernel_call(product_body, [w, gathered, others], (8, 48, 224), BF16, 2 * flops)
    back = exchange(rows, Z).reshape(4, 2, 48, 224).astype(F32)
    product = jnp.concatenate([back[:, 0], back[:, 1]], axis=2)
    result = 0.2 * math.sqrt(width) * (A1 * kept.astype(F32) + product)
    return result.astype(BF16)


def solution(mesh):
    split = Mesh(mesh.devices.reshape(4, 2, 4, 8, 2), ("zl", "zh", "x", "y", "core"))
    placed = P(None, ("zl", "zh", "x"), ("y", "core"))
    return jax.shard_map(local, mesh=split, in_specs=(placed,), out_specs=placed, check_vma=False)
```

time: 121 us -> 119 us (0.983)
  blocking collectives: 109 us -> 111 us
  starting transfers between devices: 3.83 us -> 1.91 us
  waiting for transfers between devices: 3.16 us -> 1.6 us
    all_gather x0 -> x1, blocking collectives: none -> 2.51 us  [local(): got = lax.all_gather(send, 'core', axis=0)]
    ppermute x2 -> x1, starting transfers between devices: 3.83 us -> 1.91 us  [swap(): return lax.ppermute(array, 'core', [(0, 1), (1, 0)])]
    ppermute x2 -> x1, waiting for transfers between devices: 3.16 us -> 1.6 us  [swap(): return lax.ppermute(array, 'core', [(0, 1), (1, 0)])]
  transfers between devices with their start and end apart: 2 -> 1, of which waited for: 2 -> 1; matrix products, arithmetic and copies ran while one was open for 0% -> 0% of each run, Pallas kernels for 1% -> 0%
where the time goes in v6:
time: 119 us
  blocking collectives  111 us (93%)
  Pallas kernels  2.08 us (2%)
  starting transfers between devices  1.91 us (2%)
  waiting for transfers between devices  1.6 us (1%)
    all_to_all x4, blocking collectives, exchange(): return lax.all_to_all(array, axes, 0, 0, tiled=True)  79.9 us
    all_gather x1, blocking collectives, local(): m = lax.all_gather(exchange(sent, Z), 'x', axis=0, tiled=True)  14.6 us
    all_gather x1, blocking collectives, local(): w = lax.all_gather(both, 'x', axis=0, tiled=True)  14.2 us
    all_gather x1, blocking collectives, local(): got = lax.all_gather(send, 'core', axis=0)  2.51 us
  transfers between devices with their start and end apart: 1, of which 1 were waited for; matrix products, arithmetic and copies ran while one was open for 0% of the time, Pallas kernels for 0%

profile of v6, /device:TPU:8, one launch (start us, length us, event | category | flops | bytes accessed | tf_op | source)
XLA Modules:
  0.0 119.0 jit_solution(2969562050029254137)
XLA Ops:
  0.0 0.0 copy-start
  0.0 0.9 copy-done
  0.9 0.1 shard_map.17
  1.0 20.6 %all_to_all.20 = bf16[8,48,224]{2,1,0:T(8,128)(2,1)S(1)} all-to-all(bf16[8,48,224]{2,1,0:T(8,128)(2,1)S(1)} %get-tuple-element.8), channel_id=1, replica_groups=mesh['zl'=4,'zh'=2,'x'=4,'y'=8,'core'=2] {'zl','zh'}, dimensions={0} | all-to-all | bytes 344064 | tf_op jit(solution)/shard_map/all_to_all | solution.py:38
  21.6 14.6 %all_gather.12.m = bf16[32,48,224]{2,1,0:T(8,128)(2,1)S(1)} all-gather(bf16[8,48,224]{2,1,0:T(8,128)(2,1)S(1)} %all_to_all.20), channel_id=1, replica_groups=mesh['zl'=4,'zh'=2,'x'=4,'y'=8,'core'=2] {'x'}, dimensions={0}, use_global_device_ids=true | all-gather | bytes 860160 | tf_op jit(solution)/shard_map/all_gather | solution.py:110
  36.3 2.5 %all-gather = bf16[40,48,224]{2,1,0:T(8,128)(2,1)S(1)} all-gather(bf16[20,48,224]{2,1,0:T(8,128)(2,1)S(1)} %shard_map.18), channel_id=2, replica_groups=mesh['zl'=4,'zh'=2,'x'=4,'y'=8,'core'=2] {'core'}, dimensions={0}, use_global_device_ids=true | all-gather | bytes 1290240 | tf_op jit(solution)/shard_map/all_gather | solution.py:114
  38.8 0.7 shard_map.19
  39.5 25.7 %all_to_all.21 = bf16[16,48,384]{2,1,0:T(8,128)(2,1)S(1)} all-to-all(bf16[16,48,384]{2,1,0:T(8,128)(2,1)S(1)} %bitcast.13), channel_id=1, replica_groups=mesh['zl'=4,'zh'=2,'x'=4,'y'=8,'core'=2] {'zh','y'}, dimensions={0} | all-to-all | bytes 1179648 | tf_op jit(solution)/shard_map/all_to_all | solution.py:38
  65.2 0.1 reduce_sum.12
  65.3 0.1 broadcast_in_dim.2
  65.3 21.5 %all_to_all.22.tiles = bf16[16,48,384]{2,1,0:T(8,128)(2,1)S(1)} all-to-all(bf16[16,48,384]{2,1,0:T(8,128)(2,1)S(1)} %broadcast_in_dim.2), channel_id=1, replica_groups=mesh['zl'=4,'zh'=2,'x'=4,'y'=8,'core'=2] {'zh','y'}, dimensions={0} | all-to-all | bytes 1179648 | tf_op jit(solution)/shard_map/all_to_all | solution.py:38
  86.8 1.9 %collective-permute-start = (bf16[16,48,384]{2,1,0:T(8,128)(2,1)S(1)}, bf16[16,48,384]{2,1,0:T(8,128)(2,1)S(1)}, u32[]{:S(2)}, u32[]{:S(2)}) collective-permute-start(bf16[16,48,384]{2,1,0:T(8,128)(2,1)S(1)} %all_to_all.22.tiles), channel_id=1, source_target_pairs={{0,1},{1,0},{2,3},{3,2},{4,5},{5,4},{6,7},{7,6},{8,9},{9,8},{10,11... | collective-permute-start | bytes 1769480 | tf_op jit(solution)/shard_map/ppermute | solution.py:34
  88.8 0.4 shard_map.20.first
  89.1 1.6 %collective-permute-done.others = bf16[16,48,384]{2,1,0:T(8,128)(2,1)S(1)} collective-permute-done((bf16[16,48,384]{2,1,0:T(8,128)(2,1)S(1)}, bf16[16,48,384]{2,1,0:T(8,128)(2,1)S(1)}, u32[]{:S(2)}, u32[]{:S(2)}) %collective-permute-start) | collective-permute-done | bytes 589856 | tf_op jit(solution)/shard_map/ppermute | solution.py:34
  90.7 0.4 shard_map.21
  91.1 14.2 %all_gather.15.w = bf16[32,48,224]{2,1,0:T(8,128)(2,1)S(1)} all-gather(bf16[8,48,224]{2,1,0:T(8,128)(2,1)S(1)} %shard_map.21), channel_id=1, replica_groups=mesh['zl'=4,'zh'=2,'x'=4,'y'=8,'core'=2] {'x'}, dimensions={0}, use_global_device_ids=true | all-gather | bytes 860160 | tf_op jit(solution)/shard_map/all_gather | solution.py:123
  105.3 0.6 shard_map.22
  105.9 12.2 %all_to_all.23 = bf16[8,48,224]{2,1,0:T(8,128)(2,1)S(1)} all-to-all(bf16[8,48,224]{2,1,0:T(8,128)(2,1)S(1)} %shard_map.22), channel_id=1, replica_groups=mesh['zl'=4,'zh'=2,'x'=4,'y'=8,'core'=2] {'zl','zh'}, dimensions={0} | all-to-all | bytes 344064 | tf_op jit(solution)/shard_map/all_to_all | solution.py:38
  118.1 0.8 fusion.1
  (3 shorter events, 0.1 us)
Async XLA Ops:
  0.0 0.9 copy-start
  86.8 3.9 %collective-permute-start = (bf16[16,48,384]{2,1,0:T(8,128)(2,1)S(1)}, bf16[16,48,384]{2,1,0:T(8,128)(2,1)S(1)}, u32[]{:S(2)}, u32[]{:S(2)}) collective-permute-start(bf16[16,48,384]{2,1,0:T(8,128)(2,1)S(1)} %all_to_all.22.tiles), channel_id=1, source_target_pairs={{0,1},{1,0},{2,3},{3,2},{4,5},{5,4},{6,7},{7,6},{8,9},{9,8},{10,11... | collective-permute-start | bytes 1769480 | tf_op jit(solution)/shard_map/ppermute | solution.py:34

commit v7 on v6

--- a/solution.py
+++ b/solution.py
@@ -15,16 +15,17 @@
 VMEM = pl.BlockSpec(memory_space=pltpu.VMEM)
 
 
-def kernel_call(body, inputs, shape, dtype, flops):
-    return kernel_calls(body, inputs, [jax.ShapeDtypeStruct(shape, dtype)], flops)[0]
+def kernel_call(body, inputs, shape, dtype, flops, scratch=()):
+    return kernel_calls(body, inputs, [shape], dtype, flops, scratch)[0]
 
 
-def kernel_calls(body, inputs, outputs, flops):
+def kernel_calls(body, inputs, shapes, dtype, flops, scratch=()):
     return pl.pallas_call(
         body,
-        out_shape=outputs,
+        out_shape=[jax.ShapeDtypeStruct(shape, dtype) for shape in shapes],
         in_specs=[VMEM] * len(inputs),
-        out_specs=[VMEM] * len(outputs),
+        out_specs=[VMEM] * len(shapes),
+        scratch_shapes=scratch,
         cost_estimate=pl.CostEstimate(flops=flops, bytes_accessed=0, transcendentals=0),
         compiler_params=pltpu.CompilerParams(vmem_limit_bytes=40 * 2**20),
     )(*inputs)
@@ -53,7 +54,31 @@
     kept[...] = momentum[...]
 
 
-def send_body(m, out):
+def squeeze(blocks, out):
+    for z in range(8):
+        out[z] = blocks[z][:, :128]
+    for h in range(2):
+        tails = jnp.concatenate([blocks[h * 4 + i][:, 128:] for i in range(4)], axis=1)
+        for k in range(3):
+            out[8 + h * 3 + k] = tails[:, k * 128 : k * 128 + 128]
+
+
+def unsqueeze(packed, m):
+    for x in range(4):
+        for h in range(2):
+            tails = jnp.concatenate([packed[x * 14 + 8 + h * 3 + k] for k in range(3)], axis=1)
+            for i in range(4):
+                head = packed[x * 14 + h * 4 + i]
+                tail = tails[:, i * 96 : i * 96 + 96]
+                m[x * 8 + h * 4 + i] = jnp.concatenate([head, tail], axis=1)
+
+
+def squeeze_body(blocks, out):
+    squeeze([blocks[z] for z in range(8)], out)
+
+
+def spread_body(packed, m, out):
+    unsqueeze(packed, m)
     core = lax.axis_index("core")
     for x in range(4):
         out[x * 4 : x * 4 + 4] = half(m, x, 1 - core)
@@ -94,23 +119,31 @@
 def weight_body(m, others, first, out):
     gm = first[...] + times(others, m, 1 - lax.axis_index("core"))
     own = m[pl.ds(lax.axis_index("x") * 8, 8)].astype(F32)
-    out[...] = (A3 * own + A5 * gm).astype(BF16)
+    w = (A3 * own + A5 * gm).astype(BF16)
+    squeeze([w[z] for z in range(8)], out)
 
 
-def product_body(w, tiles, others, out):
+def product_body(packed, tiles, others, out, w):
+    unsqueeze(packed, w)
     core = lax.axis_index("core")
     out[...] = (times(tiles, w, core) + times(others, w, 1 - core)).astype(BF16)
 
 
 def local(momentum):
     width = 7168
-    packed = jax.ShapeDtypeStruct((8, 48, 224), BF16)
-    kept = jax.ShapeDtypeStruct(momentum.shape, BF16)
-    sent, kept = kernel_calls(pack_body, [momentum], [packed, kept], 10**6)
-    m = lax.all_gather(exchange(sent, Z), "x", axis=0, tiled=True)
+    sent, kept = kernel_calls(
+        pack_body, [momentum], [(8, 48, 224), momentum.shape], BF16, 10**6
+    )
+    packed = kernel_call(squeeze_body, [exchange(sent, Z)], (14, 48, 128), BF16, 10**6)
+    m, send = kernel_calls(
+        spread_body,
+        [lax.all_gather(packed, "x", axis=0, tiled=True)],
+        [(32, 48, 224), (20, 48, 224)],
+        BF16,
+        10**6,
+    )
 
     flops = 2 * 384 * 768 * 224
-    send = kernel_call(send_body, [m], (20, 48, 224), BF16, 10**6)
     got = lax.all_gather(send, "core", axis=0)
     part = kernel_call(gram_body, [m, got], (8, 2, 48, 384), BF16, 2 * flops)
     parts = exchange(part.reshape(16, 48, 384), HY)
@@ -119,9 +152,12 @@
 
     others = swap(gathered)
     first = kernel_call(first_body, [m, gathered], (8, 48, 224), F32, flops)
-    both = kernel_call(weight_body, [m, others, first], (8, 48, 224), BF16, flops)
+    both = kernel_call(weight_body, [m, others, first], (14, 48, 128), BF16, flops)
     w = lax.all_gather(both, "x", axis=0, tiled=True)
-    rows = kernel_call(product_body, [w, gathered, others], (8, 48, 224), BF16, 2 * flops)
+    whole = [pltpu.VMEM((32, 48, 224), BF16)]
+    rows = kernel_call(
+        product_body, [w, gathered, others], (8, 48, 224), BF16, 2 * flops, scratch=whole
+    )
     back = exchange(rows, Z).reshape(4, 2, 48, 224).astype(F32)
     product = jnp.concatenate([back[:, 0], back[:, 1]], axis=2)
     result = 0.2 * math.sqrt(width) * (A1 * kept.astype(F32) + product)

time: 119 us -> 119 us (level)
  the two profiles are of different devices: /device:TPU:8 before, /device:TPU:2 now
where the time goes in v7:
time: 119 us
  blocking collectives  110 us (92%)
  Pallas kernels  2.65 us (2%)
  starting transfers between devices  1.91 us (2%)
  waiting for transfers between devices  1.6 us (1%)
    all_to_all x4, blocking collectives, exchange(): return lax.all_to_all(array, axes, 0, 0, tiled=True)  81.3 us
    all_gather x1, blocking collectives, local(): w = lax.all_gather(both, 'x', axis=0, tiled=True)  13.3 us
    all_gather x1, blocking collectives, local(): lax.all_gather(packed, 'x', axis=0, tiled=True)  13.2 us
    pallas_call x7, Pallas kernels, kernel_calls(): pl.pallas_call(body, out_shape=[jax.ShapeDtypeStruct(shape, dtype) for sh...  2.65 us
    all_gather x1, blocking collectives, local(): got = lax.all_gather(send, 'core', axis=0)  2.51 us
  transfers between devices with their start and end apart: 1, of which 1 were waited for; matrix products, arithmetic and copies ran while one was open for 0% of the time, Pallas kernels for 0%

profile of v7, /device:TPU:2, one launch (start us, length us, event | category | flops | bytes accessed | tf_op | source)
XLA Modules:
  0.0 118.5 jit_solution(11817786925765620846)
XLA Ops:
  0.0 0.0 copy-start
  0.0 0.9 copy-done
  0.9 0.1 shard_map.17
  1.0 20.6 %all_to_all.20.blocks = bf16[8,48,224]{2,1,0:T(8,128)(2,1)S(1)} all-to-all(bf16[8,48,224]{2,1,0:T(8,128)(2,1)S(1)} %get-tuple-element.10), channel_id=1, replica_groups=mesh['zl'=4,'zh'=2,'x'=4,'y'=8,'core'=2] {'zl','zh'}, dimensions={0} | all-to-all | bytes 344064 | tf_op jit(solution)/shard_map/all_to_all | solution.py:39
  21.6 0.1 shard_map.18
  21.7 13.2 %all_gather.12.packed = bf16[56,48,128]{2,1,0:T(8,128)(2,1)S(1)} all-gather(bf16[14,48,128]{2,1,0:T(8,128)(2,1)S(1)} %shard_map.18), channel_id=1, replica_groups=mesh['zl'=4,'zh'=2,'x'=4,'y'=8,'core'=2] {'x'}, dimensions={0}, use_global_device_ids=true | all-gather | bytes 860160 | tf_op jit(solution)/shard_map/all_gather | solution.py:140
  34.9 0.3 shard_map.19
  35.2 2.5 %all-gather = bf16[40,48,224]{2,1,0:T(8,128)(2,1)S(1)} all-gather(bf16[20,48,224]{2,1,0:T(8,128)(2,1)S(1)} %get-tuple-element.12), channel_id=2, replica_groups=mesh['zl'=4,'zh'=2,'x'=4,'y'=8,'core'=2] {'core'}, dimensions={0}, use_global_device_ids=true | all-gather | bytes 1290240 | tf_op jit(solution)/shard_map/all_gather | solution.py:147
  37.7 0.7 shard_map.20
  38.3 26.4 %all_to_all.21 = bf16[16,48,384]{2,1,0:T(8,128)(2,1)S(1)} all-to-all(bf16[16,48,384]{2,1,0:T(8,128)(2,1)S(1)} %bitcast.13), channel_id=1, replica_groups=mesh['zl'=4,'zh'=2,'x'=4,'y'=8,'core'=2] {'zh','y'}, dimensions={0} | all-to-all | bytes 1179648 | tf_op jit(solution)/shard_map/all_to_all | solution.py:39
  64.7 0.1 reduce_sum.12
  64.8 0.1 broadcast_in_dim.2
  64.9 21.6 %all_to_all.22.tiles = bf16[16,48,384]{2,1,0:T(8,128)(2,1)S(1)} all-to-all(bf16[16,48,384]{2,1,0:T(8,128)(2,1)S(1)} %broadcast_in_dim.2), channel_id=1, replica_groups=mesh['zl'=4,'zh'=2,'x'=4,'y'=8,'core'=2] {'zh','y'}, dimensions={0} | all-to-all | bytes 1179648 | tf_op jit(solution)/shard_map/all_to_all | solution.py:39
  86.4 1.9 %collective-permute-start = (bf16[16,48,384]{2,1,0:T(8,128)(2,1)S(1)}, bf16[16,48,384]{2,1,0:T(8,128)(2,1)S(1)}, u32[]{:S(2)}, u32[]{:S(2)}) collective-permute-start(bf16[16,48,384]{2,1,0:T(8,128)(2,1)S(1)} %all_to_all.22.tiles), channel_id=1, source_target_pairs={{0,1},{1,0},{2,3},{3,2},{4,5},{5,4},{6,7},{7,6},{8,9},{9,8},{10,11... | collective-permute-start | bytes 1769480 | tf_op jit(solution)/shard_map/ppermute | solution.py:35
  88.3 0.4 shard_map.21.first
  88.7 1.6 %collective-permute-done.others = bf16[16,48,384]{2,1,0:T(8,128)(2,1)S(1)} collective-permute-done((bf16[16,48,384]{2,1,0:T(8,128)(2,1)S(1)}, bf16[16,48,384]{2,1,0:T(8,128)(2,1)S(1)}, u32[]{:S(2)}, u32[]{:S(2)}) %collective-permute-start) | collective-permute-done | bytes 589856 | tf_op jit(solution)/shard_map/ppermute | solution.py:35
  90.3 0.4 shard_map.22
  90.7 13.3 %all_gather.15.packed = bf16[56,48,128]{2,1,0:T(8,128)(2,1)S(1)} all-gather(bf16[14,48,128]{2,1,0:T(8,128)(2,1)S(1)} %shard_map.22), channel_id=1, replica_groups=mesh['zl'=4,'zh'=2,'x'=4,'y'=8,'core'=2] {'x'}, dimensions={0}, use_global_device_ids=true | all-gather | bytes 860160 | tf_op jit(solution)/shard_map/all_gather | solution.py:156
  104.0 0.8 shard_map.23
  104.8 12.8 %all_to_all.23 = bf16[8,48,224]{2,1,0:T(8,128)(2,1)S(1)} all-to-all(bf16[8,48,224]{2,1,0:T(8,128)(2,1)S(1)} %shard_map.23), channel_id=1, replica_groups=mesh['zl'=4,'zh'=2,'x'=4,'y'=8,'core'=2] {'zl','zh'}, dimensions={0} | all-to-all | bytes 344064 | tf_op jit(solution)/shard_map/all_to_all | solution.py:39
  117.7 0.8 fusion.1
  (2 shorter events, 0.1 us)
Async XLA Ops:
  0.0 0.9 copy-start
  86.4 3.9 %collective-permute-start = (bf16[16,48,384]{2,1,0:T(8,128)(2,1)S(1)}, bf16[16,48,384]{2,1,0:T(8,128)(2,1)S(1)}, u32[]{:S(2)}, u32[]{:S(2)}) collective-permute-start(bf16[16,48,384]{2,1,0:T(8,128)(2,1)S(1)} %all_to_all.22.tiles), channel_id=1, source_target_pairs={{0,1},{1,0},{2,3},{3,2},{4,5},{5,4},{6,7},{7,6},{8,9},{9,8},{10,11... | collective-permute-start | bytes 1769480 | tf_op jit(solution)/shard_map/ppermute | solution.py:35

commit v8 on v6

v8 whole, which is shorter than its diff:
```python
import math

import jax
import jax.numpy as jnp
from jax import lax
from jax.experimental import pallas as pl
from jax.experimental.pallas import tpu as pltpu
from jax.sharding import Mesh, PartitionSpec as P

F32 = jnp.float32
BF16 = jnp.bfloat16
A1, A3, A5 = 3.4445, -4.775, 2.0315
Z = ("zl", "zh")
HY = ("zh", "y")
VMEM = pl.BlockSpec(memory_space=pltpu.VMEM)


def kernel_call(body, inputs, shape, dtype, flops):
    return kernel_calls(body, inputs, [jax.ShapeDtypeStruct(shape, dtype)], flops)[0]


def kernel_calls(body, inputs, outputs, flops):
    return pl.pallas_call(
        body,
        out_shape=outputs,
        in_specs=[VMEM] * len(inputs),
        out_specs=[VMEM] * len(outputs),
        cost_estimate=pl.CostEstimate(flops=flops, bytes_accessed=0, transcendentals=0),
        compiler_params=pltpu.CompilerParams(vmem_limit_bytes=40 * 2**20),
    )(*inputs)


def swap(array):
    return lax.ppermute(array, "core", [(0, 1), (1, 0)])


def exchange(array, axes):
    return lax.all_to_all(array, axes, 0, 0, tiled=True)


def stack(blocks):
    return jnp.concatenate([block.reshape(192, 224) for block in blocks], axis=0)


def pack_body(momentum, sent, kept):
    for layer in range(4):
        sent[layer * 2] = momentum[layer, :, :224]
        sent[layer * 2 + 1] = momentum[layer, :, 224:]
    kept[...] = momentum[...]


def shard_body(both, out):
    for columns in range(2):
        out[columns] = both[columns, pl.ds(lax.axis_index("core") * 4, 4)]


def gram_body(both, m, out):
    for group in range(2):
        total = jnp.zeros((384, 384), F32)
        for columns in range(2):
            total = total + lax.dot_general(
                both[columns].reshape(384, 224),
                stack([m[2 * group + i, columns] for i in range(2)]),
                (((1,), (1,)), ((), ())),
                preferred_element_type=F32,
            )
        out[:, group] = total.astype(BF16).reshape(8, 48, 384)


def send_body(m, out):
    out[...] = m[:, 1 - lax.axis_index("core")]


def times(tiles, groups):
    total = jnp.zeros((384, 224), F32)
    for group in range(2):
        panel = jnp.concatenate([tiles[2 * block + group] for block in range(8)], axis=0)
        total = total + jnp.dot(panel, groups[group], preferred_element_type=F32)
    return total.reshape(8, 48, 224)


def first_body(m, tiles, out):
    core = lax.axis_index("core")
    out[...] = times(tiles, [stack([m[2 * g + i, core] for i in range(2)]) for g in range(2)])


def weight_body(both, got, others, first, out):
    core = lax.axis_index("core")
    theirs = got.at[1 - core]
    groups = [stack([theirs[2 * g + i] for i in range(2)]) for g in range(2)]
    gm = first[...] + times(others, groups)
    out[...] = (A3 * both[core].astype(F32) + A5 * gm).astype(BF16)


def product_body(w, tiles, others, out):
    core = lax.axis_index("core")
    total = jnp.zeros((8, 48, 224), F32)
    for held, h in ((tiles, core), (others, 1 - core)):
        groups = [
            stack([w[2 * g + i, pl.ds(h * 4, 4)] for i in range(2)]) for g in range(2)
        ]
        total = total + times(held, groups)
    out[...] = total.astype(BF16)


def local(momentum):
    width = 7168
    packed = jax.ShapeDtypeStruct((8, 48, 224), BF16)
    kept = jax.ShapeDtypeStruct(momentum.shape, BF16)
    sent, kept = kernel_calls(pack_body, [momentum], [packed, kept], 10**6)
    flops = 2 * 384 * 768 * 224
    both = lax.all_gather(exchange(sent, Z), "core", axis=0)
    shard = kernel_call(shard_body, [both], (2, 4, 48, 224), BF16, 10**6)
    m = lax.all_gather(shard, "x", axis=0)
    part = kernel_call(gram_body, [both, m], (8, 2, 48, 384), BF16, 2 * flops)
    parts = exchange(part.reshape(16, 48, 384), HY)
    tile = jnp.sum(parts.astype(F32), axis=0).astype(BF16)
    tile, later = lax.optimization_barrier((tile, m))
    gathered = exchange(jnp.broadcast_to(tile[None], (16, 48, 384)), HY)
    send = kernel_call(send_body, [later], (4, 4, 48, 224), BF16, 10**6)
    got = lax.all_gather(send, "core", axis=0)
    gathered, got = lax.optimization_barrier((gathered, got))

    others = swap(gathered)
    first = kernel_call(first_body, [m, gathered], (8, 48, 224), F32, flops)
    weighted = kernel_call(
        weight_body, [both, got, others, first], (8, 48, 224), BF16, flops
    )
    w = lax.all_gather(weighted, "x", axis=0)
    rows = kernel_call(product_body, [w, gathered, others], (8, 48, 224), BF16, 2 * flops)
    back = exchange(rows, Z).reshape(4, 2, 48, 224).astype(F32)
    product = jnp.concatenate([back[:, 0], back[:, 1]], axis=2)
    result = 0.2 * math.sqrt(width) * (A1 * kept.astype(F32) + product)
    return result.astype(BF16)


def solution(mesh):
    split = Mesh(mesh.devices.reshape(4, 2, 4, 8, 2), ("zl", "zh", "x", "y", "core"))
    placed = P(None, ("zl", "zh", "x"), ("y", "core"))
    return jax.shard_map(local, mesh=split, in_specs=(placed,), out_specs=placed, check_vma=False)
```

time: 119 us -> 115 us (0.966)
  blocking collectives: 111 us -> 89.6 us
  waiting for transfers between devices: 1.6 us -> 13.9 us
  starting transfers between devices: 1.91 us -> 6.33 us
    all_to_all x4 -> x3, blocking collectives: 79.9 us -> 56.7 us  [exchange(): return lax.all_to_all(array, axes, 0, 0, tiled=True)]
    all_to_all x0 -> x1, waiting for transfers between devices: none -> 12.3 us  [exchange(): return lax.all_to_all(array, axes, 0, 0, tiled=True)]
    all_to_all x0 -> x1, starting transfers between devices: none -> 4.42 us  [exchange(): return lax.all_to_all(array, axes, 0, 0, tiled=True)]
    all_gather x2 -> x3, blocking collectives: 28.9 us -> 30.5 us  [the longest x1 14.5 us: local(): w = lax.all_gather(weighted, 'x', axis=0)]
  transfers between devices with their start and end apart: 1 -> 2, of which waited for: 1 -> 2; matrix products, arithmetic and copies ran while one was open for 0% -> 0% of each run, Pallas kernels for 0% -> 0%
where the time goes in v8:
time: 115 us
  blocking collectives  89.6 us (78%)
  waiting for transfers between devices  13.9 us (12%)
  starting transfers between devices  6.33 us (6%)
  Pallas kernels  2 us (2%)
  local copies, waits for them, and re-layouts  1.82 us (2%)
    all_to_all x3, blocking collectives, exchange(): return lax.all_to_all(array, axes, 0, 0, tiled=True)  56.7 us
    all_gather x1, blocking collectives, local(): w = lax.all_gather(weighted, 'x', axis=0)  14.5 us
    all_gather x1, blocking collectives, local(): m = lax.all_gather(shard, 'x', axis=0)  13.9 us
    all_to_all x1, waiting for transfers between devices, exchange(): return lax.all_to_all(array, axes, 0, 0, tiled=True)  12.3 us
    all_to_all x1, starting transfers between devices, exchange(): return lax.all_to_all(array, axes, 0, 0, tiled=True)  4.42 us
    all_gather x1, blocking collectives, local(): got = lax.all_gather(send, 'core', axis=0)  2.37 us
  transfers between devices with their start and end apart: 2, of which 2 were waited for; matrix products, arithmetic and copies ran while one was open for 0% of the time, Pallas kernels for 0%

profile of v8, /device:TPU:8, one launch (start us, length us, event | category | flops | bytes accessed | tf_op | source)
XLA Modules:
  0.0 114.7 jit_solution(2043956032574445511)
XLA Ops:
  0.0 0.0 copy-start
  0.0 0.9 copy-done
  0.9 0.1 shard_map.17
  1.0 20.6 %all_to_all.20 = bf16[8,48,224]{2,1,0:T(8,128)(2,1)S(1)} all-to-all(bf16[8,48,224]{2,1,0:T(8,128)(2,1)S(1)} %get-tuple-element.12), channel_id=1, replica_groups=mesh['zl'=4,'zh'=2,'x'=4,'y'=8,'core'=2] {'zl','zh'}, dimensions={0} | all-to-all | bytes 344064 | tf_op jit(solution)/shard_map/all_to_all | solution.py:38
  21.6 2.1 %all-gather = bf16[16,48,224]{2,1,0:T(8,128)(2,1)S(1)} all-gather(bf16[8,48,224]{2,1,0:T(8,128)(2,1)S(1)} %all_to_all.20), channel_id=2, replica_groups=mesh['zl'=4,'zh'=2,'x'=4,'y'=8,'core'=2] {'core'}, dimensions={0}, use_global_device_ids=true | all-gather | bytes 516096 | tf_op jit(solution)/shard_map/all_gather | solution.py:112
  23.7 13.9 %all-gather.1 = bf16[8,4,48,224]{3,2,1,0:T(8,128)(2,1)S(1)} all-gather(bf16[2,4,48,224]{3,2,1,0:T(8,128)(2,1)S(1)} %shard_map.18), channel_id=3, replica_groups=mesh['zl'=4,'zh'=2,'x'=4,'y'=8,'core'=2] {'x'}, dimensions={0}, use_global_device_ids=true | all-gather | bytes 860160 | tf_op jit(solution)/shard_map/all_gather | solution.py:114
  37.6 0.6 shard_map.19
  38.2 23.9 %all_to_all.21 = bf16[16,48,384]{2,1,0:T(8,128)(2,1)S(1)} all-to-all(bf16[16,48,384]{2,1,0:T(8,128)(2,1)S(1)} %bitcast.23), channel_id=1, replica_groups=mesh['zl'=4,'zh'=2,'x'=4,'y'=8,'core'=2] {'zh','y'}, dimensions={0} | all-to-all | bytes 1179648 | tf_op jit(solution)/shard_map/all_to_all | solution.py:38
  62.0 0.1 reduce_sum.12
  62.1 0.9 broadcast_in_dim.2
  63.0 4.4 %all-to-all-start.2 = ((bf16[16,48,384]{2,1,0:T(8,128)(2,1)}), bf16[16,48,384]{2,1,0:T(8,128)(2,1)S(1)}, u32[]{:S(2)}, u32[]{:S(2)}) async-start(bf16[16,48,384]{2,1,0:T(8,128)(2,1)} %broadcast_in_dim.2), calls=%async_computation.2 | async-start | bytes 1179648 | tf_op jit(solution)/shard_map/all_to_all | solution.py:38
  67.5 2.4 %all-gather.2 = bf16[8,4,48,224]{3,2,1,0:T(8,128)(2,1)S(1)} all-gather(bf16[4,4,48,224]{3,2,1,0:T(8,128)(2,1)S(1)} %shard_map.20), channel_id=4, replica_groups=mesh['zl'=4,'zh'=2,'x'=4,'y'=8,'core'=2] {'core'}, dimensions={0}, use_global_device_ids=true | all-gather | bytes 1032192 | tf_op jit(solution)/shard_map/all_gather | solution.py:121
  69.8 12.3 %all-to-all-done.2.tiles = bf16[16,48,384]{2,1,0:T(8,128)(2,1)S(1)} async-done(((bf16[16,48,384]{2,1,0:T(8,128)(2,1)}), bf16[16,48,384]{2,1,0:T(8,128)(2,1)S(1)}, u32[]{:S(2)}, u32[]{:S(2)}) %all-to-all-start.2) | async-done | bytes 589856 | tf_op jit(solution)/shard_map/all_to_all | solution.py:38
  82.2 1.9 %collective-permute-start = (bf16[16,48,384]{2,1,0:T(8,128)(2,1)S(1)}, bf16[16,48,384]{2,1,0:T(8,128)(2,1)S(1)}, u32[]{:S(2)}, u32[]{:S(2)}) collective-permute-start(bf16[16,48,384]{2,1,0:T(8,128)(2,1)S(1)} %all-to-all-done.2.tiles), channel_id=1, source_target_pairs={{0,1},{1,0},{2,3},{3,2},{4,5},{5,4},{6,7},{7,6},{8,9},{9,8},{10,11... | collective-permute-start | bytes 1769480 | tf_op jit(solution)/shard_map/ppermute | solution.py:34
  84.1 0.4 shard_map.21.first
  84.5 1.6 %collective-permute-done.others = bf16[16,48,384]{2,1,0:T(8,128)(2,1)S(1)} collective-permute-done((bf16[16,48,384]{2,1,0:T(8,128)(2,1)S(1)}, bf16[16,48,384]{2,1,0:T(8,128)(2,1)S(1)}, u32[]{:S(2)}, u32[]{:S(2)}) %collective-permute-start) | collective-permute-done | bytes 589856 | tf_op jit(solution)/shard_map/ppermute | solution.py:34
  86.1 0.4 shard_map.22
  86.4 14.5 %all-gather.3 = bf16[32,48,224]{2,1,0:T(8,128)(2,1)S(1)} all-gather(bf16[8,48,224]{2,1,0:T(8,128)(2,1)S(1)} %shard_map.22), channel_id=5, replica_groups=mesh['zl'=4,'zh'=2,'x'=4,'y'=8,'core'=2] {'x'}, dimensions={0}, use_global_device_ids=true | all-gather | bytes 860160 | tf_op jit(solution)/shard_map/all_gather | solution.py:129
  100.9 0.6 shard_map.23
  101.5 12.3 %all_to_all.22 = bf16[8,48,224]{2,1,0:T(8,128)(2,1)S(1)} all-to-all(bf16[8,48,224]{2,1,0:T(8,128)(2,1)S(1)} %shard_map.23), channel_id=1, replica_groups=mesh['zl'=4,'zh'=2,'x'=4,'y'=8,'core'=2] {'zl','zh'}, dimensions={0} | all-to-all | bytes 344064 | tf_op jit(solution)/shard_map/all_to_all | solution.py:38
  113.9 0.8 fusion.1
  (4 shorter events, 0.1 us)
Async XLA Ops:
  0.0 0.9 copy-start
  63.0 19.2 %all-to-all-start.2 = ((bf16[16,48,384]{2,1,0:T(8,128)(2,1)}), bf16[16,48,384]{2,1,0:T(8,128)(2,1)S(1)}, u32[]{:S(2)}, u32[]{:S(2)}) async-start(bf16[16,48,384]{2,1,0:T(8,128)(2,1)} %broadcast_in_dim.2), calls=%async_computation.2 | async-start | bytes 1179648 | tf_op jit(solution)/shard_map/all_to_all | solution.py:38
  82.2 3.9 %collective-permute-start = (bf16[16,48,384]{2,1,0:T(8,128)(2,1)S(1)}, bf16[16,48,384]{2,1,0:T(8,128)(2,1)S(1)}, u32[]{:S(2)}, u32[]{:S(2)}) collective-permute-start(bf16[16,48,384]{2,1,0:T(8,128)(2,1)S(1)} %all-to-all-done.2.tiles), channel_id=1, source_target_pairs={{0,1},{1,0},{2,3},{3,2},{4,5},{5,4},{6,7},{7,6},{8,9},{9,8},{10,11... | collective-permute-start | bytes 1769480 | tf_op jit(solution)/shard_map/ppermute | solution.py:34

commit v9 on v8

--- a/solution.py
+++ b/solution.py
@@ -67,8 +67,13 @@
         out[:, group] = total.astype(BF16).reshape(8, 48, 384)
 
 
-def send_body(m, out):
-    out[...] = m[:, 1 - lax.axis_index("core")]
+def tile_body(parts, out):
+    total = parts[0].astype(F32)
+    for k in range(1, 16):
+        total = total + parts[k].astype(F32)
+    tile = total.astype(BF16)
+    for k in range(16):
+        out[k] = tile
 
 
 def times(tiles, groups):
@@ -79,16 +84,16 @@
     return total.reshape(8, 48, 224)
 
 
-def first_body(m, tiles, out):
+def gm_body(m, tiles, keep, send):
     core = lax.axis_index("core")
-    out[...] = times(tiles, [stack([m[2 * g + i, core] for i in range(2)]) for g in range(2)])
+    for columns, out in ((1 - core, send), (core, keep)):
+        groups = [stack([m[2 * g + i, columns] for i in range(2)]) for g in range(2)]
+        out[...] = times(tiles, groups).astype(out.dtype)
 
 
-def weight_body(both, got, others, first, out):
+def weight_body(both, keep, got, out):
     core = lax.axis_index("core")
-    theirs = got.at[1 - core]
-    groups = [stack([theirs[2 * g + i] for i in range(2)]) for g in range(2)]
-    gm = first[...] + times(others, groups)
+    gm = keep[...] + got[1 - core].astype(F32)
     out[...] = (A3 * both[core].astype(F32) + A5 * gm).astype(BF16)
 
 
@@ -114,18 +119,15 @@
     m = lax.all_gather(shard, "x", axis=0)
     part = kernel_call(gram_body, [both, m], (8, 2, 48, 384), BF16, 2 * flops)
     parts = exchange(part.reshape(16, 48, 384), HY)
-    tile = jnp.sum(parts.astype(F32), axis=0).astype(BF16)
-    tile, later = lax.optimization_barrier((tile, m))
-    gathered = exchange(jnp.broadcast_to(tile[None], (16, 48, 384)), HY)
-    send = kernel_call(send_body, [later], (4, 4, 48, 224), BF16, 10**6)
-    got = lax.all_gather(send, "core", axis=0)
-    gathered, got = lax.optimization_barrier((gathered, got))
+    copies = kernel_call(tile_body, [parts], (16, 48, 384), BF16, 10**6)
+    gathered = exchange(copies, HY)
 
     others = swap(gathered)
-    first = kernel_call(first_body, [m, gathered], (8, 48, 224), F32, flops)
-    weighted = kernel_call(
-        weight_body, [both, got, others, first], (8, 48, 224), BF16, flops
-    )
+    block = (8, 48, 224)
+    outputs = [jax.ShapeDtypeStruct(block, F32), jax.ShapeDtypeStruct(block, BF16)]
+    keep, send = kernel_calls(gm_body, [m, gathered], outputs, 2 * flops)
+    got = lax.all_gather(send, "core", axis=0)
+    weighted = kernel_call(weight_body, [both, keep, got], block, BF16, 10**6)
     w = lax.all_gather(weighted, "x", axis=0)
     rows = kernel_call(product_body, [w, gathered, others], (8, 48, 224), BF16, 2 * flops)
     back = exchange(rows, Z).reshape(4, 2, 48, 224).astype(F32)

time: 115 us -> 116 us (level)
  blocking collectives: 89.6 us -> 110 us
  waiting for transfers between devices: 13.9 us -> 0.01 us
  starting transfers between devices: 6.33 us -> 1.91 us
    all_to_all x3 -> x4, blocking collectives: 56.7 us -> 77.1 us  [exchange(): return lax.all_to_all(array, axes, 0, 0, tiled=True)]
    all_to_all x1 -> x0, waiting for transfers between devices: 12.3 us -> none  [exchange(): return lax.all_to_all(array, axes, 0, 0, tiled=True)]
    all_to_all x1 -> x0, starting transfers between devices: 4.42 us -> none  [exchange(): return lax.all_to_all(array, axes, 0, 0, tiled=True)]
    ppermute x1, waiting for transfers between devices: 1.6 us -> 0.01 us  [swap(): return lax.ppermute(array, 'core', [(0, 1), (1, 0)])]
  transfers between devices with their start and end apart: 2 -> 1, of which waited for: 2 -> 0; matrix products, arithmetic and copies ran while one was open for 0% -> 0% of each run, Pallas kernels for 0% -> 1%
where the time goes in v9:
time: 116 us
  blocking collectives  110 us (95%)
  Pallas kernels  2.01 us (2%)
  starting transfers between devices  1.91 us (2%)
    all_to_all x4, blocking collectives, exchange(): return lax.all_to_all(array, axes, 0, 0, tiled=True)  77.1 us
    all_gather x1, blocking collectives, local(): w = lax.all_gather(weighted, 'x', axis=0)  14.6 us
    all_gather x1, blocking collectives, local(): m = lax.all_gather(shard, 'x', axis=0)  13.9 us
  transfers between devices with their start and end apart: 1, of which 0 were waited for; matrix products, arithmetic and copies ran while one was open for 0% of the time, Pallas kernels for 1%

profile of v9, /device:TPU:8, one launch (start us, length us, event | category | flops | bytes accessed | tf_op | source)
XLA Modules:
  0.0 115.7 jit_solution(6860987838693135646)
XLA Ops:
  0.0 0.0 copy-start
  0.0 0.9 copy-done
  0.9 0.1 shard_map.17
  1.0 20.6 %all_to_all.20 = bf16[8,48,224]{2,1,0:T(8,128)(2,1)S(1)} all-to-all(bf16[8,48,224]{2,1,0:T(8,128)(2,1)S(1)} %get-tuple-element.10), channel_id=1, replica_groups=mesh['zl'=4,'zh'=2,'x'=4,'y'=8,'core'=2] {'zl','zh'}, dimensions={0} | all-to-all | bytes 344064 | tf_op jit(solution)/shard_map/all_to_all | solution.py:38
  21.6 2.1 %all-gather = bf16[16,48,224]{2,1,0:T(8,128)(2,1)S(1)} all-gather(bf16[8,48,224]{2,1,0:T(8,128)(2,1)S(1)} %all_to_all.20), channel_id=2, replica_groups=mesh['zl'=4,'zh'=2,'x'=4,'y'=8,'core'=2] {'core'}, dimensions={0}, use_global_device_ids=true | all-gather | bytes 516096 | tf_op jit(solution)/shard_map/all_gather | solution.py:117
  23.7 13.9 %all-gather.1 = bf16[8,4,48,224]{3,2,1,0:T(8,128)(2,1)S(1)} all-gather(bf16[2,4,48,224]{3,2,1,0:T(8,128)(2,1)S(1)} %shard_map.18), channel_id=3, replica_groups=mesh['zl'=4,'zh'=2,'x'=4,'y'=8,'core'=2] {'x'}, dimensions={0}, use_global_device_ids=true | all-gather | bytes 860160 | tf_op jit(solution)/shard_map/all_gather | solution.py:119
  37.6 0.6 shard_map.19
  38.2 23.9 %all_to_all.21.parts = bf16[16,48,384]{2,1,0:T(8,128)(2,1)S(1)} all-to-all(bf16[16,48,384]{2,1,0:T(8,128)(2,1)S(1)} %bitcast.21), channel_id=1, replica_groups=mesh['zl'=4,'zh'=2,'x'=4,'y'=8,'core'=2] {'zh','y'}, dimensions={0} | all-to-all | bytes 1179648 | tf_op jit(solution)/shard_map/all_to_all | solution.py:38
  62.0 0.1 shard_map.20
  62.1 20.5 %all_to_all.22.tiles = bf16[16,48,384]{2,1,0:T(8,128)(2,1)S(1)} all-to-all(bf16[16,48,384]{2,1,0:T(8,128)(2,1)S(1)} %shard_map.20), channel_id=1, replica_groups=mesh['zl'=4,'zh'=2,'x'=4,'y'=8,'core'=2] {'zh','y'}, dimensions={0} | all-to-all | bytes 1179648 | tf_op jit(solution)/shard_map/all_to_all | solution.py:38
  82.7 1.9 %collective-permute-start = (bf16[16,48,384]{2,1,0:T(8,128)(2,1)S(1)}, bf16[16,48,384]{2,1,0:T(8,128)(2,1)S(1)}, u32[]{:S(2)}, u32[]{:S(2)}) collective-permute-start(bf16[16,48,384]{2,1,0:T(8,128)(2,1)S(1)} %all_to_all.22.tiles), channel_id=1, source_target_pairs={{0,1},{1,0},{2,3},{3,2},{4,5},{5,4},{6,7},{7,6},{8,9},{9,8},{10,11... | collective-permute-start | bytes 1769480 | tf_op jit(solution)/shard_map/ppermute | solution.py:34
  84.6 0.6 shard_map.21
  85.2 2.2 %all-gather.2 = bf16[16,48,224]{2,1,0:T(8,128)(2,1)S(1)} all-gather(bf16[8,48,224]{2,1,0:T(8,128)(2,1)S(1)} %get-tuple-element.12), channel_id=4, replica_groups=mesh['zl'=4,'zh'=2,'x'=4,'y'=8,'core'=2] {'core'}, dimensions={0}, use_global_device_ids=true | all-gather | bytes 516096 | tf_op jit(solution)/shard_map/all_gather | solution.py:129
  87.4 0.1 shard_map.22
  87.5 14.6 %all-gather.3 = bf16[32,48,224]{2,1,0:T(8,128)(2,1)S(1)} all-gather(bf16[8,48,224]{2,1,0:T(8,128)(2,1)S(1)} %shard_map.22), channel_id=5, replica_groups=mesh['zl'=4,'zh'=2,'x'=4,'y'=8,'core'=2] {'x'}, dimensions={0}, use_global_device_ids=true | all-gather | bytes 860160 | tf_op jit(solution)/shard_map/all_gather | solution.py:131
  102.0 0.0 collective-permute-done.others
  102.0 0.6 shard_map.23
  102.6 12.2 %all_to_all.23 = bf16[8,48,224]{2,1,0:T(8,128)(2,1)S(1)} all-to-all(bf16[8,48,224]{2,1,0:T(8,128)(2,1)S(1)} %shard_map.23), channel_id=1, replica_groups=mesh['zl'=4,'zh'=2,'x'=4,'y'=8,'core'=2] {'zl','zh'}, dimensions={0} | all-to-all | bytes 344064 | tf_op jit(solution)/shard_map/all_to_all | solution.py:38
  114.8 0.8 fusion.1
  (3 shorter events, 0.1 us)
Async XLA Ops:
  0.0 0.9 copy-start
  82.7 19.4 %collective-permute-start = (bf16[16,48,384]{2,1,0:T(8,128)(2,1)S(1)}, bf16[16,48,384]{2,1,0:T(8,128)(2,1)S(1)}, u32[]{:S(2)}, u32[]{:S(2)}) collective-permute-start(bf16[16,48,384]{2,1,0:T(8,128)(2,1)S(1)} %all_to_all.22.tiles), channel_id=1, source_target_pairs={{0,1},{1,0},{2,3},{3,2},{4,5},{5,4},{6,7},{7,6},{8,9},{9,8},{10,11... | collective-permute-start | bytes 1769480 | tf_op jit(solution)/shard_map/ppermute | solution.py:34

commit v10 on v8

--- a/solution.py
+++ b/solution.py
@@ -10,6 +10,7 @@
 F32 = jnp.float32
 BF16 = jnp.bfloat16
 A1, A3, A5 = 3.4445, -4.775, 2.0315
+SCALE = 0.2 * math.sqrt(7168)
 Z = ("zl", "zh")
 HY = ("zh", "y")
 VMEM = pl.BlockSpec(memory_space=pltpu.VMEM)
@@ -67,6 +68,14 @@
         out[:, group] = total.astype(BF16).reshape(8, 48, 384)
 
 
+def base_body(both, out):
+    out[...] = A3 * both[lax.axis_index("core")].astype(F32)
+
+
+def kept_body(kept, out):
+    out[...] = SCALE * A1 * kept[...].astype(F32)
+
+
 def send_body(m, out):
     out[...] = m[:, 1 - lax.axis_index("core")]
 
@@ -84,12 +93,12 @@
     out[...] = times(tiles, [stack([m[2 * g + i, core] for i in range(2)]) for g in range(2)])
 
 
-def weight_body(both, got, others, first, out):
+def weight_body(base, got, others, first, out):
     core = lax.axis_index("core")
     theirs = got.at[1 - core]
     groups = [stack([theirs[2 * g + i] for i in range(2)]) for g in range(2)]
     gm = first[...] + times(others, groups)
-    out[...] = (A3 * both[core].astype(F32) + A5 * gm).astype(BF16)
+    out[...] = (base[...] + A5 * gm).astype(BF16)
 
 
 def product_body(w, tiles, others, out):
@@ -104,7 +113,6 @@
 
 
 def local(momentum):
-    width = 7168
     packed = jax.ShapeDtypeStruct((8, 48, 224), BF16)
     kept = jax.ShapeDtypeStruct(momentum.shape, BF16)
     sent, kept = kernel_calls(pack_body, [momentum], [packed, kept], 10**6)
@@ -113,7 +121,10 @@
     shard = kernel_call(shard_body, [both], (2, 4, 48, 224), BF16, 10**6)
     m = lax.all_gather(shard, "x", axis=0)
     part = kernel_call(gram_body, [both, m], (8, 2, 48, 384), BF16, 2 * flops)
+    part, early = lax.optimization_barrier((part, both))
+    base = kernel_call(base_body, [early], (8, 48, 224), F32, 10**6)
     parts = exchange(part.reshape(16, 48, 384), HY)
+    parts, base = lax.optimization_barrier((parts, base))
     tile = jnp.sum(parts.astype(F32), axis=0).astype(BF16)
     tile, later = lax.optimization_barrier((tile, m))
     gathered = exchange(jnp.broadcast_to(tile[None], (16, 48, 384)), HY)
@@ -124,14 +135,17 @@
     others = swap(gathered)
     first = kernel_call(first_body, [m, gathered], (8, 48, 224), F32, flops)
     weighted = kernel_call(
-        weight_body, [both, got, others, first], (8, 48, 224), BF16, flops
+        weight_body, [base, got, others, first], (8, 48, 224), BF16, flops
     )
     w = lax.all_gather(weighted, "x", axis=0)
     rows = kernel_call(product_body, [w, gathered, others], (8, 48, 224), BF16, 2 * flops)
-    back = exchange(rows, Z).reshape(4, 2, 48, 224).astype(F32)
+    rows, kept = lax.optimization_barrier((rows, kept))
+    scaled = kernel_call(kept_body, [kept], momentum.shape, F32, 10**6)
+    back = exchange(rows, Z)
+    back, scaled = lax.optimization_barrier((back, scaled))
+    back = back.reshape(4, 2, 48, 224).astype(F32)
     product = jnp.concatenate([back[:, 0], back[:, 1]], axis=2)
-    result = 0.2 * math.sqrt(width) * (A1 * kept.astype(F32) + product)
-    return result.astype(BF16)
+    return (scaled + SCALE * product).astype(BF16)
 
 
 def solution(mesh):

time: 115 us -> 117 us (1.017)
  blocking collectives: 89.6 us -> 53.2 us
  waiting for transfers between devices: 13.9 us -> 38.7 us
  starting transfers between devices: 6.33 us -> 18 us
  Pallas kernels: 2 us -> 3.56 us
    all_to_all x3 -> x1, blocking collectives: 56.7 us -> 20.6 us  [exchange(): return lax.all_to_all(array, axes, 0, 0, tiled=True)]
    all_to_all x1 -> x3, waiting for transfers between devices: 12.3 us -> 37.1 us  [exchange(): return lax.all_to_all(array, axes, 0, 0, tiled=True)]
    all_to_all x1 -> x3, starting transfers between devices: 4.42 us -> 16.1 us  [exchange(): return lax.all_to_all(array, axes, 0, 0, tiled=True)]
    pallas_call x7 -> x9, Pallas kernels: 2 us -> 3.56 us  [kernel_calls(): pl.pallas_call(body, out_shape=outputs, in_specs=[VMEM] * len(inputs), ou...]
  transfers between devices with their start and end apart: 2 -> 4, of which waited for: 2 -> 4; matrix products, arithmetic and copies ran while one was open for 0% -> 0% of each run, Pallas kernels for 0% -> 0%
where the time goes in v10:
time: 117 us; the launch traced here: 116 us
  blocking collectives  53.2 us (45%)
  waiting for transfers between devices  38.7 us (33%)
  starting transfers between devices  18 us (15%)
  Pallas kernels  3.56 us (3%)
  local copies, waits for them, and re-layouts  1.81 us (2%)
    all_to_all x3, waiting for transfers between devices, exchange(): return lax.all_to_all(array, axes, 0, 0, tiled=True)  37.1 us
    all_to_all x1, blocking collectives, exchange(): return lax.all_to_all(array, axes, 0, 0, tiled=True)  20.6 us
    all_to_all x3, starting transfers between devices, exchange(): return lax.all_to_all(array, axes, 0, 0, tiled=True)  16.1 us
    all_gather x1, blocking collectives, local(): w = lax.all_gather(weighted, 'x', axis=0)  14.3 us
    all_gather x1, blocking collectives, local(): m = lax.all_gather(shard, 'x', axis=0)  13.9 us
    pallas_call x9, Pallas kernels, kernel_calls(): pl.pallas_call(body, out_shape=outputs, in_specs=[VMEM] * len(inputs), ou...  3.56 us
    all_gather x1, blocking collectives, local(): got = lax.all_gather(send, 'core', axis=0)  2.37 us
  transfers between devices with their start and end apart: 4, of which 4 were waited for; matrix products, arithmetic and copies ran while one was open for 0% of the time, Pallas kernels for 0%

profile of v10, /device:TPU:8, one launch (start us, length us, event | category | flops | bytes accessed | tf_op | source)
XLA Modules:
  0.0 116.4 jit_solution(10599578694067329948)
XLA Ops:
  0.0 0.0 copy-start
  0.0 0.9 copy-done
  0.9 0.1 shard_map.17
  1.0 20.6 %all_to_all.20 = bf16[8,48,224]{2,1,0:T(8,128)(2,1)S(1)} all-to-all(bf16[8,48,224]{2,1,0:T(8,128)(2,1)S(1)} %get-tuple-element.19), channel_id=1, replica_groups=mesh['zl'=4,'zh'=2,'x'=4,'y'=8,'core'=2] {'zl','zh'}, dimensions={0} | all-to-all | bytes 344064 | tf_op jit(solution)/shard_map/all_to_all | solution.py:39
  21.6 2.1 %all-gather = bf16[16,48,224]{2,1,0:T(8,128)(2,1)S(1)} all-gather(bf16[8,48,224]{2,1,0:T(8,128)(2,1)S(1)} %all_to_all.20), channel_id=2, replica_groups=mesh['zl'=4,'zh'=2,'x'=4,'y'=8,'core'=2] {'core'}, dimensions={0}, use_global_device_ids=true | all-gather | bytes 516096 | tf_op jit(solution)/shard_map/all_gather | solution.py:120
  23.7 13.9 %all-gather.1 = bf16[8,4,48,224]{3,2,1,0:T(8,128)(2,1)S(1)} all-gather(bf16[2,4,48,224]{3,2,1,0:T(8,128)(2,1)S(1)} %shard_map.18), channel_id=3, replica_groups=mesh['zl'=4,'zh'=2,'x'=4,'y'=8,'core'=2] {'x'}, dimensions={0}, use_global_device_ids=true | all-gather | bytes 860160 | tf_op jit(solution)/shard_map/all_gather | solution.py:122
  37.6 1.4 %shard_map.19 = bf16[8,2,48,384]{3,2,1,0:T(8,128)(2,1)} custom-call(bf16[2,8,48,224]{3,2,1,0:T(8,128)(2,1)S(1)} %bitcast.19, bf16[4,2,4,48,224]{4,3,2,1,0:T(8,128)(2,1)S(1)} %bitcast.15), custom_call_target="tpu_custom_call" | custom-call | flops 264241152 | tf_op jit(solution)/shard_map/pallas_call | solution.py:24
  39.0 7.6 %all-to-all-start.1 = ((bf16[16,48,384]{2,1,0:T(8,128)(2,1)}), bf16[16,48,384]{2,1,0:T(8,128)(2,1)S(1)}, u32[]{:S(2)}, u32[]{:S(2)}) async-start(bf16[16,48,384]{2,1,0:T(8,128)(2,1)} %bitcast.2), calls=%async_computation.1 | async-start | bytes 1179648 | tf_op jit(solution)/shard_map/all_to_all | solution.py:39
  46.6 14.9 %all-to-all-done.1 = bf16[16,48,384]{2,1,0:T(8,128)(2,1)S(1)} async-done(((bf16[16,48,384]{2,1,0:T(8,128)(2,1)}), bf16[16,48,384]{2,1,0:T(8,128)(2,1)S(1)}, u32[]{:S(2)}, u32[]{:S(2)}) %all-to-all-start.1) | async-done | bytes 589856 | tf_op jit(solution)/shard_map/all_to_all | solution.py:39
  61.5 0.1 reduce_sum.12
  61.6 0.9 broadcast_in_dim.2
  62.4 5.2 %all-to-all-start.2 = ((bf16[16,48,384]{2,1,0:T(8,128)(2,1)}), bf16[16,48,384]{2,1,0:T(8,128)(2,1)S(1)}, u32[]{:S(2)}, u32[]{:S(2)}) async-start(bf16[16,48,384]{2,1,0:T(8,128)(2,1)} %broadcast_in_dim.2), calls=%async_computation.2 | async-start | bytes 1179648 | tf_op jit(solution)/shard_map/all_to_all | solution.py:39
  67.6 2.4 %all-gather.2 = bf16[8,4,48,224]{3,2,1,0:T(8,128)(2,1)S(1)} all-gather(bf16[4,4,48,224]{3,2,1,0:T(8,128)(2,1)S(1)} %shard_map.21), channel_id=4, replica_groups=mesh['zl'=4,'zh'=2,'x'=4,'y'=8,'core'=2] {'core'}, dimensions={0}, use_global_device_ids=true | all-gather | bytes 1032192 | tf_op jit(solution)/shard_map/all_gather | solution.py:132
  70.0 12.6 %all-to-all-done.2.tiles = bf16[16,48,384]{2,1,0:T(8,128)(2,1)S(1)} async-done(((bf16[16,48,384]{2,1,0:T(8,128)(2,1)}), bf16[16,48,384]{2,1,0:T(8,128)(2,1)S(1)}, u32[]{:S(2)}, u32[]{:S(2)}) %all-to-all-start.2) | async-done | bytes 589856 | tf_op jit(solution)/shard_map/all_to_all | solution.py:39
  82.6 1.9 %collective-permute-start = (bf16[16,48,384]{2,1,0:T(8,128)(2,1)S(1)}, bf16[16,48,384]{2,1,0:T(8,128)(2,1)S(1)}, u32[]{:S(2)}, u32[]{:S(2)}) collective-permute-start(bf16[16,48,384]{2,1,0:T(8,128)(2,1)S(1)} %all-to-all-done.2.tiles), channel_id=1, source_target_pairs={{0,1},{1,0},{2,3},{3,2},{4,5},{5,4},{6,7},{7,6},{8,9},{9,8},{10,11... | collective-permute-start | bytes 1769480 | tf_op jit(solution)/shard_map/ppermute | solution.py:35
  84.5 0.4 shard_map.22.first
  84.9 1.6 %collective-permute-done.others = bf16[16,48,384]{2,1,0:T(8,128)(2,1)S(1)} collective-permute-done((bf16[16,48,384]{2,1,0:T(8,128)(2,1)S(1)}, bf16[16,48,384]{2,1,0:T(8,128)(2,1)S(1)}, u32[]{:S(2)}, u32[]{:S(2)}) %collective-permute-start) | collective-permute-done | bytes 589856 | tf_op jit(solution)/shard_map/ppermute | solution.py:35
  86.5 0.4 shard_map.23
  86.9 14.3 %all-gather.3 = bf16[32,48,224]{2,1,0:T(8,128)(2,1)S(1)} all-gather(bf16[8,48,224]{2,1,0:T(8,128)(2,1)S(1)} %shard_map.23), channel_id=5, replica_groups=mesh['zl'=4,'zh'=2,'x'=4,'y'=8,'core'=2] {'x'}, dimensions={0}, use_global_device_ids=true | all-gather | bytes 860160 | tf_op jit(solution)/shard_map/all_gather | solution.py:140
  101.2 1.2 %shard_map.24 = bf16[8,48,224]{2,1,0:T(8,128)(2,1)} custom-call(bf16[4,8,48,224]{3,2,1,0:T(8,128)(2,1)S(1)} %bitcast.22, bf16[16,48,384]{2,1,0:T(8,128)(2,1)S(1)} %all-to-all-done.2.tiles, bf16[16,48,384]{2,1,0:T(8,128)(2,1)S(1)} %collective-permute-done.others), custom_call_target="tpu_custom_call" | custom-call | flops 264241152 | tf_op jit(solution)/shard_map/pallas_call | solution.py:24
  102.4 3.4 %all-to-all-start.3 = ((bf16[8,48,224]{2,1,0:T(8,128)(2,1)}), bf16[8,48,224]{2,1,0:T(8,128)(2,1)S(1)}, u32[]{:S(2)}, u32[]{:S(2)}) async-start(bf16[8,48,224]{2,1,0:T(8,128)(2,1)} %shard_map.24), calls=%async_computation.3 | async-start | bytes 393216 | tf_op jit(solution)/shard_map/all_to_all | solution.py:39
  105.8 9.6 %all-to-all-done.3 = bf16[8,48,224]{2,1,0:T(8,128)(2,1)S(1)} async-done(((bf16[8,48,224]{2,1,0:T(8,128)(2,1)}), bf16[8,48,224]{2,1,0:T(8,128)(2,1)S(1)}, u32[]{:S(2)}, u32[]{:S(2)}) %all-to-all-start.3) | async-done | bytes 172064 | tf_op jit(solution)/shard_map/all_to_all | solution.py:39
  115.6 0.8 fusion.1
  (6 shorter events, 0.2 us)
Async XLA Ops:
  0.0 0.9 copy-start
  39.0 22.5 %all-to-all-start.1 = ((bf16[16,48,384]{2,1,0:T(8,128)(2,1)}), bf16[16,48,384]{2,1,0:T(8,128)(2,1)S(1)}, u32[]{:S(2)}, u32[]{:S(2)}) async-start(bf16[16,48,384]{2,1,0:T(8,128)(2,1)} %bitcast.2), calls=%async_computation.1 | async-start | bytes 1179648 | tf_op jit(solution)/shard_map/all_to_all | solution.py:39
  62.4 20.2 %all-to-all-start.2 = ((bf16[16,48,384]{2,1,0:T(8,128)(2,1)}), bf16[16,48,384]{2,1,0:T(8,128)(2,1)S(1)}, u32[]{:S(2)}, u32[]{:S(2)}) async-start(bf16[16,48,384]{2,1,0:T(8,128)(2,1)} %broadcast_in_dim.2), calls=%async_computation.2 | async-start | bytes 1179648 | tf_op jit(solution)/shard_map/all_to_all | solution.py:39
  82.6 3.9 %collective-permute-start = (bf16[16,48,384]{2,1,0:T(8,128)(2,1)S(1)}, bf16[16,48,384]{2,1,0:T(8,128)(2,1)S(1)}, u32[]{:S(2)}, u32[]{:S(2)}) collective-permute-start(bf16[16,48,384]{2,1,0:T(8,128)(2,1)S(1)} %all-to-all-done.2.tiles), channel_id=1, source_target_pairs={{0,1},{1,0},{2,3},{3,2},{4,5},{5,4},{6,7},{7,6},{8,9},{9,8},{10,11... | collective-permute-start | bytes 1769480 | tf_op jit(solution)/shard_map/ppermute | solution.py:35
  102.4 13.1 %all-to-all-start.3 = ((bf16[8,48,224]{2,1,0:T(8,128)(2,1)}), bf16[8,48,224]{2,1,0:T(8,128)(2,1)S(1)}, u32[]{:S(2)}, u32[]{:S(2)}) async-start(bf16[8,48,224]{2,1,0:T(8,128)(2,1)} %shard_map.24), calls=%async_computation.3 | async-start | bytes 393216 | tf_op jit(solution)/shard_map/all_to_all | solution.py:39

commit v11 on v8

--- a/solution.py
+++ b/solution.py
@@ -10,7 +10,7 @@
 F32 = jnp.float32
 BF16 = jnp.bfloat16
 A1, A3, A5 = 3.4445, -4.775, 2.0315
-Z = ("zl", "zh")
+Z = ("zh", "zl")
 HY = ("zh", "y")
 VMEM = pl.BlockSpec(memory_space=pltpu.VMEM)
 
@@ -44,8 +44,8 @@
 
 def pack_body(momentum, sent, kept):
     for layer in range(4):
-        sent[layer * 2] = momentum[layer, :, :224]
-        sent[layer * 2 + 1] = momentum[layer, :, 224:]
+        sent[layer] = momentum[layer, :, :224]
+        sent[4 + layer] = momentum[layer, :, 224:]
     kept[...] = momentum[...]
 
 
@@ -128,8 +128,8 @@
     )
     w = lax.all_gather(weighted, "x", axis=0)
     rows = kernel_call(product_body, [w, gathered, others], (8, 48, 224), BF16, 2 * flops)
-    back = exchange(rows, Z).reshape(4, 2, 48, 224).astype(F32)
-    product = jnp.concatenate([back[:, 0], back[:, 1]], axis=2)
+    back = exchange(rows, Z).reshape(2, 4, 48, 224).astype(F32)
+    product = jnp.concatenate([back[0], back[1]], axis=2)
     result = 0.2 * math.sqrt(width) * (A1 * kept.astype(F32) + product)
     return result.astype(BF16)
 

time: 115 us -> 114 us (level)
  blocking collectives: 89.6 us -> 88.2 us
    all_to_all x3, blocking collectives: 56.7 us -> 55.3 us  [exchange(): return lax.all_to_all(array, axes, 0, 0, tiled=True)]
where the time goes in v11:
time: 114 us; the launch traced here: 113 us
  blocking collectives  88.2 us (77%)
  waiting for transfers between devices  13.9 us (12%)
  starting transfers between devices  6.33 us (6%)
  Pallas kernels  2 us (2%)
  local copies, waits for them, and re-layouts  1.82 us (2%)
    all_to_all x3, blocking collectives, exchange(): return lax.all_to_all(array, axes, 0, 0, tiled=True)  55.3 us
    all_gather x1, blocking collectives, local(): w = lax.all_gather(weighted, 'x', axis=0)  14.5 us
    all_gather x1, blocking collectives, local(): m = lax.all_gather(shard, 'x', axis=0)  13.9 us
    all_to_all x1, waiting for transfers between devices, exchange(): return lax.all_to_all(array, axes, 0, 0, tiled=True)  12.3 us
    all_to_all x1, starting transfers between devices, exchange(): return lax.all_to_all(array, axes, 0, 0, tiled=True)  4.42 us
    all_gather x1, blocking collectives, local(): got = lax.all_gather(send, 'core', axis=0)  2.37 us
  transfers between devices with their start and end apart: 2, of which 2 were waited for; matrix products, arithmetic and copies ran while one was open for 0% of the time, Pallas kernels for 0%

profile of v11, /device:TPU:8, one launch (start us, length us, event | category | flops | bytes accessed | tf_op | source)
XLA Modules:
  0.0 113.2 jit_solution(12400786025063433435)
XLA Ops:
  0.0 0.0 copy-start
  0.0 0.9 copy-done
  0.9 0.1 shard_map.17
  1.0 19.0 %all_to_all.20 = bf16[8,48,224]{2,1,0:T(8,128)(2,1)S(1)} all-to-all(bf16[8,48,224]{2,1,0:T(8,128)(2,1)S(1)} %get-tuple-element.12), channel_id=1, replica_groups=mesh['zl'=4,'zh'=2,'x'=4,'y'=8,'core'=2] {'zh','zl'}, dimensions={0} | all-to-all | bytes 344064 | tf_op jit(solution)/shard_map/all_to_all | solution.py:38
  20.1 2.1 %all-gather = bf16[16,48,224]{2,1,0:T(8,128)(2,1)S(1)} all-gather(bf16[8,48,224]{2,1,0:T(8,128)(2,1)S(1)} %all_to_all.20), channel_id=2, replica_groups=mesh['zl'=4,'zh'=2,'x'=4,'y'=8,'core'=2] {'core'}, dimensions={0}, use_global_device_ids=true | all-gather | bytes 516096 | tf_op jit(solution)/shard_map/all_gather | solution.py:112
  22.2 13.9 %all-gather.1 = bf16[8,4,48,224]{3,2,1,0:T(8,128)(2,1)S(1)} all-gather(bf16[2,4,48,224]{3,2,1,0:T(8,128)(2,1)S(1)} %shard_map.18), channel_id=3, replica_groups=mesh['zl'=4,'zh'=2,'x'=4,'y'=8,'core'=2] {'x'}, dimensions={0}, use_global_device_ids=true | all-gather | bytes 860160 | tf_op jit(solution)/shard_map/all_gather | solution.py:114
  36.1 0.6 shard_map.19
  36.6 25.4 %all_to_all.21 = bf16[16,48,384]{2,1,0:T(8,128)(2,1)S(1)} all-to-all(bf16[16,48,384]{2,1,0:T(8,128)(2,1)S(1)} %bitcast.13), channel_id=1, replica_groups=mesh['zl'=4,'zh'=2,'x'=4,'y'=8,'core'=2] {'zh','y'}, dimensions={0} | all-to-all | bytes 1179648 | tf_op jit(solution)/shard_map/all_to_all | solution.py:38
  62.0 0.1 reduce_sum.12
  62.1 0.9 broadcast_in_dim.2
  63.0 4.4 %all-to-all-start.2 = ((bf16[16,48,384]{2,1,0:T(8,128)(2,1)}), bf16[16,48,384]{2,1,0:T(8,128)(2,1)S(1)}, u32[]{:S(2)}, u32[]{:S(2)}) async-start(bf16[16,48,384]{2,1,0:T(8,128)(2,1)} %broadcast_in_dim.2), calls=%async_computation.2 | async-start | bytes 1179648 | tf_op jit(solution)/shard_map/all_to_all | solution.py:38
  67.5 2.4 %all-gather.2 = bf16[8,4,48,224]{3,2,1,0:T(8,128)(2,1)S(1)} all-gather(bf16[4,4,48,224]{3,2,1,0:T(8,128)(2,1)S(1)} %shard_map.20), channel_id=4, replica_groups=mesh['zl'=4,'zh'=2,'x'=4,'y'=8,'core'=2] {'core'}, dimensions={0}, use_global_device_ids=true | all-gather | bytes 1032192 | tf_op jit(solution)/shard_map/all_gather | solution.py:121
  69.8 12.3 %all-to-all-done.2.tiles = bf16[16,48,384]{2,1,0:T(8,128)(2,1)S(1)} async-done(((bf16[16,48,384]{2,1,0:T(8,128)(2,1)}), bf16[16,48,384]{2,1,0:T(8,128)(2,1)S(1)}, u32[]{:S(2)}, u32[]{:S(2)}) %all-to-all-start.2) | async-done | bytes 589856 | tf_op jit(solution)/shard_map/all_to_all | solution.py:38
  82.2 1.9 %collective-permute-start = (bf16[16,48,384]{2,1,0:T(8,128)(2,1)S(1)}, bf16[16,48,384]{2,1,0:T(8,128)(2,1)S(1)}, u32[]{:S(2)}, u32[]{:S(2)}) collective-permute-start(bf16[16,48,384]{2,1,0:T(8,128)(2,1)S(1)} %all-to-all-done.2.tiles), channel_id=1, source_target_pairs={{0,1},{1,0},{2,3},{3,2},{4,5},{5,4},{6,7},{7,6},{8,9},{9,8},{10,11... | collective-permute-start | bytes 1769480 | tf_op jit(solution)/shard_map/ppermute | solution.py:34
  84.1 0.4 shard_map.21.first
  84.4 1.6 %collective-permute-done.others = bf16[16,48,384]{2,1,0:T(8,128)(2,1)S(1)} collective-permute-done((bf16[16,48,384]{2,1,0:T(8,128)(2,1)S(1)}, bf16[16,48,384]{2,1,0:T(8,128)(2,1)S(1)}, u32[]{:S(2)}, u32[]{:S(2)}) %collective-permute-start) | collective-permute-done | bytes 589856 | tf_op jit(solution)/shard_map/ppermute | solution.py:34
  86.1 0.4 shard_map.22
  86.4 14.5 %all-gather.3 = bf16[32,48,224]{2,1,0:T(8,128)(2,1)S(1)} all-gather(bf16[8,48,224]{2,1,0:T(8,128)(2,1)S(1)} %shard_map.22), channel_id=5, replica_groups=mesh['zl'=4,'zh'=2,'x'=4,'y'=8,'core'=2] {'x'}, dimensions={0}, use_global_device_ids=true | all-gather | bytes 860160 | tf_op jit(solution)/shard_map/all_gather | solution.py:129
  100.9 0.6 shard_map.23
  101.5 10.9 %all_to_all.22 = bf16[8,48,224]{2,1,0:T(8,128)(2,1)S(1)} all-to-all(bf16[8,48,224]{2,1,0:T(8,128)(2,1)S(1)} %shard_map.23), channel_id=1, replica_groups=mesh['zl'=4,'zh'=2,'x'=4,'y'=8,'core'=2] {'zh','zl'}, dimensions={0} | all-to-all | bytes 344064 | tf_op jit(solution)/shard_map/all_to_all | solution.py:38
  112.4 0.8 fusion.1
  (3 shorter events, 0.1 us)
Async XLA Ops:
  0.0 0.9 copy-start
  63.0 19.2 %all-to-all-start.2 = ((bf16[16,48,384]{2,1,0:T(8,128)(2,1)}), bf16[16,48,384]{2,1,0:T(8,128)(2,1)S(1)}, u32[]{:S(2)}, u32[]{:S(2)}) async-start(bf16[16,48,384]{2,1,0:T(8,128)(2,1)} %broadcast_in_dim.2), calls=%async_computation.2 | async-start | bytes 1179648 | tf_op jit(solution)/shard_map/all_to_all | solution.py:38
  82.2 3.9 %collective-permute-start = (bf16[16,48,384]{2,1,0:T(8,128)(2,1)S(1)}, bf16[16,48,384]{2,1,0:T(8,128)(2,1)S(1)}, u32[]{:S(2)}, u32[]{:S(2)}) collective-permute-start(bf16[16,48,384]{2,1,0:T(8,128)(2,1)S(1)} %all-to-all-done.2.tiles), channel_id=1, source_target_pairs={{0,1},{1,0},{2,3},{3,2},{4,5},{5,4},{6,7},{7,6},{8,9},{9,8},{10,11... | collective-permute-start | bytes 1769480 | tf_op jit(solution)/shard_map/ppermute | solution.py:34

commit v12 on v11

--- a/solution.py
+++ b/solution.py
@@ -10,8 +10,10 @@
 F32 = jnp.float32
 BF16 = jnp.bfloat16
 A1, A3, A5 = 3.4445, -4.775, 2.0315
-Z = ("zh", "zl")
-HY = ("zh", "y")
+Z = ("z0", "z1", "z2")
+HY = ("y1", "y0", "y2", "z0")
+X = ("x1", "x0")
+AXES = ("z2", "z1", "z0", "x1", "x0", "y2", "y1", "y0", "core")
 VMEM = pl.BlockSpec(memory_space=pltpu.VMEM)
 
 
@@ -42,10 +44,15 @@
     return jnp.concatenate([block.reshape(192, 224) for block in blocks], axis=0)
 
 
+def places():
+    for member in range(8):
+        bit = {name: member >> (2 - at) & 1 for at, name in enumerate(Z)}
+        yield member, bit["z2"] * 2 + bit["z1"], bit["z0"]
+
+
 def pack_body(momentum, sent, kept):
-    for layer in range(4):
-        sent[layer] = momentum[layer, :, :224]
-        sent[4 + layer] = momentum[layer, :, 224:]
+    for member, layer, h in places():
+        sent[member] = momentum[layer, :, h * 224 : h * 224 + 224]
     kept[...] = momentum[...]
 
 
@@ -111,7 +118,7 @@
     flops = 2 * 384 * 768 * 224
     both = lax.all_gather(exchange(sent, Z), "core", axis=0)
     shard = kernel_call(shard_body, [both], (2, 4, 48, 224), BF16, 10**6)
-    m = lax.all_gather(shard, "x", axis=0)
+    m = lax.all_gather(shard, X, axis=0)
     part = kernel_call(gram_body, [both, m], (8, 2, 48, 384), BF16, 2 * flops)
     parts = exchange(part.reshape(16, 48, 384), HY)
     tile = jnp.sum(parts.astype(F32), axis=0).astype(BF16)
@@ -126,15 +133,17 @@
     weighted = kernel_call(
         weight_body, [both, got, others, first], (8, 48, 224), BF16, flops
     )
-    w = lax.all_gather(weighted, "x", axis=0)
+    w = lax.all_gather(weighted, X, axis=0)
     rows = kernel_call(product_body, [w, gathered, others], (8, 48, 224), BF16, 2 * flops)
-    back = exchange(rows, Z).reshape(2, 4, 48, 224).astype(F32)
-    product = jnp.concatenate([back[0], back[1]], axis=2)
+    back = exchange(rows, Z).astype(F32)
+    at = {(layer, h): member for member, layer, h in places()}
+    halves = [[back[at[layer, h]] for layer in range(4)] for h in range(2)]
+    product = jnp.concatenate([jnp.stack(half) for half in halves], axis=2)
     result = 0.2 * math.sqrt(width) * (A1 * kept.astype(F32) + product)
     return result.astype(BF16)
 
 
 def solution(mesh):
-    split = Mesh(mesh.devices.reshape(4, 2, 4, 8, 2), ("zl", "zh", "x", "y", "core"))
-    placed = P(None, ("zl", "zh", "x"), ("y", "core"))
+    split = Mesh(mesh.devices.reshape((2,) * 9), AXES)
+    placed = P(None, AXES[:5], AXES[5:])
     return jax.shard_map(local, mesh=split, in_specs=(placed,), out_specs=placed, check_vma=False)

time: 114 us -> 113 us (level)
  the two profiles are of different devices: /device:TPU:8 before, /device:TPU:64 now
where the time goes in v12:
time: 113 us
  blocking collectives  87.8 us (78%)
  waiting for transfers between devices  13.6 us (12%)
  starting transfers between devices  6.74 us (6%)
  Pallas kernels  2.01 us (2%)
  local copies, waits for them, and re-layouts  1.82 us (2%)
    all_to_all x3, blocking collectives, exchange(): return lax.all_to_all(array, axes, 0, 0, tiled=True)  55 us
    all_gather x1, blocking collectives, local(): w = lax.all_gather(weighted, X, axis=0)  14.4 us
    all_gather x1, blocking collectives, local(): m = lax.all_gather(shard, X, axis=0)  13.9 us
    all_to_all x1, waiting for transfers between devices, exchange(): return lax.all_to_all(array, axes, 0, 0, tiled=True)  12 us
    all_to_all x1, starting transfers between devices, exchange(): return lax.all_to_all(array, axes, 0, 0, tiled=True)  4.83 us
    all_gather x1, blocking collectives, local(): got = lax.all_gather(send, 'core', axis=0)  2.37 us
  transfers between devices with their start and end apart: 2, of which 2 were waited for; matrix products, arithmetic and copies ran while one was open for 0% of the time, Pallas kernels for 0%

profile of v12, /device:TPU:64, one launch (start us, length us, event | category | flops | bytes accessed | tf_op | source)
XLA Modules:
  0.0 112.9 jit_solution(16912127889521466207)
XLA Ops:
  0.0 0.0 copy-start
  0.0 0.9 copy-done
  0.9 0.1 shard_map.17
  1.0 17.7 %all_to_all.20 = bf16[8,48,224]{2,1,0:T(8,128)(2,1)S(1)} all-to-all(bf16[8,48,224]{2,1,0:T(8,128)(2,1)S(1)} %get-tuple-element.12), channel_id=1, replica_groups=mesh['z2'=2,'z1'=2,'z0'=2,'x1'=2,'x0'=2,'y2'=2,'y1'=2,'y0'=2,'core'=2] {..., dimensions={0} | all-to-all | bytes 344064 | tf_op jit(solution)/shard_map/all_to_all | solution.py:40
  18.8 2.1 %all-gather = bf16[16,48,224]{2,1,0:T(8,128)(2,1)S(1)} all-gather(bf16[8,48,224]{2,1,0:T(8,128)(2,1)S(1)} %all_to_all.20), channel_id=2, replica_groups=mesh['z2'=2,'z1'=2,'z0'=2,'x1'=2,'x0'=2,'y2'=2,'y1'=2,'y0'=2,'core'=2] {..., dimensions={0}, use_global_device_ids=true | all-gather | bytes 516096 | tf_op jit(solution)/shard_map/all_gather | solution.py:119
  20.9 13.9 %all-gather.1 = bf16[8,4,48,224]{3,2,1,0:T(8,128)(2,1)S(1)} all-gather(bf16[2,4,48,224]{3,2,1,0:T(8,128)(2,1)S(1)} %shard_map.18), channel_id=3, replica_groups=mesh['z2'=2,'z1'=2,'z0'=2,'x1'=2,'x0'=2,'y2'=2,'y1'=2,'y0'=2,'core'=2] {..., dimensions={0}, use_global_device_ids=true | all-gather | bytes 860160 | tf_op jit(solution)/shard_map/all_gather | solution.py:121
  34.8 0.6 shard_map.19
  35.4 25.0 %all_to_all.21 = bf16[16,48,384]{2,1,0:T(8,128)(2,1)S(1)} all-to-all(bf16[16,48,384]{2,1,0:T(8,128)(2,1)S(1)} %bitcast.13), channel_id=1, replica_groups=mesh['z2'=2,'z1'=2,'z0'=2,'x1'=2,'x0'=2,'y2'=2,'y1'=2,'y0'=2,'core'=2] {..., dimensions={0} | all-to-all | bytes 1179648 | tf_op jit(solution)/shard_map/all_to_all | solution.py:40
  60.4 0.1 reduce_sum.12
  60.5 0.9 broadcast_in_dim.2
  61.3 4.8 %all-to-all-start.2 = ((bf16[16,48,384]{2,1,0:T(8,128)(2,1)}), bf16[16,48,384]{2,1,0:T(8,128)(2,1)S(1)}, u32[]{:S(2)}, u32[]{:S(2)}) async-start(bf16[16,48,384]{2,1,0:T(8,128)(2,1)} %broadcast_in_dim.2), calls=%async_computation.2 | async-start | bytes 1179648 | tf_op jit(solution)/shard_map/all_to_all | solution.py:40
  66.2 2.4 %all-gather.2 = bf16[8,4,48,224]{3,2,1,0:T(8,128)(2,1)S(1)} all-gather(bf16[4,4,48,224]{3,2,1,0:T(8,128)(2,1)S(1)} %shard_map.20), channel_id=4, replica_groups=mesh['z2'=2,'z1'=2,'z0'=2,'x1'=2,'x0'=2,'y2'=2,'y1'=2,'y0'=2,'core'=2] {..., dimensions={0}, use_global_device_ids=true | all-gather | bytes 1032192 | tf_op jit(solution)/shard_map/all_gather | solution.py:128
  68.6 12.0 %all-to-all-done.2.tiles = bf16[16,48,384]{2,1,0:T(8,128)(2,1)S(1)} async-done(((bf16[16,48,384]{2,1,0:T(8,128)(2,1)}), bf16[16,48,384]{2,1,0:T(8,128)(2,1)S(1)}, u32[]{:S(2)}, u32[]{:S(2)}) %all-to-all-start.2) | async-done | bytes 589856 | tf_op jit(solution)/shard_map/all_to_all | solution.py:40
  80.5 1.9 %collective-permute-start = (bf16[16,48,384]{2,1,0:T(8,128)(2,1)S(1)}, bf16[16,48,384]{2,1,0:T(8,128)(2,1)S(1)}, u32[]{:S(2)}, u32[]{:S(2)}) collective-permute-start(bf16[16,48,384]{2,1,0:T(8,128)(2,1)S(1)} %all-to-all-done.2.tiles), channel_id=1, source_target_pairs={{0,1},{1,0},{2,3},{3,2},{4,5},{5,4},{6,7},{7,6},{8,9},{9,8},{10,11... | collective-permute-start | bytes 1769480 | tf_op jit(solution)/shard_map/ppermute | solution.py:36
  82.5 0.4 shard_map.21.first
  82.8 1.6 %collective-permute-done.others = bf16[16,48,384]{2,1,0:T(8,128)(2,1)S(1)} collective-permute-done((bf16[16,48,384]{2,1,0:T(8,128)(2,1)S(1)}, bf16[16,48,384]{2,1,0:T(8,128)(2,1)S(1)}, u32[]{:S(2)}, u32[]{:S(2)}) %collective-permute-start) | collective-permute-done | bytes 589856 | tf_op jit(solution)/shard_map/ppermute | solution.py:36
  84.4 0.4 shard_map.22
  84.8 14.4 %all-gather.3 = bf16[32,48,224]{2,1,0:T(8,128)(2,1)S(1)} all-gather(bf16[8,48,224]{2,1,0:T(8,128)(2,1)S(1)} %shard_map.22), channel_id=5, replica_groups=mesh['z2'=2,'z1'=2,'z0'=2,'x1'=2,'x0'=2,'y2'=2,'y1'=2,'y0'=2,'core'=2] {..., dimensions={0}, use_global_device_ids=true | all-gather | bytes 860160 | tf_op jit(solution)/shard_map/all_gather | solution.py:136
  99.2 0.6 shard_map.23
  99.8 12.2 %all_to_all.22 = bf16[8,48,224]{2,1,0:T(8,128)(2,1)S(1)} all-to-all(bf16[8,48,224]{2,1,0:T(8,128)(2,1)S(1)} %shard_map.23), channel_id=1, replica_groups=mesh['z2'=2,'z1'=2,'z0'=2,'x1'=2,'x0'=2,'y2'=2,'y1'=2,'y0'=2,'core'=2] {..., dimensions={0} | all-to-all | bytes 344064 | tf_op jit(solution)/shard_map/all_to_all | solution.py:40
  112.1 0.8 fusion.1
  (3 shorter events, 0.1 us)
Async XLA Ops:
  0.0 0.9 copy-start
  61.3 19.2 %all-to-all-start.2 = ((bf16[16,48,384]{2,1,0:T(8,128)(2,1)}), bf16[16,48,384]{2,1,0:T(8,128)(2,1)S(1)}, u32[]{:S(2)}, u32[]{:S(2)}) async-start(bf16[16,48,384]{2,1,0:T(8,128)(2,1)} %broadcast_in_dim.2), calls=%async_computation.2 | async-start | bytes 1179648 | tf_op jit(solution)/shard_map/all_to_all | solution.py:40
  80.5 3.9 %collective-permute-start = (bf16[16,48,384]{2,1,0:T(8,128)(2,1)S(1)}, bf16[16,48,384]{2,1,0:T(8,128)(2,1)S(1)}, u32[]{:S(2)}, u32[]{:S(2)}) collective-permute-start(bf16[16,48,384]{2,1,0:T(8,128)(2,1)S(1)} %all-to-all-done.2.tiles), channel_id=1, source_target_pairs={{0,1},{1,0},{2,3},{3,2},{4,5},{5,4},{6,7},{7,6},{8,9},{9,8},{10,11... | collective-permute-start | bytes 1769480 | tf_op jit(solution)/shard_map/ppermute | solution.py:36

commit v13 on v12

--- a/solution.py
+++ b/solution.py
@@ -11,7 +11,7 @@
 BF16 = jnp.bfloat16
 A1, A3, A5 = 3.4445, -4.775, 2.0315
 Z = ("z0", "z1", "z2")
-HY = ("y1", "y0", "y2", "z0")
+HY = ("z0", "y2", "y1", "y0")
 X = ("x1", "x0")
 AXES = ("z2", "z1", "z0", "x1", "x0", "y2", "y1", "y0", "core")
 VMEM = pl.BlockSpec(memory_space=pltpu.VMEM)

time: 113 us -> 113 us (level)
  the two profiles are of different devices: /device:TPU:64 before, /device:TPU:8 now
where the time goes in v13:
time: 113 us
  blocking collectives  87.8 us (78%)
  waiting for transfers between devices  13.9 us (12%)
  starting transfers between devices  6.33 us (6%)
  Pallas kernels  2.01 us (2%)
  local copies, waits for them, and re-layouts  1.82 us (2%)
    all_to_all x3, blocking collectives, exchange(): return lax.all_to_all(array, axes, 0, 0, tiled=True)  54.9 us
    all_gather x1, blocking collectives, local(): w = lax.all_gather(weighted, X, axis=0)  14.5 us
    all_gather x1, blocking collectives, local(): m = lax.all_gather(shard, X, axis=0)  13.9 us
    all_to_all x1, waiting for transfers between devices, exchange(): return lax.all_to_all(array, axes, 0, 0, tiled=True)  12.3 us
    all_to_all x1, starting transfers between devices, exchange(): return lax.all_to_all(array, axes, 0, 0, tiled=True)  4.42 us
    all_gather x1, blocking collectives, local(): got = lax.all_gather(send, 'core', axis=0)  2.37 us
  transfers between devices with their start and end apart: 2, of which 2 were waited for; matrix products, arithmetic and copies ran while one was open for 0% of the time, Pallas kernels for 0%

profile of v13, /device:TPU:8, one launch (start us, length us, event | category | flops | bytes accessed | tf_op | source)
XLA Modules:
  0.0 112.8 jit_solution(3207677368844167189)
XLA Ops:
  0.0 0.0 copy-start
  0.0 0.9 copy-done
  0.9 0.1 shard_map.17
  1.0 18.5 %all_to_all.20 = bf16[8,48,224]{2,1,0:T(8,128)(2,1)S(1)} all-to-all(bf16[8,48,224]{2,1,0:T(8,128)(2,1)S(1)} %get-tuple-element.12), channel_id=1, replica_groups=mesh['z2'=2,'z1'=2,'z0'=2,'x1'=2,'x0'=2,'y2'=2,'y1'=2,'y0'=2,'core'=2] {..., dimensions={0} | all-to-all | bytes 344064 | tf_op jit(solution)/shard_map/all_to_all | solution.py:40
  19.6 2.1 %all-gather = bf16[16,48,224]{2,1,0:T(8,128)(2,1)S(1)} all-gather(bf16[8,48,224]{2,1,0:T(8,128)(2,1)S(1)} %all_to_all.20), channel_id=2, replica_groups=mesh['z2'=2,'z1'=2,'z0'=2,'x1'=2,'x0'=2,'y2'=2,'y1'=2,'y0'=2,'core'=2] {..., dimensions={0}, use_global_device_ids=true | all-gather | bytes 516096 | tf_op jit(solution)/shard_map/all_gather | solution.py:119
  21.7 13.9 %all-gather.1 = bf16[8,4,48,224]{3,2,1,0:T(8,128)(2,1)S(1)} all-gather(bf16[2,4,48,224]{3,2,1,0:T(8,128)(2,1)S(1)} %shard_map.18), channel_id=3, replica_groups=mesh['z2'=2,'z1'=2,'z0'=2,'x1'=2,'x0'=2,'y2'=2,'y1'=2,'y0'=2,'core'=2] {..., dimensions={0}, use_global_device_ids=true | all-gather | bytes 860160 | tf_op jit(solution)/shard_map/all_gather | solution.py:121
  35.6 0.6 shard_map.19
  36.1 24.9 %all_to_all.21 = bf16[16,48,384]{2,1,0:T(8,128)(2,1)S(1)} all-to-all(bf16[16,48,384]{2,1,0:T(8,128)(2,1)S(1)} %bitcast.13), channel_id=1, replica_groups=mesh['z2'=2,'z1'=2,'z0'=2,'x1'=2,'x0'=2,'y2'=2,'y1'=2,'y0'=2,'core'=2] {..., dimensions={0} | all-to-all | bytes 1179648 | tf_op jit(solution)/shard_map/all_to_all | solution.py:40
  61.0 0.1 reduce_sum.12
  61.1 0.9 broadcast_in_dim.2
  62.0 4.4 %all-to-all-start.2 = ((bf16[16,48,384]{2,1,0:T(8,128)(2,1)}), bf16[16,48,384]{2,1,0:T(8,128)(2,1)S(1)}, u32[]{:S(2)}, u32[]{:S(2)}) async-start(bf16[16,48,384]{2,1,0:T(8,128)(2,1)} %broadcast_in_dim.2), calls=%async_computation.2 | async-start | bytes 1179648 | tf_op jit(solution)/shard_map/all_to_all | solution.py:40
  66.4 2.4 %all-gather.2 = bf16[8,4,48,224]{3,2,1,0:T(8,128)(2,1)S(1)} all-gather(bf16[4,4,48,224]{3,2,1,0:T(8,128)(2,1)S(1)} %shard_map.20), channel_id=4, replica_groups=mesh['z2'=2,'z1'=2,'z0'=2,'x1'=2,'x0'=2,'y2'=2,'y1'=2,'y0'=2,'core'=2] {..., dimensions={0}, use_global_device_ids=true | all-gather | bytes 1032192 | tf_op jit(solution)/shard_map/all_gather | solution.py:128
  68.8 12.3 %all-to-all-done.2.tiles = bf16[16,48,384]{2,1,0:T(8,128)(2,1)S(1)} async-done(((bf16[16,48,384]{2,1,0:T(8,128)(2,1)}), bf16[16,48,384]{2,1,0:T(8,128)(2,1)S(1)}, u32[]{:S(2)}, u32[]{:S(2)}) %all-to-all-start.2) | async-done | bytes 589856 | tf_op jit(solution)/shard_map/all_to_all | solution.py:40
  81.1 1.9 %collective-permute-start = (bf16[16,48,384]{2,1,0:T(8,128)(2,1)S(1)}, bf16[16,48,384]{2,1,0:T(8,128)(2,1)S(1)}, u32[]{:S(2)}, u32[]{:S(2)}) collective-permute-start(bf16[16,48,384]{2,1,0:T(8,128)(2,1)S(1)} %all-to-all-done.2.tiles), channel_id=1, source_target_pairs={{0,1},{1,0},{2,3},{3,2},{4,5},{5,4},{6,7},{7,6},{8,9},{9,8},{10,11... | collective-permute-start | bytes 1769480 | tf_op jit(solution)/shard_map/ppermute | solution.py:36
  83.0 0.4 shard_map.21.first
  83.4 1.6 %collective-permute-done.others = bf16[16,48,384]{2,1,0:T(8,128)(2,1)S(1)} collective-permute-done((bf16[16,48,384]{2,1,0:T(8,128)(2,1)S(1)}, bf16[16,48,384]{2,1,0:T(8,128)(2,1)S(1)}, u32[]{:S(2)}, u32[]{:S(2)}) %collective-permute-start) | collective-permute-done | bytes 589856 | tf_op jit(solution)/shard_map/ppermute | solution.py:36
  85.0 0.4 shard_map.22
  85.4 14.5 %all-gather.3 = bf16[32,48,224]{2,1,0:T(8,128)(2,1)S(1)} all-gather(bf16[8,48,224]{2,1,0:T(8,128)(2,1)S(1)} %shard_map.22), channel_id=5, replica_groups=mesh['z2'=2,'z1'=2,'z0'=2,'x1'=2,'x0'=2,'y2'=2,'y1'=2,'y0'=2,'core'=2] {..., dimensions={0}, use_global_device_ids=true | all-gather | bytes 860160 | tf_op jit(solution)/shard_map/all_gather | solution.py:136
  99.9 0.6 shard_map.23
  100.5 11.5 %all_to_all.22 = bf16[8,48,224]{2,1,0:T(8,128)(2,1)S(1)} all-to-all(bf16[8,48,224]{2,1,0:T(8,128)(2,1)S(1)} %shard_map.23), channel_id=1, replica_groups=mesh['z2'=2,'z1'=2,'z0'=2,'x1'=2,'x0'=2,'y2'=2,'y1'=2,'y0'=2,'core'=2] {..., dimensions={0} | all-to-all | bytes 344064 | tf_op jit(solution)/shard_map/all_to_all | solution.py:40
  112.0 0.8 fusion.1
  (3 shorter events, 0.1 us)
Async XLA Ops:
  0.0 0.9 copy-start
  62.0 19.2 %all-to-all-start.2 = ((bf16[16,48,384]{2,1,0:T(8,128)(2,1)}), bf16[16,48,384]{2,1,0:T(8,128)(2,1)S(1)}, u32[]{:S(2)}, u32[]{:S(2)}) async-start(bf16[16,48,384]{2,1,0:T(8,128)(2,1)} %broadcast_in_dim.2), calls=%async_computation.2 | async-start | bytes 1179648 | tf_op jit(solution)/shard_map/all_to_all | solution.py:40
  81.1 3.9 %collective-permute-start = (bf16[16,48,384]{2,1,0:T(8,128)(2,1)S(1)}, bf16[16,48,384]{2,1,0:T(8,128)(2,1)S(1)}, u32[]{:S(2)}, u32[]{:S(2)}) collective-permute-start(bf16[16,48,384]{2,1,0:T(8,128)(2,1)S(1)} %all-to-all-done.2.tiles), channel_id=1, source_target_pairs={{0,1},{1,0},{2,3},{3,2},{4,5},{5,4},{6,7},{7,6},{8,9},{9,8},{10,11... | collective-permute-start | bytes 1769480 | tf_op jit(solution)/shard_map/ppermute | solution.py:36

commit v14 on v13

--- a/solution.py
+++ b/solution.py
@@ -10,6 +10,8 @@
 F32 = jnp.float32
 BF16 = jnp.bfloat16
 A1, A3, A5 = 3.4445, -4.775, 2.0315
+SCALE = 0.2 * math.sqrt(7168)
+KAPPA = 2.7
 Z = ("z0", "z1", "z2")
 HY = ("z0", "y2", "y1", "y0")
 X = ("x1", "x0")
@@ -50,10 +52,9 @@
         yield member, bit["z2"] * 2 + bit["z1"], bit["z0"]
 
 
-def pack_body(momentum, sent, kept):
+def pack_body(momentum, sent):
     for member, layer, h in places():
         sent[member] = momentum[layer, :, h * 224 : h * 224 + 224]
-    kept[...] = momentum[...]
 
 
 def shard_body(both, out):
@@ -91,30 +92,28 @@
     out[...] = times(tiles, [stack([m[2 * g + i, core] for i in range(2)]) for g in range(2)])
 
 
-def weight_body(both, got, others, first, out):
+def weight_body(both, got, others, first, out, product):
     core = lax.axis_index("core")
     theirs = got.at[1 - core]
     groups = [stack([theirs[2 * g + i] for i in range(2)]) for g in range(2)]
     gm = first[...] + times(others, groups)
-    out[...] = (A3 * both[core].astype(F32) + A5 * gm).astype(BF16)
+    out[...] = ((A3 + KAPPA) * both[core].astype(F32) + A5 * gm).astype(BF16)
+    product[...] = gm
 
 
-def product_body(w, tiles, others, out):
+def product_body(w, tiles, others, both, gm, out):
     core = lax.axis_index("core")
-    total = jnp.zeros((8, 48, 224), F32)
+    total = A1 * both[core].astype(F32) - KAPPA * gm[...]
     for held, h in ((tiles, core), (others, 1 - core)):
         groups = [
             stack([w[2 * g + i, pl.ds(h * 4, 4)] for i in range(2)]) for g in range(2)
         ]
         total = total + times(held, groups)
-    out[...] = total.astype(BF16)
+    out[...] = (SCALE * total).astype(BF16)
 
 
 def local(momentum):
-    width = 7168
-    packed = jax.ShapeDtypeStruct((8, 48, 224), BF16)
-    kept = jax.ShapeDtypeStruct(momentum.shape, BF16)
-    sent, kept = kernel_calls(pack_body, [momentum], [packed, kept], 10**6)
+    sent = kernel_call(pack_body, [momentum], (8, 48, 224), BF16, 10**6)
     flops = 2 * 384 * 768 * 224
     both = lax.all_gather(exchange(sent, Z), "core", axis=0)
     shard = kernel_call(shard_body, [both], (2, 4, 48, 224), BF16, 10**6)
@@ -130,17 +129,17 @@
 
     others = swap(gathered)
     first = kernel_call(first_body, [m, gathered], (8, 48, 224), F32, flops)
-    weighted = kernel_call(
-        weight_body, [both, got, others, first], (8, 48, 224), BF16, flops
+    block = (8, 48, 224)
+    outputs = [jax.ShapeDtypeStruct(block, BF16), jax.ShapeDtypeStruct(block, F32)]
+    weighted, gm = kernel_calls(weight_body, [both, got, others, first], outputs, flops)
+    w = lax.all_gather(weighted, X, axis=0)
+    rows = kernel_call(
+        product_body, [w, gathered, others, both, gm], block, BF16, 2 * flops
     )
-    w = lax.all_gather(weighted, X, axis=0)
-    rows = kernel_call(product_body, [w, gathered, others], (8, 48, 224), BF16, 2 * flops)
-    back = exchange(rows, Z).astype(F32)
+    back = exchange(rows, Z)
     at = {(layer, h): member for member, layer, h in places()}
     halves = [[back[at[layer, h]] for layer in range(4)] for h in range(2)]
-    product = jnp.concatenate([jnp.stack(half) for half in halves], axis=2)
-    result = 0.2 * math.sqrt(width) * (A1 * kept.astype(F32) + product)
-    return result.astype(BF16)
+    return jnp.concatenate([jnp.stack(half) for half in halves], axis=2)
 
 
 def solution(mesh):

time: 113 us -> 113 us (level)
  no operation moved by 1% of the time
where the time goes in v14:
time: 113 us
  blocking collectives  87.8 us (78%)
  waiting for transfers between devices  13.9 us (12%)
  starting transfers between devices  6.33 us (6%)
  Pallas kernels  2.01 us (2%)
  local copies, waits for them, and re-layouts  1.81 us (2%)
    all_to_all x3, blocking collectives, exchange(): return lax.all_to_all(array, axes, 0, 0, tiled=True)  54.9 us
    all_gather x1, blocking collectives, local(): w = lax.all_gather(weighted, X, axis=0)  14.5 us
    all_gather x1, blocking collectives, local(): m = lax.all_gather(shard, X, axis=0)  13.9 us
    all_to_all x1, waiting for transfers between devices, exchange(): return lax.all_to_all(array, axes, 0, 0, tiled=True)  12.3 us
    all_to_all x1, starting transfers between devices, exchange(): return lax.all_to_all(array, axes, 0, 0, tiled=True)  4.42 us
    all_gather x1, blocking collectives, local(): got = lax.all_gather(send, 'core', axis=0)  2.37 us
  transfers between devices with their start and end apart: 2, of which 2 were waited for; matrix products, arithmetic and copies ran while one was open for 0% of the time, Pallas kernels for 0%

profile of v14, /device:TPU:8, one launch (start us, length us, event | category | flops | bytes accessed | tf_op | source)
XLA Modules:
  0.0 112.8 jit_solution(1741291968042469869)
XLA Ops:
  0.0 0.0 copy-start
  0.0 0.9 copy-done
  0.9 0.1 shard_map.17
  1.0 18.5 %all_to_all.20 = bf16[8,48,224]{2,1,0:T(8,128)(2,1)S(1)} all-to-all(bf16[8,48,224]{2,1,0:T(8,128)(2,1)S(1)} %shard_map.17), channel_id=1, replica_groups=mesh['z2'=2,'z1'=2,'z0'=2,'x1'=2,'x0'=2,'y2'=2,'y1'=2,'y0'=2,'core'=2] {..., dimensions={0} | all-to-all | bytes 344064 | tf_op jit(solution)/shard_map/all_to_all | solution.py:42
  19.6 2.1 %all-gather = bf16[16,48,224]{2,1,0:T(8,128)(2,1)S(1)} all-gather(bf16[8,48,224]{2,1,0:T(8,128)(2,1)S(1)} %all_to_all.20), channel_id=2, replica_groups=mesh['z2'=2,'z1'=2,'z0'=2,'x1'=2,'x0'=2,'y2'=2,'y1'=2,'y0'=2,'core'=2] {..., dimensions={0}, use_global_device_ids=true | all-gather | bytes 516096 | tf_op jit(solution)/shard_map/all_gather | solution.py:118
  21.7 13.9 %all-gather.1 = bf16[8,4,48,224]{3,2,1,0:T(8,128)(2,1)S(1)} all-gather(bf16[2,4,48,224]{3,2,1,0:T(8,128)(2,1)S(1)} %shard_map.18), channel_id=3, replica_groups=mesh['z2'=2,'z1'=2,'z0'=2,'x1'=2,'x0'=2,'y2'=2,'y1'=2,'y0'=2,'core'=2] {..., dimensions={0}, use_global_device_ids=true | all-gather | bytes 860160 | tf_op jit(solution)/shard_map/all_gather | solution.py:120
  35.6 0.6 shard_map.19
  36.1 24.9 %all_to_all.21 = bf16[16,48,384]{2,1,0:T(8,128)(2,1)S(1)} all-to-all(bf16[16,48,384]{2,1,0:T(8,128)(2,1)S(1)} %bitcast.14), channel_id=1, replica_groups=mesh['z2'=2,'z1'=2,'z0'=2,'x1'=2,'x0'=2,'y2'=2,'y1'=2,'y0'=2,'core'=2] {..., dimensions={0} | all-to-all | bytes 1179648 | tf_op jit(solution)/shard_map/all_to_all | solution.py:42
  61.0 0.1 reduce_sum.12
  61.1 0.9 broadcast_in_dim.2
  62.0 4.4 %all-to-all-start.2 = ((bf16[16,48,384]{2,1,0:T(8,128)(2,1)}), bf16[16,48,384]{2,1,0:T(8,128)(2,1)S(1)}, u32[]{:S(2)}, u32[]{:S(2)}) async-start(bf16[16,48,384]{2,1,0:T(8,128)(2,1)} %broadcast_in_dim.2), calls=%async_computation.2 | async-start | bytes 1179648 | tf_op jit(solution)/shard_map/all_to_all | solution.py:42
  66.4 2.4 %all-gather.2 = bf16[8,4,48,224]{3,2,1,0:T(8,128)(2,1)S(1)} all-gather(bf16[4,4,48,224]{3,2,1,0:T(8,128)(2,1)S(1)} %shard_map.20), channel_id=4, replica_groups=mesh['z2'=2,'z1'=2,'z0'=2,'x1'=2,'x0'=2,'y2'=2,'y1'=2,'y0'=2,'core'=2] {..., dimensions={0}, use_global_device_ids=true | all-gather | bytes 1032192 | tf_op jit(solution)/shard_map/all_gather | solution.py:127
  68.8 12.3 %all-to-all-done.2.tiles = bf16[16,48,384]{2,1,0:T(8,128)(2,1)S(1)} async-done(((bf16[16,48,384]{2,1,0:T(8,128)(2,1)}), bf16[16,48,384]{2,1,0:T(8,128)(2,1)S(1)}, u32[]{:S(2)}, u32[]{:S(2)}) %all-to-all-start.2) | async-done | bytes 589856 | tf_op jit(solution)/shard_map/all_to_all | solution.py:42
  81.1 1.9 %collective-permute-start = (bf16[16,48,384]{2,1,0:T(8,128)(2,1)S(1)}, bf16[16,48,384]{2,1,0:T(8,128)(2,1)S(1)}, u32[]{:S(2)}, u32[]{:S(2)}) collective-permute-start(bf16[16,48,384]{2,1,0:T(8,128)(2,1)S(1)} %all-to-all-done.2.tiles), channel_id=1, source_target_pairs={{0,1},{1,0},{2,3},{3,2},{4,5},{5,4},{6,7},{7,6},{8,9},{9,8},{10,11... | collective-permute-start | bytes 1769480 | tf_op jit(solution)/shard_map/ppermute | solution.py:38
  83.0 0.4 shard_map.21.first
  83.4 1.6 %collective-permute-done.others = bf16[16,48,384]{2,1,0:T(8,128)(2,1)S(1)} collective-permute-done((bf16[16,48,384]{2,1,0:T(8,128)(2,1)S(1)}, bf16[16,48,384]{2,1,0:T(8,128)(2,1)S(1)}, u32[]{:S(2)}, u32[]{:S(2)}) %collective-permute-start) | collective-permute-done | bytes 589856 | tf_op jit(solution)/shard_map/ppermute | solution.py:38
  85.0 0.4 shard_map.22
  85.4 14.5 %all-gather.3 = bf16[32,48,224]{2,1,0:T(8,128)(2,1)S(1)} all-gather(bf16[8,48,224]{2,1,0:T(8,128)(2,1)S(1)} %get-tuple-element.15), channel_id=5, replica_groups=mesh['z2'=2,'z1'=2,'z0'=2,'x1'=2,'x0'=2,'y2'=2,'y1'=2,'y0'=2,'core'=2] {..., dimensions={0}, use_global_device_ids=true | all-gather | bytes 860160 | tf_op jit(solution)/shard_map/all_gather | solution.py:135
  99.9 0.6 shard_map.23
  100.5 11.5 %all_to_all.22 = bf16[8,48,224]{2,1,0:T(8,128)(2,1)S(1)} all-to-all(bf16[8,48,224]{2,1,0:T(8,128)(2,1)S(1)} %shard_map.23), channel_id=1, replica_groups=mesh['z2'=2,'z1'=2,'z0'=2,'x1'=2,'x0'=2,'y2'=2,'y1'=2,'y0'=2,'core'=2] {..., dimensions={0} | all-to-all | bytes 344064 | tf_op jit(solution)/shard_map/all_to_all | solution.py:42
  112.0 0.8 maximum_maximum_fusion
  (3 shorter events, 0.1 us)
Async XLA Ops:
  0.0 0.9 copy-start
  62.0 19.2 %all-to-all-start.2 = ((bf16[16,48,384]{2,1,0:T(8,128)(2,1)}), bf16[16,48,384]{2,1,0:T(8,128)(2,1)S(1)}, u32[]{:S(2)}, u32[]{:S(2)}) async-start(bf16[16,48,384]{2,1,0:T(8,128)(2,1)} %broadcast_in_dim.2), calls=%async_computation.2 | async-start | bytes 1179648 | tf_op jit(solution)/shard_map/all_to_all | solution.py:42
  81.1 3.9 %collective-permute-start = (bf16[16,48,384]{2,1,0:T(8,128)(2,1)S(1)}, bf16[16,48,384]{2,1,0:T(8,128)(2,1)S(1)}, u32[]{:S(2)}, u32[]{:S(2)}) collective-permute-start(bf16[16,48,384]{2,1,0:T(8,128)(2,1)S(1)} %all-to-all-done.2.tiles), channel_id=1, source_target_pairs={{0,1},{1,0},{2,3},{3,2},{4,5},{5,4},{6,7},{7,6},{8,9},{9,8},{10,11... | collective-permute-start | bytes 1769480 | tf_op jit(solution)/shard_map/ppermute | solution.py:38

commit v15 on v14

--- a/solution.py
+++ b/solution.py
@@ -19,16 +19,17 @@
 VMEM = pl.BlockSpec(memory_space=pltpu.VMEM)
 
 
-def kernel_call(body, inputs, shape, dtype, flops):
-    return kernel_calls(body, inputs, [jax.ShapeDtypeStruct(shape, dtype)], flops)[0]
+def kernel_call(body, inputs, shape, dtype, flops, scratch=()):
+    return kernel_calls(body, inputs, [jax.ShapeDtypeStruct(shape, dtype)], flops, scratch)[0]
 
 
-def kernel_calls(body, inputs, outputs, flops):
+def kernel_calls(body, inputs, outputs, flops, scratch=()):
     return pl.pallas_call(
         body,
         out_shape=outputs,
         in_specs=[VMEM] * len(inputs),
         out_specs=[VMEM] * len(outputs),
+        scratch_shapes=scratch,
         cost_estimate=pl.CostEstimate(flops=flops, bytes_accessed=0, transcendentals=0),
         compiler_params=pltpu.CompilerParams(vmem_limit_bytes=40 * 2**20),
     )(*inputs)
@@ -92,16 +93,36 @@
     out[...] = times(tiles, [stack([m[2 * g + i, core] for i in range(2)]) for g in range(2)])
 
 
+def squeeze(blocks, out):
+    for z in range(8):
+        out[z] = blocks[z][:, :128]
+    for h in range(2):
+        tails = jnp.concatenate([blocks[h * 4 + i][:, 128:] for i in range(4)], axis=1)
+        for k in range(3):
+            out[8 + h * 3 + k] = tails[:, k * 128 : k * 128 + 128]
+
+
+def unsqueeze(packed, w):
+    for x in range(4):
+        for h in range(2):
+            tails = jnp.concatenate([packed[x, 8 + h * 3 + k] for k in range(3)], axis=1)
+            for i in range(4):
+                tail = tails[:, i * 96 : i * 96 + 96]
+                w[x, h * 4 + i] = jnp.concatenate([packed[x, h * 4 + i], tail], axis=1)
+
+
 def weight_body(both, got, others, first, out, product):
     core = lax.axis_index("core")
     theirs = got.at[1 - core]
     groups = [stack([theirs[2 * g + i] for i in range(2)]) for g in range(2)]
     gm = first[...] + times(others, groups)
-    out[...] = ((A3 + KAPPA) * both[core].astype(F32) + A5 * gm).astype(BF16)
+    w = ((A3 + KAPPA) * both[core].astype(F32) + A5 * gm).astype(BF16)
+    squeeze([w[z] for z in range(8)], out)
     product[...] = gm
 
 
-def product_body(w, tiles, others, both, gm, out):
+def product_body(packed, tiles, others, both, gm, out, w):
+    unsqueeze(packed, w)
     core = lax.axis_index("core")
     total = A1 * both[core].astype(F32) - KAPPA * gm[...]
     for held, h in ((tiles, core), (others, 1 - core)):
@@ -130,11 +151,16 @@
     others = swap(gathered)
     first = kernel_call(first_body, [m, gathered], (8, 48, 224), F32, flops)
     block = (8, 48, 224)
-    outputs = [jax.ShapeDtypeStruct(block, BF16), jax.ShapeDtypeStruct(block, F32)]
+    outputs = [jax.ShapeDtypeStruct((14, 48, 128), BF16), jax.ShapeDtypeStruct(block, F32)]
     weighted, gm = kernel_calls(weight_body, [both, got, others, first], outputs, flops)
     w = lax.all_gather(weighted, X, axis=0)
     rows = kernel_call(
-        product_body, [w, gathered, others, both, gm], block, BF16, 2 * flops
+        product_body,
+        [w, gathered, others, both, gm],
+        block,
+        BF16,
+        2 * flops,
+        [pltpu.VMEM((4, 8, 48, 224), BF16)],
     )
     back = exchange(rows, Z)
     at = {(layer, h): member for member, layer, h in places()}

time: 113 us -> 113 us (level)
  no operation moved by 1% of the time
where the time goes in v15:
time: 113 us
  blocking collectives  87.2 us (77%)
  waiting for transfers between devices  13.9 us (12%)
  starting transfers between devices  6.33 us (6%)
  Pallas kernels  2.28 us (2%)
  local copies, waits for them, and re-layouts  1.81 us (2%)
    all_to_all x3, blocking collectives, exchange(): return lax.all_to_all(array, axes, 0, 0, tiled=True)  55 us
    all_gather x1, blocking collectives, local(): w = lax.all_gather(weighted, X, axis=0)  13.9 us
    all_gather x1, blocking collectives, local(): m = lax.all_gather(shard, X, axis=0)  13.9 us
    all_to_all x1, waiting for transfers between devices, exchange(): return lax.all_to_all(array, axes, 0, 0, tiled=True)  12.3 us
    all_to_all x1, starting transfers between devices, exchange(): return lax.all_to_all(array, axes, 0, 0, tiled=True)  4.42 us
    all_gather x1, blocking collectives, local(): got = lax.all_gather(send, 'core', axis=0)  2.37 us
    pallas_call x7, Pallas kernels, kernel_calls(): pl.pallas_call(body, out_shape=outputs, in_specs=[VMEM] * len(inputs), ou...  2.28 us
  transfers between devices with their start and end apart: 2, of which 2 were waited for; matrix products, arithmetic and copies ran while one was open for 0% of the time, Pallas kernels for 0%

profile of v15, /device:TPU:8, one launch (start us, length us, event | category | flops | bytes accessed | tf_op | source)
XLA Modules:
  0.0 112.5 jit_solution(18298142197375053547)
XLA Ops:
  0.0 0.0 copy-start
  0.0 0.9 copy-done
  0.9 0.1 shard_map.17
  1.0 18.5 %all_to_all.20 = bf16[8,48,224]{2,1,0:T(8,128)(2,1)S(1)} all-to-all(bf16[8,48,224]{2,1,0:T(8,128)(2,1)S(1)} %shard_map.17), channel_id=1, replica_groups=mesh['z2'=2,'z1'=2,'z0'=2,'x1'=2,'x0'=2,'y2'=2,'y1'=2,'y0'=2,'core'=2] {..., dimensions={0} | all-to-all | bytes 344064 | tf_op jit(solution)/shard_map/all_to_all | solution.py:43
  19.6 2.1 %all-gather = bf16[16,48,224]{2,1,0:T(8,128)(2,1)S(1)} all-gather(bf16[8,48,224]{2,1,0:T(8,128)(2,1)S(1)} %all_to_all.20), channel_id=2, replica_groups=mesh['z2'=2,'z1'=2,'z0'=2,'x1'=2,'x0'=2,'y2'=2,'y1'=2,'y0'=2,'core'=2] {..., dimensions={0}, use_global_device_ids=true | all-gather | bytes 516096 | tf_op jit(solution)/shard_map/all_gather | solution.py:139
  21.7 13.9 %all-gather.1 = bf16[8,4,48,224]{3,2,1,0:T(8,128)(2,1)S(1)} all-gather(bf16[2,4,48,224]{3,2,1,0:T(8,128)(2,1)S(1)} %shard_map.18), channel_id=3, replica_groups=mesh['z2'=2,'z1'=2,'z0'=2,'x1'=2,'x0'=2,'y2'=2,'y1'=2,'y0'=2,'core'=2] {..., dimensions={0}, use_global_device_ids=true | all-gather | bytes 860160 | tf_op jit(solution)/shard_map/all_gather | solution.py:141
  35.6 0.6 shard_map.19
  36.1 24.9 %all_to_all.21 = bf16[16,48,384]{2,1,0:T(8,128)(2,1)S(1)} all-to-all(bf16[16,48,384]{2,1,0:T(8,128)(2,1)S(1)} %bitcast.14), channel_id=1, replica_groups=mesh['z2'=2,'z1'=2,'z0'=2,'x1'=2,'x0'=2,'y2'=2,'y1'=2,'y0'=2,'core'=2] {..., dimensions={0} | all-to-all | bytes 1179648 | tf_op jit(solution)/shard_map/all_to_all | solution.py:43
  61.0 0.1 reduce_sum.12
  61.1 0.9 broadcast_in_dim.2
  62.0 4.4 %all-to-all-start.2 = ((bf16[16,48,384]{2,1,0:T(8,128)(2,1)}), bf16[16,48,384]{2,1,0:T(8,128)(2,1)S(1)}, u32[]{:S(2)}, u32[]{:S(2)}) async-start(bf16[16,48,384]{2,1,0:T(8,128)(2,1)} %broadcast_in_dim.2), calls=%async_computation.2 | async-start | bytes 1179648 | tf_op jit(solution)/shard_map/all_to_all | solution.py:43
  66.4 2.4 %all-gather.2 = bf16[8,4,48,224]{3,2,1,0:T(8,128)(2,1)S(1)} all-gather(bf16[4,4,48,224]{3,2,1,0:T(8,128)(2,1)S(1)} %shard_map.20), channel_id=4, replica_groups=mesh['z2'=2,'z1'=2,'z0'=2,'x1'=2,'x0'=2,'y2'=2,'y1'=2,'y0'=2,'core'=2] {..., dimensions={0}, use_global_device_ids=true | all-gather | bytes 1032192 | tf_op jit(solution)/shard_map/all_gather | solution.py:148
  68.8 12.3 %all-to-all-done.2.tiles = bf16[16,48,384]{2,1,0:T(8,128)(2,1)S(1)} async-done(((bf16[16,48,384]{2,1,0:T(8,128)(2,1)}), bf16[16,48,384]{2,1,0:T(8,128)(2,1)S(1)}, u32[]{:S(2)}, u32[]{:S(2)}) %all-to-all-start.2) | async-done | bytes 589856 | tf_op jit(solution)/shard_map/all_to_all | solution.py:43
  81.1 1.9 %collective-permute-start = (bf16[16,48,384]{2,1,0:T(8,128)(2,1)S(1)}, bf16[16,48,384]{2,1,0:T(8,128)(2,1)S(1)}, u32[]{:S(2)}, u32[]{:S(2)}) collective-permute-start(bf16[16,48,384]{2,1,0:T(8,128)(2,1)S(1)} %all-to-all-done.2.tiles), channel_id=1, source_target_pairs={{0,1},{1,0},{2,3},{3,2},{4,5},{5,4},{6,7},{7,6},{8,9},{9,8},{10,11... | collective-permute-start | bytes 1769480 | tf_op jit(solution)/shard_map/ppermute | solution.py:39
  83.0 0.4 shard_map.21.first
  83.4 1.6 %collective-permute-done.others = bf16[16,48,384]{2,1,0:T(8,128)(2,1)S(1)} collective-permute-done((bf16[16,48,384]{2,1,0:T(8,128)(2,1)S(1)}, bf16[16,48,384]{2,1,0:T(8,128)(2,1)S(1)}, u32[]{:S(2)}, u32[]{:S(2)}) %collective-permute-start) | collective-permute-done | bytes 589856 | tf_op jit(solution)/shard_map/ppermute | solution.py:39
  85.0 0.4 shard_map.22
  85.4 13.9 %all-gather.3 = bf16[56,48,128]{2,1,0:T(8,128)(2,1)S(1)} all-gather(bf16[14,48,128]{2,1,0:T(8,128)(2,1)S(1)} %get-tuple-element.15), channel_id=5, replica_groups=mesh['z2'=2,'z1'=2,'z0'=2,'x1'=2,'x0'=2,'y2'=2,'y1'=2,'y0'=2,'core'=2] {..., dimensions={0}, use_global_device_ids=true | all-gather | bytes 860160 | tf_op jit(solution)/shard_map/all_gather | solution.py:156
  99.4 0.8 shard_map.23
  100.2 11.6 %all_to_all.22 = bf16[8,48,224]{2,1,0:T(8,128)(2,1)S(1)} all-to-all(bf16[8,48,224]{2,1,0:T(8,128)(2,1)S(1)} %shard_map.23), channel_id=1, replica_groups=mesh['z2'=2,'z1'=2,'z0'=2,'x1'=2,'x0'=2,'y2'=2,'y1'=2,'y0'=2,'core'=2] {..., dimensions={0} | all-to-all | bytes 344064 | tf_op jit(solution)/shard_map/all_to_all | solution.py:43
  111.7 0.8 maximum_maximum_fusion
  (3 shorter events, 0.1 us)
Async XLA Ops:
  0.0 0.9 copy-start
  62.0 19.2 %all-to-all-start.2 = ((bf16[16,48,384]{2,1,0:T(8,128)(2,1)}), bf16[16,48,384]{2,1,0:T(8,128)(2,1)S(1)}, u32[]{:S(2)}, u32[]{:S(2)}) async-start(bf16[16,48,384]{2,1,0:T(8,128)(2,1)} %broadcast_in_dim.2), calls=%async_computation.2 | async-start | bytes 1179648 | tf_op jit(solution)/shard_map/all_to_all | solution.py:43
  81.1 3.9 %collective-permute-start = (bf16[16,48,384]{2,1,0:T(8,128)(2,1)S(1)}, bf16[16,48,384]{2,1,0:T(8,128)(2,1)S(1)}, u32[]{:S(2)}, u32[]{:S(2)}) collective-permute-start(bf16[16,48,384]{2,1,0:T(8,128)(2,1)S(1)} %all-to-all-done.2.tiles), channel_id=1, source_target_pairs={{0,1},{1,0},{2,3},{3,2},{4,5},{5,4},{6,7},{7,6},{8,9},{9,8},{10,11... | collective-permute-start | bytes 1769480 | tf_op jit(solution)/shard_map/ppermute | solution.py:39

commit v16 on v15

--- a/solution.py
+++ b/solution.py
@@ -58,41 +58,6 @@
         sent[member] = momentum[layer, :, h * 224 : h * 224 + 224]
 
 
-def shard_body(both, out):
-    for columns in range(2):
-        out[columns] = both[columns, pl.ds(lax.axis_index("core") * 4, 4)]
-
-
-def gram_body(both, m, out):
-    for group in range(2):
-        total = jnp.zeros((384, 384), F32)
-        for columns in range(2):
-            total = total + lax.dot_general(
-                both[columns].reshape(384, 224),
-                stack([m[2 * group + i, columns] for i in range(2)]),
-                (((1,), (1,)), ((), ())),
-                preferred_element_type=F32,
-            )
-        out[:, group] = total.astype(BF16).reshape(8, 48, 384)
-
-
-def send_body(m, out):
-    out[...] = m[:, 1 - lax.axis_index("core")]
-
-
-def times(tiles, groups):
-    total = jnp.zeros((384, 224), F32)
-    for group in range(2):
-        panel = jnp.concatenate([tiles[2 * block + group] for block in range(8)], axis=0)
-        total = total + jnp.dot(panel, groups[group], preferred_element_type=F32)
-    return total.reshape(8, 48, 224)
-
-
-def first_body(m, tiles, out):
-    core = lax.axis_index("core")
-    out[...] = times(tiles, [stack([m[2 * g + i, core] for i in range(2)]) for g in range(2)])
-
-
 def squeeze(blocks, out):
     for z in range(8):
         out[z] = blocks[z][:, :128]
@@ -109,6 +74,43 @@
             for i in range(4):
                 tail = tails[:, i * 96 : i * 96 + 96]
                 w[x, h * 4 + i] = jnp.concatenate([packed[x, h * 4 + i], tail], axis=1)
+
+
+def shard_body(both, out):
+    mine = pl.ds(lax.axis_index("core") * 4, 4)
+    blocks = [both[columns, mine] for columns in range(2)]
+    squeeze([blocks[k // 4][k % 4] for k in range(8)], out)
+
+
+def gram_body(both, packed, out, m):
+    unsqueeze(packed, m)
+    for group in range(2):
+        total = jnp.zeros((384, 384), F32)
+        for columns in range(2):
+            total = total + lax.dot_general(
+                both[columns].reshape(384, 224),
+                stack([m[2 * group + i, columns * 4 : columns * 4 + 4] for i in range(2)]),
+                (((1,), (1,)), ((), ())),
+                preferred_element_type=F32,
+            )
+        out[:, group] = total.astype(BF16).reshape(8, 48, 384)
+
+
+def send_body(m, out):
+    out[...] = m[:, pl.ds((1 - lax.axis_index("core")) * 4, 4)]
+
+
+def times(tiles, groups):
+    total = jnp.zeros((384, 224), F32)
+    for group in range(2):
+        panel = jnp.concatenate([tiles[2 * block + group] for block in range(8)], axis=0)
+        total = total + jnp.dot(panel, groups[group], preferred_element_type=F32)
+    return total.reshape(8, 48, 224)
+
+
+def first_body(m, tiles, out):
+    own = pl.ds(lax.axis_index("core") * 4, 4)
+    out[...] = times(tiles, [stack([m[2 * g + i, own] for i in range(2)]) for g in range(2)])
 
 
 def weight_body(both, got, others, first, out, product):
@@ -137,9 +139,10 @@
     sent = kernel_call(pack_body, [momentum], (8, 48, 224), BF16, 10**6)
     flops = 2 * 384 * 768 * 224
     both = lax.all_gather(exchange(sent, Z), "core", axis=0)
-    shard = kernel_call(shard_body, [both], (2, 4, 48, 224), BF16, 10**6)
-    m = lax.all_gather(shard, X, axis=0)
-    part = kernel_call(gram_body, [both, m], (8, 2, 48, 384), BF16, 2 * flops)
+    shard = kernel_call(shard_body, [both], (14, 48, 128), BF16, 10**6)
+    outputs = [jax.ShapeDtypeStruct(dims, BF16) for dims in ((8, 2, 48, 384), (4, 8, 48, 224))]
+    packed = lax.all_gather(shard, X, axis=0)
+    part, m = kernel_calls(gram_body, [both, packed], outputs, 2 * flops)
     parts = exchange(part.reshape(16, 48, 384), HY)
     tile = jnp.sum(parts.astype(F32), axis=0).astype(BF16)
     tile, later = lax.optimization_barrier((tile, m))

time: 113 us -> 113 us (level)
  no operation moved by 1% of the time
where the time goes in v16:
time: 113 us; the launch traced here: 112 us
  blocking collectives  86.8 us (77%)
  waiting for transfers between devices  13.9 us (12%)
  starting transfers between devices  6.35 us (6%)
  Pallas kernels  2.46 us (2%)
  local copies, waits for them, and re-layouts  1.82 us (2%)
    all_to_all x3, blocking collectives, exchange(): return lax.all_to_all(array, axes, 0, 0, tiled=True)  54.9 us
    all_gather x1, blocking collectives, local(): w = lax.all_gather(weighted, X, axis=0)  13.9 us
    all_gather x1, blocking collectives, local(): packed = lax.all_gather(shard, X, axis=0)  13.6 us
    all_to_all x1, waiting for transfers between devices, exchange(): return lax.all_to_all(array, axes, 0, 0, tiled=True)  12.3 us
    all_to_all x1, starting transfers between devices, exchange(): return lax.all_to_all(array, axes, 0, 0, tiled=True)  4.44 us
    pallas_call x7, Pallas kernels, kernel_calls(): pl.pallas_call(body, out_shape=outputs, in_specs=[VMEM] * len(inputs), ou...  2.46 us
    all_gather x1, blocking collectives, local(): got = lax.all_gather(send, 'core', axis=0)  2.37 us
  transfers between devices with their start and end apart: 2, of which 2 were waited for; matrix products, arithmetic and copies ran while one was open for 0% of the time, Pallas kernels for 0%

profile of v16, /device:TPU:8, one launch (start us, length us, event | category | flops | bytes accessed | tf_op | source)
XLA Modules:
  0.0 112.3 jit_solution(18091214359217966609)
XLA Ops:
  0.0 0.0 copy-start
  0.0 0.9 copy-done
  0.9 0.1 shard_map.17
  1.0 18.5 %all_to_all.20 = bf16[8,48,224]{2,1,0:T(8,128)(2,1)S(1)} all-to-all(bf16[8,48,224]{2,1,0:T(8,128)(2,1)S(1)} %shard_map.17), channel_id=1, replica_groups=mesh['z2'=2,'z1'=2,'z0'=2,'x1'=2,'x0'=2,'y2'=2,'y1'=2,'y0'=2,'core'=2] {..., dimensions={0} | all-to-all | bytes 344064 | tf_op jit(solution)/shard_map/all_to_all | solution.py:43
  19.6 2.1 %all-gather = bf16[16,48,224]{2,1,0:T(8,128)(2,1)S(1)} all-gather(bf16[8,48,224]{2,1,0:T(8,128)(2,1)S(1)} %all_to_all.20), channel_id=2, replica_groups=mesh['z2'=2,'z1'=2,'z0'=2,'x1'=2,'x0'=2,'y2'=2,'y1'=2,'y0'=2,'core'=2] {..., dimensions={0}, use_global_device_ids=true | all-gather | bytes 516096 | tf_op jit(solution)/shard_map/all_gather | solution.py:141
  21.6 0.1 shard_map.18
  21.7 13.6 %all-gather.1 = bf16[56,48,128]{2,1,0:T(8,128)(2,1)S(1)} all-gather(bf16[14,48,128]{2,1,0:T(8,128)(2,1)S(1)} %shard_map.18), channel_id=3, replica_groups=mesh['z2'=2,'z1'=2,'z0'=2,'x1'=2,'x0'=2,'y2'=2,'y1'=2,'y0'=2,'core'=2] {..., dimensions={0}, use_global_device_ids=true | all-gather | bytes 860160 | tf_op jit(solution)/shard_map/all_gather | solution.py:144
  35.3 0.7 shard_map.19
  36.0 24.8 %all_to_all.21 = bf16[16,48,384]{2,1,0:T(8,128)(2,1)S(1)} all-to-all(bf16[16,48,384]{2,1,0:T(8,128)(2,1)S(1)} %bitcast.12), channel_id=1, replica_groups=mesh['z2'=2,'z1'=2,'z0'=2,'x1'=2,'x0'=2,'y2'=2,'y1'=2,'y0'=2,'core'=2] {..., dimensions={0} | all-to-all | bytes 1179648 | tf_op jit(solution)/shard_map/all_to_all | solution.py:43
  60.8 0.1 reduce_sum.12
  60.9 0.9 broadcast_in_dim.2
  61.8 4.4 %all-to-all-start.2 = ((bf16[16,48,384]{2,1,0:T(8,128)(2,1)}), bf16[16,48,384]{2,1,0:T(8,128)(2,1)S(1)}, u32[]{:S(2)}, u32[]{:S(2)}) async-start(bf16[16,48,384]{2,1,0:T(8,128)(2,1)} %broadcast_in_dim.2), calls=%async_computation.2 | async-start | bytes 1179648 | tf_op jit(solution)/shard_map/all_to_all | solution.py:43
  66.3 2.4 %all-gather.2 = bf16[8,4,48,224]{3,2,1,0:T(8,128)(2,1)S(1)} all-gather(bf16[4,4,48,224]{3,2,1,0:T(8,128)(2,1)S(1)} %shard_map.20), channel_id=4, replica_groups=mesh['z2'=2,'z1'=2,'z0'=2,'x1'=2,'x0'=2,'y2'=2,'y1'=2,'y0'=2,'core'=2] {..., dimensions={0}, use_global_device_ids=true | all-gather | bytes 1032192 | tf_op jit(solution)/shard_map/all_gather | solution.py:151
  68.6 12.3 %all-to-all-done.2.tiles = bf16[16,48,384]{2,1,0:T(8,128)(2,1)S(1)} async-done(((bf16[16,48,384]{2,1,0:T(8,128)(2,1)}), bf16[16,48,384]{2,1,0:T(8,128)(2,1)S(1)}, u32[]{:S(2)}, u32[]{:S(2)}) %all-to-all-start.2) | async-done | bytes 589856 | tf_op jit(solution)/shard_map/all_to_all | solution.py:43
  80.9 1.9 %collective-permute-start = (bf16[16,48,384]{2,1,0:T(8,128)(2,1)S(1)}, bf16[16,48,384]{2,1,0:T(8,128)(2,1)S(1)}, u32[]{:S(2)}, u32[]{:S(2)}) collective-permute-start(bf16[16,48,384]{2,1,0:T(8,128)(2,1)S(1)} %all-to-all-done.2.tiles), channel_id=1, source_target_pairs={{0,1},{1,0},{2,3},{3,2},{4,5},{5,4},{6,7},{7,6},{8,9},{9,8},{10,11... | collective-permute-start | bytes 1769480 | tf_op jit(solution)/shard_map/ppermute | solution.py:39
  82.9 0.4 shard_map.21.first
  83.2 1.6 %collective-permute-done.others = bf16[16,48,384]{2,1,0:T(8,128)(2,1)S(1)} collective-permute-done((bf16[16,48,384]{2,1,0:T(8,128)(2,1)S(1)}, bf16[16,48,384]{2,1,0:T(8,128)(2,1)S(1)}, u32[]{:S(2)}, u32[]{:S(2)}) %collective-permute-start) | collective-permute-done | bytes 589856 | tf_op jit(solution)/shard_map/ppermute | solution.py:39
  84.8 0.4 shard_map.22
  85.3 13.9 %all-gather.3 = bf16[56,48,128]{2,1,0:T(8,128)(2,1)S(1)} all-gather(bf16[14,48,128]{2,1,0:T(8,128)(2,1)S(1)} %get-tuple-element.19), channel_id=5, replica_groups=mesh['z2'=2,'z1'=2,'z0'=2,'x1'=2,'x0'=2,'y2'=2,'y1'=2,'y0'=2,'core'=2] {..., dimensions={0}, use_global_device_ids=true | all-gather | bytes 860160 | tf_op jit(solution)/shard_map/all_gather | solution.py:159
  99.2 0.8 shard_map.23
  100.0 11.6 %all_to_all.22 = bf16[8,48,224]{2,1,0:T(8,128)(2,1)S(1)} all-to-all(bf16[8,48,224]{2,1,0:T(8,128)(2,1)S(1)} %shard_map.23), channel_id=1, replica_groups=mesh['z2'=2,'z1'=2,'z0'=2,'x1'=2,'x0'=2,'y2'=2,'y1'=2,'y0'=2,'core'=2] {..., dimensions={0} | all-to-all | bytes 344064 | tf_op jit(solution)/shard_map/all_to_all | solution.py:43
  111.5 0.8 maximum_maximum_fusion
  (2 shorter events, 0.0 us)
Async XLA Ops:
  0.0 0.9 copy-start
  61.8 19.2 %all-to-all-start.2 = ((bf16[16,48,384]{2,1,0:T(8,128)(2,1)}), bf16[16,48,384]{2,1,0:T(8,128)(2,1)S(1)}, u32[]{:S(2)}, u32[]{:S(2)}) async-start(bf16[16,48,384]{2,1,0:T(8,128)(2,1)} %broadcast_in_dim.2), calls=%async_computation.2 | async-start | bytes 1179648 | tf_op jit(solution)/shard_map/all_to_all | solution.py:43
  80.9 3.9 %collective-permute-start = (bf16[16,48,384]{2,1,0:T(8,128)(2,1)S(1)}, bf16[16,48,384]{2,1,0:T(8,128)(2,1)S(1)}, u32[]{:S(2)}, u32[]{:S(2)}) collective-permute-start(bf16[16,48,384]{2,1,0:T(8,128)(2,1)S(1)} %all-to-all-done.2.tiles), channel_id=1, source_target_pairs={{0,1},{1,0},{2,3},{3,2},{4,5},{5,4},{6,7},{7,6},{8,9},{9,8},{10,11... | collective-permute-start | bytes 1769480 | tf_op jit(solution)/shard_map/ppermute | solution.py:39

commit v17 on v16

--- a/solution.py
+++ b/solution.py
@@ -62,18 +62,20 @@
     for z in range(8):
         out[z] = blocks[z][:, :128]
     for h in range(2):
-        tails = jnp.concatenate([blocks[h * 4 + i][:, 128:] for i in range(4)], axis=1)
+        last = blocks[h * 4 + 3][:, 128:]
         for k in range(3):
-            out[8 + h * 3 + k] = tails[:, k * 128 : k * 128 + 128]
+            third = last[:, k * 32 : k * 32 + 32]
+            out[8 + h * 3 + k] = jnp.concatenate([blocks[h * 4 + k][:, 128:], third], axis=1)
 
 
 def unsqueeze(packed, w):
     for x in range(4):
         for h in range(2):
-            tails = jnp.concatenate([packed[x, 8 + h * 3 + k] for k in range(3)], axis=1)
+            tiles = [packed[x, 8 + h * 3 + k] for k in range(3)]
+            tails = [tile[:, :96] for tile in tiles]
+            tails.append(jnp.concatenate([tile[:, 96:] for tile in tiles], axis=1))
             for i in range(4):
-                tail = tails[:, i * 96 : i * 96 + 96]
-                w[x, h * 4 + i] = jnp.concatenate([packed[x, h * 4 + i], tail], axis=1)
+                w[x, h * 4 + i] = jnp.concatenate([packed[x, h * 4 + i], tails[i]], axis=1)
 
 
 def shard_body(both, out):

time: 113 us -> 113 us (level)
  no operation moved by 1% of the time
where the time goes in v17:
time: 113 us; the launch traced here: 112 us
  blocking collectives  86.9 us (77%)
  waiting for transfers between devices  13.9 us (12%)
  starting transfers between devices  6.35 us (6%)
  Pallas kernels  2.35 us (2%)
  local copies, waits for them, and re-layouts  1.82 us (2%)
    all_to_all x3, blocking collectives, exchange(): return lax.all_to_all(array, axes, 0, 0, tiled=True)  55 us
    all_gather x1, blocking collectives, local(): w = lax.all_gather(weighted, X, axis=0)  13.8 us
    all_gather x1, blocking collectives, local(): packed = lax.all_gather(shard, X, axis=0)  13.6 us
    all_to_all x1, waiting for transfers between devices, exchange(): return lax.all_to_all(array, axes, 0, 0, tiled=True)  12.3 us
    all_to_all x1, starting transfers between devices, exchange(): return lax.all_to_all(array, axes, 0, 0, tiled=True)  4.44 us
    all_gather x1, blocking collectives, local(): got = lax.all_gather(send, 'core', axis=0)  2.37 us
    pallas_call x7, Pallas kernels, kernel_calls(): pl.pallas_call(body, out_shape=outputs, in_specs=[VMEM] * len(inputs), ou...  2.35 us
  transfers between devices with their start and end apart: 2, of which 2 were waited for; matrix products, arithmetic and copies ran while one was open for 0% of the time, Pallas kernels for 0%

profile of v17, /device:TPU:8, one launch (start us, length us, event | category | flops | bytes accessed | tf_op | source)
XLA Modules:
  0.0 112.2 jit_solution(6440779682254482574)
XLA Ops:
  0.0 0.0 copy-start
  0.0 0.9 copy-done
  0.9 0.1 shard_map.17
  1.0 18.5 %all_to_all.20 = bf16[8,48,224]{2,1,0:T(8,128)(2,1)S(1)} all-to-all(bf16[8,48,224]{2,1,0:T(8,128)(2,1)S(1)} %shard_map.17), channel_id=1, replica_groups=mesh['z2'=2,'z1'=2,'z0'=2,'x1'=2,'x0'=2,'y2'=2,'y1'=2,'y0'=2,'core'=2] {..., dimensions={0} | all-to-all | bytes 344064 | tf_op jit(solution)/shard_map/all_to_all | solution.py:43
  19.6 2.1 %all-gather = bf16[16,48,224]{2,1,0:T(8,128)(2,1)S(1)} all-gather(bf16[8,48,224]{2,1,0:T(8,128)(2,1)S(1)} %all_to_all.20), channel_id=2, replica_groups=mesh['z2'=2,'z1'=2,'z0'=2,'x1'=2,'x0'=2,'y2'=2,'y1'=2,'y0'=2,'core'=2] {..., dimensions={0}, use_global_device_ids=true | all-gather | bytes 516096 | tf_op jit(solution)/shard_map/all_gather | solution.py:143
  21.6 0.1 shard_map.18
  21.7 13.6 %all-gather.1 = bf16[56,48,128]{2,1,0:T(8,128)(2,1)S(1)} all-gather(bf16[14,48,128]{2,1,0:T(8,128)(2,1)S(1)} %shard_map.18), channel_id=3, replica_groups=mesh['z2'=2,'z1'=2,'z0'=2,'x1'=2,'x0'=2,'y2'=2,'y1'=2,'y0'=2,'core'=2] {..., dimensions={0}, use_global_device_ids=true | all-gather | bytes 860160 | tf_op jit(solution)/shard_map/all_gather | solution.py:146
  35.3 0.7 shard_map.19
  36.0 24.8 %all_to_all.21 = bf16[16,48,384]{2,1,0:T(8,128)(2,1)S(1)} all-to-all(bf16[16,48,384]{2,1,0:T(8,128)(2,1)S(1)} %bitcast.12), channel_id=1, replica_groups=mesh['z2'=2,'z1'=2,'z0'=2,'x1'=2,'x0'=2,'y2'=2,'y1'=2,'y0'=2,'core'=2] {..., dimensions={0} | all-to-all | bytes 1179648 | tf_op jit(solution)/shard_map/all_to_all | solution.py:43
  60.8 0.1 reduce_sum.12
  60.9 0.9 broadcast_in_dim.2
  61.7 4.4 %all-to-all-start.2 = ((bf16[16,48,384]{2,1,0:T(8,128)(2,1)}), bf16[16,48,384]{2,1,0:T(8,128)(2,1)S(1)}, u32[]{:S(2)}, u32[]{:S(2)}) async-start(bf16[16,48,384]{2,1,0:T(8,128)(2,1)} %broadcast_in_dim.2), calls=%async_computation.2 | async-start | bytes 1179648 | tf_op jit(solution)/shard_map/all_to_all | solution.py:43
  66.2 2.4 %all-gather.2 = bf16[8,4,48,224]{3,2,1,0:T(8,128)(2,1)S(1)} all-gather(bf16[4,4,48,224]{3,2,1,0:T(8,128)(2,1)S(1)} %shard_map.20), channel_id=4, replica_groups=mesh['z2'=2,'z1'=2,'z0'=2,'x1'=2,'x0'=2,'y2'=2,'y1'=2,'y0'=2,'core'=2] {..., dimensions={0}, use_global_device_ids=true | all-gather | bytes 1032192 | tf_op jit(solution)/shard_map/all_gather | solution.py:153
  68.6 12.3 %all-to-all-done.2.tiles = bf16[16,48,384]{2,1,0:T(8,128)(2,1)S(1)} async-done(((bf16[16,48,384]{2,1,0:T(8,128)(2,1)}), bf16[16,48,384]{2,1,0:T(8,128)(2,1)S(1)}, u32[]{:S(2)}, u32[]{:S(2)}) %all-to-all-start.2) | async-done | bytes 589856 | tf_op jit(solution)/shard_map/all_to_all | solution.py:43
  80.9 1.9 %collective-permute-start = (bf16[16,48,384]{2,1,0:T(8,128)(2,1)S(1)}, bf16[16,48,384]{2,1,0:T(8,128)(2,1)S(1)}, u32[]{:S(2)}, u32[]{:S(2)}) collective-permute-start(bf16[16,48,384]{2,1,0:T(8,128)(2,1)S(1)} %all-to-all-done.2.tiles), channel_id=1, source_target_pairs={{0,1},{1,0},{2,3},{3,2},{4,5},{5,4},{6,7},{7,6},{8,9},{9,8},{10,11... | collective-permute-start | bytes 1769480 | tf_op jit(solution)/shard_map/ppermute | solution.py:39
  82.8 0.4 shard_map.21.first
  83.2 1.6 %collective-permute-done.others = bf16[16,48,384]{2,1,0:T(8,128)(2,1)S(1)} collective-permute-done((bf16[16,48,384]{2,1,0:T(8,128)(2,1)S(1)}, bf16[16,48,384]{2,1,0:T(8,128)(2,1)S(1)}, u32[]{:S(2)}, u32[]{:S(2)}) %collective-permute-start) | collective-permute-done | bytes 589856 | tf_op jit(solution)/shard_map/ppermute | solution.py:39
  84.8 0.4 shard_map.22
  85.2 13.8 %all-gather.3 = bf16[56,48,128]{2,1,0:T(8,128)(2,1)S(1)} all-gather(bf16[14,48,128]{2,1,0:T(8,128)(2,1)S(1)} %get-tuple-element.19), channel_id=5, replica_groups=mesh['z2'=2,'z1'=2,'z0'=2,'x1'=2,'x0'=2,'y2'=2,'y1'=2,'y0'=2,'core'=2] {..., dimensions={0}, use_global_device_ids=true | all-gather | bytes 860160 | tf_op jit(solution)/shard_map/all_gather | solution.py:161
  99.1 0.7 shard_map.23
  99.7 11.7 %all_to_all.22 = bf16[8,48,224]{2,1,0:T(8,128)(2,1)S(1)} all-to-all(bf16[8,48,224]{2,1,0:T(8,128)(2,1)S(1)} %shard_map.23), channel_id=1, replica_groups=mesh['z2'=2,'z1'=2,'z0'=2,'x1'=2,'x0'=2,'y2'=2,'y1'=2,'y0'=2,'core'=2] {..., dimensions={0} | all-to-all | bytes 344064 | tf_op jit(solution)/shard_map/all_to_all | solution.py:43
  111.4 0.8 maximum_maximum_fusion
  (2 shorter events, 0.0 us)
Async XLA Ops:
  0.0 0.9 copy-start
  61.7 19.2 %all-to-all-start.2 = ((bf16[16,48,384]{2,1,0:T(8,128)(2,1)}), bf16[16,48,384]{2,1,0:T(8,128)(2,1)S(1)}, u32[]{:S(2)}, u32[]{:S(2)}) async-start(bf16[16,48,384]{2,1,0:T(8,128)(2,1)} %broadcast_in_dim.2), calls=%async_computation.2 | async-start | bytes 1179648 | tf_op jit(solution)/shard_map/all_to_all | solution.py:43
  80.9 3.9 %collective-permute-start = (bf16[16,48,384]{2,1,0:T(8,128)(2,1)S(1)}, bf16[16,48,384]{2,1,0:T(8,128)(2,1)S(1)}, u32[]{:S(2)}, u32[]{:S(2)}) collective-permute-start(bf16[16,48,384]{2,1,0:T(8,128)(2,1)S(1)} %all-to-all-done.2.tiles), channel_id=1, source_target_pairs={{0,1},{1,0},{2,3},{3,2},{4,5},{5,4},{6,7},{7,6},{8,9},{9,8},{10,11... | collective-permute-start | bytes 1769480 | tf_op jit(solution)/shard_map/ppermute | solution.py:39

commit v18 on v17

--- a/solution.py
+++ b/solution.py
@@ -12,7 +12,7 @@
 A1, A3, A5 = 3.4445, -4.775, 2.0315
 SCALE = 0.2 * math.sqrt(7168)
 KAPPA = 2.7
-Z = ("z0", "z1", "z2")
+Z = ("z1", "z0", "z2")
 HY = ("z0", "y2", "y1", "y0")
 X = ("x1", "x0")
 AXES = ("z2", "z1", "z0", "x1", "x0", "y2", "y1", "y0", "core")

time: 113 us -> 113 us (level)
  no operation moved by 1% of the time
where the time goes in v18:
time: 113 us; the launch traced here: 112 us
  blocking collectives  86.9 us (77%)
  waiting for transfers between devices  13.9 us (12%)
  starting transfers between devices  6.35 us (6%)
  Pallas kernels  2.35 us (2%)
  local copies, waits for them, and re-layouts  1.82 us (2%)
    all_to_all x3, blocking collectives, exchange(): return lax.all_to_all(array, axes, 0, 0, tiled=True)  55.1 us
    all_gather x1, blocking collectives, local(): w = lax.all_gather(weighted, X, axis=0)  13.8 us
    all_gather x1, blocking collectives, local(): packed = lax.all_gather(shard, X, axis=0)  13.6 us
    all_to_all x1, waiting for transfers between devices, exchange(): return lax.all_to_all(array, axes, 0, 0, tiled=True)  12.3 us
    all_to_all x1, starting transfers between devices, exchange(): return lax.all_to_all(array, axes, 0, 0, tiled=True)  4.44 us
    all_gather x1, blocking collectives, local(): got = lax.all_gather(send, 'core', axis=0)  2.37 us
    pallas_call x7, Pallas kernels, kernel_calls(): pl.pallas_call(body, out_shape=outputs, in_specs=[VMEM] * len(inputs), ou...  2.35 us
  transfers between devices with their start and end apart: 2, of which 2 were waited for; matrix products, arithmetic and copies ran while one was open for 0% of the time, Pallas kernels for 0%

profile of v18, /device:TPU:8, one launch (start us, length us, event | category | flops | bytes accessed | tf_op | source)
XLA Modules:
  0.0 112.3 jit_solution(3323359391305417470)
XLA Ops:
  0.0 0.0 copy-start
  0.0 0.9 copy-done
  0.9 0.1 shard_map.17
  1.0 18.5 %all_to_all.20 = bf16[8,48,224]{2,1,0:T(8,128)(2,1)S(1)} all-to-all(bf16[8,48,224]{2,1,0:T(8,128)(2,1)S(1)} %shard_map.17), channel_id=1, replica_groups=mesh['z2'=2,'z1'=2,'z0'=2,'x1'=2,'x0'=2,'y2'=2,'y1'=2,'y0'=2,'core'=2] {..., dimensions={0} | all-to-all | bytes 344064 | tf_op jit(solution)/shard_map/all_to_all | solution.py:43
  19.6 2.1 %all-gather = bf16[16,48,224]{2,1,0:T(8,128)(2,1)S(1)} all-gather(bf16[8,48,224]{2,1,0:T(8,128)(2,1)S(1)} %all_to_all.20), channel_id=2, replica_groups=mesh['z2'=2,'z1'=2,'z0'=2,'x1'=2,'x0'=2,'y2'=2,'y1'=2,'y0'=2,'core'=2] {..., dimensions={0}, use_global_device_ids=true | all-gather | bytes 516096 | tf_op jit(solution)/shard_map/all_gather | solution.py:143
  21.7 0.1 shard_map.18
  21.8 13.6 %all-gather.1 = bf16[56,48,128]{2,1,0:T(8,128)(2,1)S(1)} all-gather(bf16[14,48,128]{2,1,0:T(8,128)(2,1)S(1)} %shard_map.18), channel_id=3, replica_groups=mesh['z2'=2,'z1'=2,'z0'=2,'x1'=2,'x0'=2,'y2'=2,'y1'=2,'y0'=2,'core'=2] {..., dimensions={0}, use_global_device_ids=true | all-gather | bytes 860160 | tf_op jit(solution)/shard_map/all_gather | solution.py:146
  35.3 0.7 shard_map.19
  36.0 25.6 %all_to_all.21 = bf16[16,48,384]{2,1,0:T(8,128)(2,1)S(1)} all-to-all(bf16[16,48,384]{2,1,0:T(8,128)(2,1)S(1)} %bitcast.12), channel_id=1, replica_groups=mesh['z2'=2,'z1'=2,'z0'=2,'x1'=2,'x0'=2,'y2'=2,'y1'=2,'y0'=2,'core'=2] {..., dimensions={0} | all-to-all | bytes 1179648 | tf_op jit(solution)/shard_map/all_to_all | solution.py:43
  61.5 0.1 reduce_sum.12
  61.6 0.9 broadcast_in_dim.2
  62.5 4.4 %all-to-all-start.2 = ((bf16[16,48,384]{2,1,0:T(8,128)(2,1)}), bf16[16,48,384]{2,1,0:T(8,128)(2,1)S(1)}, u32[]{:S(2)}, u32[]{:S(2)}) async-start(bf16[16,48,384]{2,1,0:T(8,128)(2,1)} %broadcast_in_dim.2), calls=%async_computation.2 | async-start | bytes 1179648 | tf_op jit(solution)/shard_map/all_to_all | solution.py:43
  67.0 2.4 %all-gather.2 = bf16[8,4,48,224]{3,2,1,0:T(8,128)(2,1)S(1)} all-gather(bf16[4,4,48,224]{3,2,1,0:T(8,128)(2,1)S(1)} %shard_map.20), channel_id=4, replica_groups=mesh['z2'=2,'z1'=2,'z0'=2,'x1'=2,'x0'=2,'y2'=2,'y1'=2,'y0'=2,'core'=2] {..., dimensions={0}, use_global_device_ids=true | all-gather | bytes 1032192 | tf_op jit(solution)/shard_map/all_gather | solution.py:153
  69.4 12.3 %all-to-all-done.2.tiles = bf16[16,48,384]{2,1,0:T(8,128)(2,1)S(1)} async-done(((bf16[16,48,384]{2,1,0:T(8,128)(2,1)}), bf16[16,48,384]{2,1,0:T(8,128)(2,1)S(1)}, u32[]{:S(2)}, u32[]{:S(2)}) %all-to-all-start.2) | async-done | bytes 589856 | tf_op jit(solution)/shard_map/all_to_all | solution.py:43
  81.7 1.9 %collective-permute-start = (bf16[16,48,384]{2,1,0:T(8,128)(2,1)S(1)}, bf16[16,48,384]{2,1,0:T(8,128)(2,1)S(1)}, u32[]{:S(2)}, u32[]{:S(2)}) collective-permute-start(bf16[16,48,384]{2,1,0:T(8,128)(2,1)S(1)} %all-to-all-done.2.tiles), channel_id=1, source_target_pairs={{0,1},{1,0},{2,3},{3,2},{4,5},{5,4},{6,7},{7,6},{8,9},{9,8},{10,11... | collective-permute-start | bytes 1769480 | tf_op jit(solution)/shard_map/ppermute | solution.py:39
  83.6 0.4 shard_map.21.first
  84.0 1.6 %collective-permute-done.others = bf16[16,48,384]{2,1,0:T(8,128)(2,1)S(1)} collective-permute-done((bf16[16,48,384]{2,1,0:T(8,128)(2,1)S(1)}, bf16[16,48,384]{2,1,0:T(8,128)(2,1)S(1)}, u32[]{:S(2)}, u32[]{:S(2)}) %collective-permute-start) | collective-permute-done | bytes 589856 | tf_op jit(solution)/shard_map/ppermute | solution.py:39
  85.6 0.4 shard_map.22
  86.0 13.8 %all-gather.3 = bf16[56,48,128]{2,1,0:T(8,128)(2,1)S(1)} all-gather(bf16[14,48,128]{2,1,0:T(8,128)(2,1)S(1)} %get-tuple-element.19), channel_id=5, replica_groups=mesh['z2'=2,'z1'=2,'z0'=2,'x1'=2,'x0'=2,'y2'=2,'y1'=2,'y0'=2,'core'=2] {..., dimensions={0}, use_global_device_ids=true | all-gather | bytes 860160 | tf_op jit(solution)/shard_map/all_gather | solution.py:161
  99.8 0.7 shard_map.23
  100.5 11.0 %all_to_all.22 = bf16[8,48,224]{2,1,0:T(8,128)(2,1)S(1)} all-to-all(bf16[8,48,224]{2,1,0:T(8,128)(2,1)S(1)} %shard_map.23), channel_id=1, replica_groups=mesh['z2'=2,'z1'=2,'z0'=2,'x1'=2,'x0'=2,'y2'=2,'y1'=2,'y0'=2,'core'=2] {..., dimensions={0} | all-to-all | bytes 344064 | tf_op jit(solution)/shard_map/all_to_all | solution.py:43
  111.5 0.8 maximum_maximum_fusion
  (2 shorter events, 0.0 us)
Async XLA Ops:
  0.0 0.9 copy-start
  62.5 19.2 %all-to-all-start.2 = ((bf16[16,48,384]{2,1,0:T(8,128)(2,1)}), bf16[16,48,384]{2,1,0:T(8,128)(2,1)S(1)}, u32[]{:S(2)}, u32[]{:S(2)}) async-start(bf16[16,48,384]{2,1,0:T(8,128)(2,1)} %broadcast_in_dim.2), calls=%async_computation.2 | async-start | bytes 1179648 | tf_op jit(solution)/shard_map/all_to_all | solution.py:43
  81.7 3.9 %collective-permute-start = (bf16[16,48,384]{2,1,0:T(8,128)(2,1)S(1)}, bf16[16,48,384]{2,1,0:T(8,128)(2,1)S(1)}, u32[]{:S(2)}, u32[]{:S(2)}) collective-permute-start(bf16[16,48,384]{2,1,0:T(8,128)(2,1)S(1)} %all-to-all-done.2.tiles), channel_id=1, source_target_pairs={{0,1},{1,0},{2,3},{3,2},{4,5},{5,4},{6,7},{7,6},{8,9},{9,8},{10,11... | collective-permute-start | bytes 1769480 | tf_op jit(solution)/shard_map/ppermute | solution.py:39

commit v19 on v17

--- a/solution.py
+++ b/solution.py
@@ -12,6 +12,7 @@
 A1, A3, A5 = 3.4445, -4.775, 2.0315
 SCALE = 0.2 * math.sqrt(7168)
 KAPPA = 2.7
+RATIO = KAPPA / A5
 Z = ("z0", "z1", "z2")
 HY = ("z0", "y2", "y1", "y0")
 X = ("x1", "x0")
@@ -110,25 +111,26 @@
     return total.reshape(8, 48, 224)
 
 
-def first_body(m, tiles, out):
-    own = pl.ds(lax.axis_index("core") * 4, 4)
-    out[...] = times(tiles, [stack([m[2 * g + i, own] for i in range(2)]) for g in range(2)])
+def first_body(both, m, tiles, out):
+    core = lax.axis_index("core")
+    own = pl.ds(core * 4, 4)
+    gm = times(tiles, [stack([m[2 * g + i, own] for i in range(2)]) for g in range(2)])
+    out[...] = (A3 + KAPPA) * both[core].astype(F32) + A5 * gm
 
 
-def weight_body(both, got, others, first, out, product):
-    core = lax.axis_index("core")
-    theirs = got.at[1 - core]
+def weight_body(got, others, first, out, exact):
+    theirs = got.at[1 - lax.axis_index("core")]
     groups = [stack([theirs[2 * g + i] for i in range(2)]) for g in range(2)]
-    gm = first[...] + times(others, groups)
-    w = ((A3 + KAPPA) * both[core].astype(F32) + A5 * gm).astype(BF16)
+    total = first[...] + A5 * times(others, groups)
+    w = total.astype(BF16)
     squeeze([w[z] for z in range(8)], out)
-    product[...] = gm
+    exact[...] = total
 
 
-def product_body(packed, tiles, others, both, gm, out, w):
+def product_body(packed, tiles, others, both, exact, out, w):
     unsqueeze(packed, w)
     core = lax.axis_index("core")
-    total = A1 * both[core].astype(F32) - KAPPA * gm[...]
+    total = (A1 + RATIO * (A3 + KAPPA)) * both[core].astype(F32) - RATIO * exact[...]
     for held, h in ((tiles, core), (others, 1 - core)):
         groups = [
             stack([w[2 * g + i, pl.ds(h * 4, 4)] for i in range(2)]) for g in range(2)
@@ -154,14 +156,14 @@
     gathered, got = lax.optimization_barrier((gathered, got))
 
     others = swap(gathered)
-    first = kernel_call(first_body, [m, gathered], (8, 48, 224), F32, flops)
+    first = kernel_call(first_body, [both, m, gathered], (8, 48, 224), F32, flops)
     block = (8, 48, 224)
     outputs = [jax.ShapeDtypeStruct((14, 48, 128), BF16), jax.ShapeDtypeStruct(block, F32)]
-    weighted, gm = kernel_calls(weight_body, [both, got, others, first], outputs, flops)
+    weighted, exact = kernel_calls(weight_body, [got, others, first], outputs, flops)
     w = lax.all_gather(weighted, X, axis=0)
     rows = kernel_call(
         product_body,
-        [w, gathered, others, both, gm],
+        [w, gathered, others, both, exact],
         block,
         BF16,
         2 * flops,

time: 113 us -> 113 us (level)
  no operation moved by 1% of the time
where the time goes in v19:
time: 113 us; the launch traced here: 112 us
  blocking collectives  86.9 us (77%)
  waiting for transfers between devices  13.9 us (12%)
  starting transfers between devices  6.35 us (6%)
  Pallas kernels  2.35 us (2%)
  local copies, waits for them, and re-layouts  1.82 us (2%)
    all_to_all x3, blocking collectives, exchange(): return lax.all_to_all(array, axes, 0, 0, tiled=True)  55 us
    all_gather x1, blocking collectives, local(): w = lax.all_gather(weighted, X, axis=0)  13.8 us
    all_gather x1, blocking collectives, local(): packed = lax.all_gather(shard, X, axis=0)  13.6 us
    all_to_all x1, waiting for transfers between devices, exchange(): return lax.all_to_all(array, axes, 0, 0, tiled=True)  12.3 us
    all_to_all x1, starting transfers between devices, exchange(): return lax.all_to_all(array, axes, 0, 0, tiled=True)  4.44 us
    all_gather x1, blocking collectives, local(): got = lax.all_gather(send, 'core', axis=0)  2.37 us
    pallas_call x7, Pallas kernels, kernel_calls(): pl.pallas_call(body, out_shape=outputs, in_specs=[VMEM] * len(inputs), ou...  2.35 us
  transfers between devices with their start and end apart: 2, of which 2 were waited for; matrix products, arithmetic and copies ran while one was open for 0% of the time, Pallas kernels for 0%

profile of v19, /device:TPU:8, one launch (start us, length us, event | category | flops | bytes accessed | tf_op | source)
XLA Modules:
  0.0 112.2 jit_solution(2253805367638891737)
XLA Ops:
  0.0 0.0 copy-start
  0.0 0.9 copy-done
  0.9 0.1 shard_map.17
  1.0 18.5 %all_to_all.20 = bf16[8,48,224]{2,1,0:T(8,128)(2,1)S(1)} all-to-all(bf16[8,48,224]{2,1,0:T(8,128)(2,1)S(1)} %shard_map.17), channel_id=1, replica_groups=mesh['z2'=2,'z1'=2,'z0'=2,'x1'=2,'x0'=2,'y2'=2,'y1'=2,'y0'=2,'core'=2] {..., dimensions={0} | all-to-all | bytes 344064 | tf_op jit(solution)/shard_map/all_to_all | solution.py:44
  19.6 2.1 %all-gather = bf16[16,48,224]{2,1,0:T(8,128)(2,1)S(1)} all-gather(bf16[8,48,224]{2,1,0:T(8,128)(2,1)S(1)} %all_to_all.20), channel_id=2, replica_groups=mesh['z2'=2,'z1'=2,'z0'=2,'x1'=2,'x0'=2,'y2'=2,'y1'=2,'y0'=2,'core'=2] {..., dimensions={0}, use_global_device_ids=true | all-gather | bytes 516096 | tf_op jit(solution)/shard_map/all_gather | solution.py:145
  21.6 0.1 shard_map.18
  21.7 13.6 %all-gather.1 = bf16[56,48,128]{2,1,0:T(8,128)(2,1)S(1)} all-gather(bf16[14,48,128]{2,1,0:T(8,128)(2,1)S(1)} %shard_map.18), channel_id=3, replica_groups=mesh['z2'=2,'z1'=2,'z0'=2,'x1'=2,'x0'=2,'y2'=2,'y1'=2,'y0'=2,'core'=2] {..., dimensions={0}, use_global_device_ids=true | all-gather | bytes 860160 | tf_op jit(solution)/shard_map/all_gather | solution.py:148
  35.3 0.7 shard_map.19
  36.0 24.8 %all_to_all.21 = bf16[16,48,384]{2,1,0:T(8,128)(2,1)S(1)} all-to-all(bf16[16,48,384]{2,1,0:T(8,128)(2,1)S(1)} %bitcast.12), channel_id=1, replica_groups=mesh['z2'=2,'z1'=2,'z0'=2,'x1'=2,'x0'=2,'y2'=2,'y1'=2,'y0'=2,'core'=2] {..., dimensions={0} | all-to-all | bytes 1179648 | tf_op jit(solution)/shard_map/all_to_all | solution.py:44
  60.8 0.1 reduce_sum.12
  60.9 0.9 broadcast_in_dim.2
  61.7 4.4 %all-to-all-start.2 = ((bf16[16,48,384]{2,1,0:T(8,128)(2,1)}), bf16[16,48,384]{2,1,0:T(8,128)(2,1)S(1)}, u32[]{:S(2)}, u32[]{:S(2)}) async-start(bf16[16,48,384]{2,1,0:T(8,128)(2,1)} %broadcast_in_dim.2), calls=%async_computation.2 | async-start | bytes 1179648 | tf_op jit(solution)/shard_map/all_to_all | solution.py:44
  66.2 2.4 %all-gather.2 = bf16[8,4,48,224]{3,2,1,0:T(8,128)(2,1)S(1)} all-gather(bf16[4,4,48,224]{3,2,1,0:T(8,128)(2,1)S(1)} %shard_map.20), channel_id=4, replica_groups=mesh['z2'=2,'z1'=2,'z0'=2,'x1'=2,'x0'=2,'y2'=2,'y1'=2,'y0'=2,'core'=2] {..., dimensions={0}, use_global_device_ids=true | all-gather | bytes 1032192 | tf_op jit(solution)/shard_map/all_gather | solution.py:155
  68.6 12.3 %all-to-all-done.2.tiles = bf16[16,48,384]{2,1,0:T(8,128)(2,1)S(1)} async-done(((bf16[16,48,384]{2,1,0:T(8,128)(2,1)}), bf16[16,48,384]{2,1,0:T(8,128)(2,1)S(1)}, u32[]{:S(2)}, u32[]{:S(2)}) %all-to-all-start.2) | async-done | bytes 589856 | tf_op jit(solution)/shard_map/all_to_all | solution.py:44
  80.9 1.9 %collective-permute-start = (bf16[16,48,384]{2,1,0:T(8,128)(2,1)S(1)}, bf16[16,48,384]{2,1,0:T(8,128)(2,1)S(1)}, u32[]{:S(2)}, u32[]{:S(2)}) collective-permute-start(bf16[16,48,384]{2,1,0:T(8,128)(2,1)S(1)} %all-to-all-done.2.tiles), channel_id=1, source_target_pairs={{0,1},{1,0},{2,3},{3,2},{4,5},{5,4},{6,7},{7,6},{8,9},{9,8},{10,11... | collective-permute-start | bytes 1769480 | tf_op jit(solution)/shard_map/ppermute | solution.py:40
  82.8 0.4 shard_map.21.first
  83.2 1.6 %collective-permute-done.others = bf16[16,48,384]{2,1,0:T(8,128)(2,1)S(1)} collective-permute-done((bf16[16,48,384]{2,1,0:T(8,128)(2,1)S(1)}, bf16[16,48,384]{2,1,0:T(8,128)(2,1)S(1)}, u32[]{:S(2)}, u32[]{:S(2)}) %collective-permute-start) | collective-permute-done | bytes 589856 | tf_op jit(solution)/shard_map/ppermute | solution.py:40
  84.8 0.4 shard_map.22
  85.2 13.8 %all-gather.3 = bf16[56,48,128]{2,1,0:T(8,128)(2,1)S(1)} all-gather(bf16[14,48,128]{2,1,0:T(8,128)(2,1)S(1)} %get-tuple-element.19), channel_id=5, replica_groups=mesh['z2'=2,'z1'=2,'z0'=2,'x1'=2,'x0'=2,'y2'=2,'y1'=2,'y0'=2,'core'=2] {..., dimensions={0}, use_global_device_ids=true | all-gather | bytes 860160 | tf_op jit(solution)/shard_map/all_gather | solution.py:163
  99.1 0.7 shard_map.23
  99.8 11.7 %all_to_all.22 = bf16[8,48,224]{2,1,0:T(8,128)(2,1)S(1)} all-to-all(bf16[8,48,224]{2,1,0:T(8,128)(2,1)S(1)} %shard_map.23), channel_id=1, replica_groups=mesh['z2'=2,'z1'=2,'z0'=2,'x1'=2,'x0'=2,'y2'=2,'y1'=2,'y0'=2,'core'=2] {..., dimensions={0} | all-to-all | bytes 344064 | tf_op jit(solution)/shard_map/all_to_all | solution.py:44
  111.4 0.8 maximum_maximum_fusion
  (2 shorter events, 0.0 us)
Async XLA Ops:
  0.0 0.9 copy-start
  61.7 19.2 %all-to-all-start.2 = ((bf16[16,48,384]{2,1,0:T(8,128)(2,1)}), bf16[16,48,384]{2,1,0:T(8,128)(2,1)S(1)}, u32[]{:S(2)}, u32[]{:S(2)}) async-start(bf16[16,48,384]{2,1,0:T(8,128)(2,1)} %broadcast_in_dim.2), calls=%async_computation.2 | async-start | bytes 1179648 | tf_op jit(solution)/shard_map/all_to_all | solution.py:44
  80.9 3.9 %collective-permute-start = (bf16[16,48,384]{2,1,0:T(8,128)(2,1)S(1)}, bf16[16,48,384]{2,1,0:T(8,128)(2,1)S(1)}, u32[]{:S(2)}, u32[]{:S(2)}) collective-permute-start(bf16[16,48,384]{2,1,0:T(8,128)(2,1)S(1)} %all-to-all-done.2.tiles), channel_id=1, source_target_pairs={{0,1},{1,0},{2,3},{3,2},{4,5},{5,4},{6,7},{7,6},{8,9},{9,8},{10,11... | collective-permute-start | bytes 1769480 | tf_op jit(solution)/shard_map/ppermute | solution.py:40
